TPU v7x, 32 devices: a whole 2x2x4 slice. The times are simulated.
32 devices in a mesh: ctx: 8 (over z, x), kvh: 4 (over y, core).
Axes of the slice: x: 2, y: 2, z: 4, core: 2. Of those that a mesh axis runs over, the one named last changes fastest.
Arguments:
- query_act: bfloat16 [2048, 8192], P(('ctx', 'kvh')), may hold values from -6 to 6
- key_act: bfloat16 [2048, 1024], P(('ctx', 'kvh')), may hold values from -6 to 6
- value_act: bfloat16 [2048, 1024], P(('ctx', 'kvh')), may hold values from -6 to 6
- grad_out: bfloat16 [2048, 8192], P(('ctx', 'kvh')), may hold values from -6 to 6
Outputs:
- attn_out: bfloat16 [2048, 8192], P(('ctx', 'kvh'))
- grad_query: bfloat16 [2048, 8192], P(('ctx', 'kvh'))
- grad_key: bfloat16 [2048, 1024], P(('ctx', 'kvh'))
- grad_value: bfloat16 [2048, 1024], P(('ctx', 'kvh'))
All inputs are finite; a program needn't handle non-finite values.
Results may differ from a plain program's by a relative error of at most 0.014.
Values may be sent and summed in bfloat16 or wider, within the bound.
No kernel may reach another device: no remote copies, remote signals or barrier semaphores. Data moves between devices by JAX's collectives and lax.ppermute only.
A program may use at most 128 MiB of HBM per device.

v0:
```python
import jax
import jax.numpy as jnp
from jax import lax
from jax.sharding import PartitionSpec as P

QPK = 8
HD = 128


masked_score = -1e30


def shifted(array, axis, by):
    peers = lax.axis_size(axis)
    pairs = [(i, i + by) for i in range(peers) if 0 <= i + by < peers]
    return lax.ppermute(array, axis, pairs)


def level_scores(queries, key_rows, scale, mask):
    scores = (
        jnp.einsum("tgrd,ugd->grtu", queries, key_rows, preferred_element_type=jnp.float32) * scale
    )
    return jnp.where(mask, scores, masked_score)


def shards(query_act, key_act, value_act, grad_out):
    q_heads, grad_heads, k_heads, v_heads = (
        lax.all_to_all(query_act, "kvh", split_axis=1, concat_axis=0, tiled=True),
        lax.all_to_all(grad_out, "kvh", split_axis=1, concat_axis=0, tiled=True),
        lax.all_to_all(key_act, "kvh", split_axis=1, concat_axis=0, tiled=True),
        lax.all_to_all(value_act, "kvh", split_axis=1, concat_axis=0, tiled=True),
    )
    block_len = q_heads.shape[0]
    groups = k_heads.shape[1] // HD
    scale = HD ** (-0.5)
    queries = q_heads.reshape(block_len, groups, QPK, HD)
    grad_rows = grad_heads.reshape(block_len, groups, QPK, HD)
    devices = lax.axis_size("ctx")
    levels = (devices - 1).bit_length()
    ctx_index = lax.axis_index("ctx")
    partners = []
    for level in range(levels):
        partners.append(shifted((k_heads, v_heads), "ctx", 1 << level))
    blocks = [(k_heads, v_heads)] + partners
    position = jnp.arange(block_len)
    causal = (position[None, :] <= position[:, None])[None, None]
    masks = [causal] + [
        jnp.broadcast_to(ctx_index >= 1 << level, (1, 1, 1, 1)) for level in range(levels)
    ]
    shaped = [
        (pair[0].reshape(block_len, groups, HD), pair[1].reshape(block_len, groups, HD))
        for pair in blocks
    ]
    run_max = None
    run_sum = None
    run_out = None
    for level_index in range(len(shaped)):
        key_rows, value_rows = shaped[level_index]
        mask = masks[level_index]
        scores = level_scores(queries, key_rows, scale, mask)
        level_max = jnp.max(scores, axis=3)
        expo = jnp.where(mask, jnp.exp(scores - level_max[..., None]), 0.0)
        level_sum = jnp.sum(expo, axis=3)
        level_out = jnp.einsum(
            "grtu,ugd->tgrd",
            expo.astype(jnp.bfloat16),
            value_rows,
            preferred_element_type=jnp.float32,
        )
        if level_index == 0:
            run_max, run_sum, run_out = (level_max, level_sum, level_out)
        else:
            new_max = jnp.maximum(run_max, level_max)
            old_factor = jnp.exp(run_max - new_max)
            new_factor = jnp.exp(level_max - new_max)
            run_sum = old_factor * run_sum + new_factor * level_sum
            run_out = (
                jnp.transpose(old_factor, (2, 0, 1))[..., None] * run_out
                + jnp.transpose(new_factor, (2, 0, 1))[..., None] * level_out
            )
            run_max = new_max
    logsum = run_max + jnp.log(run_sum)
    out_block = (run_out / jnp.transpose(run_sum, (2, 0, 1))[..., None]).astype(jnp.bfloat16)
    delta = jnp.transpose(
        jnp.sum(grad_rows.astype(jnp.float32) * out_block.astype(jnp.float32), axis=3), (1, 2, 0)
    )
    grad_q = jnp.zeros((block_len, groups, QPK, HD), jnp.float32)
    key_grads = []
    for level_index in range(len(shaped)):
        key_rows, value_rows = shaped[level_index]
        mask = masks[level_index]
        scores = level_scores(queries, key_rows, scale, mask)
        probs = jnp.where(mask, jnp.exp(scores - logsum[..., None]), 0.0)
        grad_val = jnp.einsum(
            "grtu,tgrd->ugd",
            probs.astype(jnp.bfloat16),
            grad_rows,
            preferred_element_type=jnp.float32,
        )
        grad_prob = jnp.einsum(
            "tgrd,ugd->grtu", grad_rows, value_rows, preferred_element_type=jnp.float32
        )
        grad_scores = (probs * (grad_prob - delta[..., None])).astype(jnp.bfloat16)
        grad_q = grad_q + scale * jnp.einsum(
            "grtu,ugd->tgrd", grad_scores, key_rows, preferred_element_type=jnp.float32
        )
        grad_k = scale * jnp.einsum(
            "grtu,tgrd->ugd", grad_scores, queries, preferred_element_type=jnp.float32
        )
        key_grads.append(
            (grad_k.reshape(block_len, groups * HD), grad_val.reshape(block_len, groups * HD))
        )
    own_key, own_value = key_grads[0]
    remote = key_grads[1:]
    carried = remote[levels - 1]
    distances = [1 << level for level in range(levels - 2, -1, -1)] + [1]
    for section_index in range(len(distances)):
        carried = shifted(carried, "ctx", -distances[section_index])
        if section_index < levels - 1:
            partial_terms = remote[levels - 2 - section_index]
            carried = (carried[0] + partial_terms[0], carried[1] + partial_terms[1])
    own_key = own_key + carried[0]
    own_value = own_value + carried[1]
    out_flat = out_block.reshape(block_len, groups * QPK * HD)
    grad_flat = grad_q.astype(jnp.bfloat16).reshape(block_len, groups * QPK * HD)
    return (
        lax.all_to_all(out_flat, "kvh", split_axis=0, concat_axis=1, tiled=True),
        lax.all_to_all(grad_flat, "kvh", split_axis=0, concat_axis=1, tiled=True),
        lax.all_to_all(
            own_key.astype(jnp.bfloat16), "kvh", split_axis=0, concat_axis=1, tiled=True
        ),
        lax.all_to_all(
            own_value.astype(jnp.bfloat16), "kvh", split_axis=0, concat_axis=1, tiled=True
        ),
    )


def solution(mesh):
    return jax.shard_map(
        shards,
        mesh=mesh,
        in_specs=(
            P(("ctx", "kvh"), None),
            P(("ctx", "kvh"), None),
            P(("ctx", "kvh"), None),
            P(("ctx", "kvh"), None),
        ),
        out_specs=(
            P(("ctx", "kvh"), None),
            P(("ctx", "kvh"), None),
            P(("ctx", "kvh"), None),
            P(("ctx", "kvh"), None),
        ),
        check_vma=False,
    )
```

profile of v0, /device:TPU:29, one launch (start us, length us, event | category | flops | bytes accessed | tf_op | source)
XLA Modules:
  0.0 190.0 jit_solution(14976263907368012310)
XLA Ops:
  0.6 1.7 copy.336
  2.3 4.1 %all-to-all-start = ((bf16[64,4,256]{2,0,1:T(8,128)(2,1)}), bf16[64,4,256]{2,0,1:T(8,128)(2,1)S(1)}, u32[]{:S(2)}, u32[]{:S(2)}) async-start(bf16[64,4,256]{2,0,1:T(8,128)(2,1)} %bitcast.395), calls=%async_computation | async-start | bytes 262144 | tf_op jit(solution)/shard_map/all_to_all | solution.py:30
  6.4 1.6 copy.335
  8.0 1.2 all-to-all-done
  9.1 5.2 %all-to-all-start.2 = ((bf16[64,4,256]{2,0,1:T(8,128)(2,1)}), bf16[64,4,256]{2,0,1:T(8,128)(2,1)S(1)}, u32[]{:S(2)}, u32[]{:S(2)}) async-start(bf16[64,4,256]{2,0,1:T(8,128)(2,1)} %bitcast.394), calls=%async_computation.2 | async-start | bytes 262144 | tf_op jit(solution)/shard_map/all_to_all | solution.py:31
  14.3 2.3 %copy.334 = bf16[8,4,8,2048]{3,2,0,1:T(8,128)(2,1)} copy(bf16[8,4,8,2048]{3,2,1,0:T(8,128)(2,1)} %bitcast.408) | data formatting | bytes 2097152 | tf_op jit(solution)/shard_map/all_to_all | solution.py:28
  17.1 5.4 %all-to-all-start.1 = ((bf16[64,4,2048]{2,0,1:T(8,128)(2,1)}), bf16[64,4,2048]{2,0,1:T(8,128)(2,1)S(1)}, u32[]{:S(2)}, u32[]{:S(2)}) async-start(bf16[64,4,2048]{2,0,1:T(8,128)(2,1)} %bitcast.393), calls=%async_computation.1 | async-start | bytes 2097152 | tf_op jit(solution)/shard_map/all_to_all | solution.py:28
  22.5 1.3 collective-permute-start.5
  23.8 1.3 collective-permute-start.4
  25.1 3.1 %collective-permute-start.3 = (bf16[256,256]{1,0:T(8,128)(2,1)S(1)}, bf16[256,256]{1,0:T(8,128)(2,1)S(1)}, u32[]{:S(2)}, u32[]{:S(2)}) collective-permute-start(bf16[256,256]{1,0:T(8,128)(2,1)S(1)} %bitcast.422), channel_id=1, source_target_pairs={{0,4},{4,8},{8,12},{12,16},{16,20},{20,24},{24,28},{1,5},{5,9},{9,... | collective-permute-start | bytes 393224 | tf_op jit(solution)/shard_map/ppermute | solution.py:16
  28.2 1.3 collective-permute-start.2
  29.5 1.3 collective-permute-start.1
  30.8 2.6 %collective-permute-done.5 = bf16[256,256]{1,0:T(8,128)(2,1)S(1)} collective-permute-done((bf16[256,256]{1,0:T(8,128)(2,1)S(1)}, bf16[256,256]{1,0:T(8,128)(2,1)S(1)}, u32[]{:S(2)}, u32[]{:S(2)}) %collective-permute-start.5) | collective-permute-done | bytes 131104 | tf_op jit(solution)/shard_map/ppermute | solution.py:16
  33.4 3.1 %collective-permute-start = (bf16[256,256]{1,0:T(8,128)(2,1)S(1)}, bf16[256,256]{1,0:T(8,128)(2,1)S(1)}, u32[]{:S(2)}, u32[]{:S(2)}) collective-permute-start(bf16[256,256]{1,0:T(8,128)(2,1)S(1)} %bitcast.418), channel_id=1, source_target_pairs={{0,4},{4,8},{8,12},{12,16},{16,20},{20,24},{24,28},{1,5},{5,9},{9,... | collective-permute-start | bytes 393224 | tf_op jit(solution)/shard_map/ppermute | solution.py:16
  43.3 7.4 %all-to-all-start.4 = ((bf16[64,4,2048]{2,0,1:T(8,128)(2,1)}), bf16[64,4,2048]{2,0,1:T(8,128)(2,1)S(1)}, u32[]{:S(2)}, u32[]{:S(2)}) async-start(bf16[64,4,2048]{2,0,1:T(8,128)(2,1)} %bitcast.392), calls=%async_computation.4 | async-start | bytes 2097152 | tf_op jit(solution)/shard_map/all_to_all | solution.py:29
  55.2 1.3 copy-done.6
  56.5 2.2 %fusion.20 = (f32[2,8,256]{2,1,0:T(8,128)S(1)}, f32[2,8,256]{2,1,0:T(8,128)S(1)}) fusion(f32[2,256,256,8]{2,1,3,0:T(8,128)S(1)} %get-tuple-element.16, f32[2,8,256]{2,1,0:T(8,128)S(1)} %get-tuple-element.15, pred[256,256]{0,1:T(8,128)(4,1)S(1)} %copy-done.12, f32[2,8,256]{2,1,0:T(8,128)S(1)} %get-tuple-element.13, ...), kind=kLoop, calls=%fused_computation.39 | loop fusion | flops 10477568 | bytes 8519681 | tf_op jit(solution)/shard_map/reduce_sum | solution.py:63
  58.8 2.0 %fusion.27 = (f32[2,8,256]{2,1,0:T(8,128)S(1)}, f32[2,8,256]{2,1,0:T(8,128)S(1)}) fusion(f32[2,256,256,8]{2,1,3,0:T(8,128)S(1)} %get-tuple-element.12, f32[2,8,256]{2,1,0:T(8,128)S(1)} %get-tuple-element.11, pred[]{:T(512)S(6)} %ge.10, f32[2,8,256]{2,1,0:T(8,128)S(1)} %get-tuple-element.17, f32[2,256,256,8]{2,1,3,0:T(8,128)S(1)} %get-tuple-element.18, ...), kind=kLoop, calls=%fused_computation.46 | loop fusion | flops 10477568 | bytes 8454146 | tf_op jit(solution)/shard_map/reduce_sum | solution.py:63
  62.1 1.2 all-to-all-done.4
  64.4 4.3 %fusion.68 = f32[2,256,128,1]{1,2,3,0:T(8,128)} fusion(bf16[256,2,8,128]{0,3,2,1:T(8,128)(2,1)S(1)} %copy.204, f32[2,256,256,8]{2,1,3,0:T(8,128)} %copy-done.6, f32[2,8,256]{2,1,0:T(8,128)} %log_add_fusion, pred[]{:T(512)S(6)} %ge.9), kind=kOutput, calls=%fused_computation.87 | convolution fusion | flops 273678336 | bytes 5521409 | tf_op jit(solution)/shard_map/grtu,tgrd->ugd/dot_general | solution.py:94
  68.6 1.7 fusion.66
  70.9 1.7 fusion.64
  74.3 1.1 fusion.35
  76.6 1.2 fusion.39
  77.8 2.9 %multiply_reduce_fusion = (f32[256,2,8]{0,2,1:T(8,128)S(1)}, bf16[256,2,8,128]{0,3,2,1:T(8,128)(2,1)}) fusion(bf16[256,2,8,128]{0,3,2,1:T(8,128)(2,1)S(1)} %copy.204, f32[256,2,8]{0,2,1:T(8,128)S(1)} %copy-done.33, bf16[256,2,128,1]{0,2,3,1:T(8,128)(2,1)S(1)} %bitcast.433, f32[2,256,256,8]{2,1,3,0:T(8,128)S(1)} %copy-done.1, ...), kind=kOutput, calls=%fused_computation.68 | convolution fusion | flops 281538560 | bytes 12861441 | tf_op jit(solution)/shard_map/grtu,ugd->tgrd/dot_general | solution.py:64
  80.8 2.8 %fusion.7 = bf16[2,8,256,256]{2,3,1,0:T(8,128)(2,1)S(1)} fusion(f32[2,256,256,8]{2,1,3,0:T(8,128)S(1)} %copy-done.5, bf16[256,2,128,1]{0,2,3,1:T(8,128)(2,1)S(1)} %copy-done.28, bf16[256,2,8,128]{0,3,2,1:T(8,128)(2,1)} %copy-done.19, f32[2,8,256]{2,1,0:T(8,128)S(1)} %bitcast.441, f32[2,8,256]{2,1,0:T(8,128)S(1)} %copy-done.31, ...), kind=kOutput, calls=%fused_computation.11 | convolution fusion | flops 275775488 | bytes 7569408 | tf_op jit(solution)/shard_map/tgrd,ugd->grtu/dot_general | solution.py:100
  83.6 2.8 %fusion.5 = bf16[2,8,256,256]{2,3,1,0:T(8,128)(2,1)} fusion(f32[2,256,256,8]{2,1,3,0:T(8,128)S(1)} %copy-done.7, bf16[256,2,128,1]{0,2,3,1:T(8,128)(2,1)S(1)} %bitcast.438, bf16[256,2,8,128]{0,3,2,1:T(8,128)(2,1)S(1)} %copy-done.20, f32[2,8,256]{2,1,0:T(8,128)S(1)} %bitcast.442, f32[2,8,256]{2,1,0:T(8,128)S(1)} %copy-done.31, pred[]{:T(512)S(6)} %ge.9), kind=kOutput, calls=%fused_computation.8 | convolution fusion | flops 275775488 | bytes 7503873 | tf_op jit(solution)/shard_map/tgrd,ugd->grtu/dot_general | solution.py:100
  86.4 2.8 %fusion.3 = bf16[2,8,256,256]{2,3,1,0:T(8,128)(2,1)} fusion(f32[2,256,256,8]{2,1,3,0:T(8,128)S(1)} %copy-done.3, bf16[256,2,128,1]{0,2,3,1:T(8,128)(2,1)S(1)} %bitcast.436, bf16[256,2,8,128]{0,3,2,1:T(8,128)(2,1)S(1)} %copy-done.20, f32[2,8,256]{2,1,0:T(8,128)S(1)} %bitcast.443, f32[2,8,256]{2,1,0:T(8,128)S(1)} %copy-done.31, pred[]{:T(512)S(6)} %ge.10), kind=kOutput, calls=%fused_computation.5 | convolution fusion | flops 275775488 | bytes 7503873 | tf_op jit(solution)/shard_map/tgrd,ugd->grtu/dot_general | solution.py:100
  89.2 2.7 %fusion.1 = bf16[2,8,256,256]{2,3,1,0:T(8,128)(2,1)} fusion(f32[2,256,256,8]{2,1,3,0:T(8,128)S(1)} %copy-done.1, bf16[256,2,128,1]{0,2,3,1:T(8,128)(2,1)S(1)} %bitcast.434, bf16[256,2,8,128]{0,3,2,1:T(8,128)(2,1)S(1)} %copy-done.20, f32[2,8,256]{2,1,0:T(8,128)S(1)} %bitcast.444, f32[2,8,256]{2,1,0:T(8,128)S(1)} %copy-done.31, pred[]{:T(512)S(6)} %ge.11), kind=kOutput, calls=%fused_computation.2 | convolution fusion | flops 275775488 | bytes 7503873 | tf_op jit(solution)/shard_map/tgrd,ugd->grtu/dot_general | solution.py:100
  91.9 1.8 copy.244
  93.7 1.8 copy.241
  95.5 1.8 copy.238
  97.3 8.1 %collective-permute-start.9 = (f32[256,256]{1,0:T(8,128)}, f32[256,256]{1,0:T(8,128)}, u32[]{:S(2)}, u32[]{:S(2)}) collective-permute-start(f32[256,256]{1,0:T(8,128)} %copy.238), channel_id=1, source_target_pairs={{8,0},{12,4},{16,8},{20,12},{24,16},{28,20},{9,1},{13,5},{17,9},{2... | collective-permute-start | bytes 786440 | tf_op jit(solution)/shard_map/ppermute | solution.py:16
  105.4 3.1 %fusion.88 = f32[2,256,128]{1,2,0:T(8,128)} fusion(bf16[2,8,256,256]{2,3,1,0:T(8,128)(2,1)} %fusion.1, bf16[256,2,8,128]{0,3,2,1:T(8,128)(2,1)S(1)} %copy.222), kind=kOutput, calls=%fused_computation.108 | convolution fusion | flops 268500992 | bytes 3407872 | tf_op jit(solution)/shard_map/grtu,tgrd->ugd/dot_general | solution.py:107
  108.5 1.8 copy.225
  110.2 2.7 %fusion.143 = f32[2,8,256,128]{3,2,1,0:T(8,128)S(1)} fusion(bf16[2,8,256,256]{2,3,1,0:T(8,128)(2,1)} %fusion.3, bf16[256,2,128,1]{0,2,3,1:T(8,128)(2,1)S(1)} %bitcast.405), kind=kOutput, calls=%fused_computation.180 | convolution fusion | flops 268435456 | bytes 4325376 | tf_op jit(solution)/shard_map/grtu,ugd->tgrd/dot_general | solution.py:104
  115.8 1.6 copy.219
  117.5 2.3 %all_to_all.126 = bf16[4,64,2048]{2,1,0:T(8,128)(2,1)} reshape(bf16[256,2,8,128]{3,2,1,0:T(8,128)(2,1)} %copy.219) | data formatting | bytes 2097152 | tf_op jit(solution)/shard_map/all_to_all | solution.py:128
  119.8 6.4 %all-to-all-start.5 = ((bf16[4,64,2048]{2,1,0:T(8,128)(2,1)}), bf16[4,64,2048]{2,1,0:T(8,128)(2,1)}, u32[]{:S(2)}, u32[]{:S(2)}) async-start(bf16[4,64,2048]{2,1,0:T(8,128)(2,1)} %all_to_all.126), calls=%async_computation.5 | async-start | bytes 2097152 | tf_op jit(solution)/shard_map/all_to_all | solution.py:128
  126.2 2.4 %fusion.87 = f32[2,256,128]{1,2,0:T(8,128)S(1)} fusion(bf16[2,8,256,256]{2,3,1,0:T(8,128)(2,1)} %fusion.3, bf16[256,2,8,128]{0,3,2,1:T(8,128)(2,1)S(1)} %copy.222), kind=kOutput, calls=%fused_computation.106 | convolution fusion | flops 268500992 | bytes 3407872 | tf_op jit(solution)/shard_map/grtu,tgrd->ugd/dot_general | solution.py:107
  129.5 2.0 %collective-permute-start.6 = (f32[256,256]{1,0:T(8,128)}, f32[256,256]{1,0:T(8,128)}, u32[]{:S(2)}, u32[]{:S(2)}) collective-permute-start(f32[256,256]{1,0:T(8,128)} %copy.225), channel_id=1, source_target_pairs={{8,0},{12,4},{16,8},{20,12},{24,16},{28,20},{9,1},{13,5},{17,9},{2... | collective-permute-start | bytes 786440 | tf_op jit(solution)/shard_map/ppermute | solution.py:16
  131.4 2.6 %copy.199 = bf16[256,2,8,128]{3,2,1,0:T(8,128)(2,1)} copy(bf16[256,2,8,128]{0,3,2,1:T(8,128)(2,1)} %get-tuple-element.20) | data formatting | bytes 2097152 | tf_op jit(solution)/shard_map/convert_element_type | solution.py:83
  134.1 2.3 %all_to_all.119 = bf16[4,64,2048]{2,1,0:T(8,128)(2,1)} reshape(bf16[256,2,8,128]{3,2,1,0:T(8,128)(2,1)} %copy.199) | data formatting | bytes 2097152 | tf_op jit(solution)/shard_map/all_to_all | solution.py:127
  136.4 4.4 %fusion.70 = f32[2,256,128,1]{1,2,3,0:T(8,128)} fusion(bf16[256,2,8,128]{0,3,2,1:T(8,128)(2,1)} %copy-done.19, f32[2,256,256,8]{2,1,3,0:T(8,128)} %copy-done.4, f32[2,8,256]{2,1,0:T(8,128)S(1)} %copy-done.32, pred[256,256]{0,1:T(8,128)(4,1)S(1)} %copy-done.14), kind=kOutput, calls=%fused_computation.88 | convolution fusion | flops 273678336 | bytes 5586944 | tf_op jit(solution)/shard_map/grtu,tgrd->ugd/dot_general | solution.py:94
  140.8 1.7 add.95
  142.5 1.9 %collective-permute-start.10 = (f32[256,256]{1,0:T(8,128)}, f32[256,256]{1,0:T(8,128)}, u32[]{:S(2)}, u32[]{:S(2)}) collective-permute-start(f32[256,256]{1,0:T(8,128)} %add.95), channel_id=1, source_target_pairs={{4,0},{8,4},{12,8},{16,12},{20,16},{24,20},{28,24},{5,1},{9,5},{13... | collective-permute-start | bytes 786440 | tf_op jit(solution)/shard_map/ppermute | solution.py:16
  144.4 1.7 add.92
  146.1 2.0 %collective-permute-start.7 = (f32[256,256]{1,0:T(8,128)}, f32[256,256]{1,0:T(8,128)}, u32[]{:S(2)}, u32[]{:S(2)}) collective-permute-start(f32[256,256]{1,0:T(8,128)} %add.92), channel_id=1, source_target_pairs={{4,0},{8,4},{12,8},{16,12},{20,16},{24,20},{28,24},{5,1},{9,5},{13... | collective-permute-start | bytes 786440 | tf_op jit(solution)/shard_map/ppermute | solution.py:16
  148.2 5.1 %all-to-all-start.3 = ((bf16[4,64,2048]{2,1,0:T(8,128)(2,1)}), bf16[4,64,2048]{2,1,0:T(8,128)(2,1)}, u32[]{:S(2)}, u32[]{:S(2)}) async-start(bf16[4,64,2048]{2,1,0:T(8,128)(2,1)} %all_to_all.119), calls=%async_computation.3 | async-start | bytes 2097152 | tf_op jit(solution)/shard_map/all_to_all | solution.py:127
  153.2 3.1 %fusion.86 = f32[2,256,128]{1,2,0:T(8,128)} fusion(bf16[2,8,256,256]{2,3,1,0:T(8,128)(2,1)} %fusion.5, bf16[256,2,8,128]{0,3,2,1:T(8,128)(2,1)S(1)} %copy.222), kind=kOutput, calls=%fused_computation.104 | convolution fusion | flops 268500992 | bytes 3407872 | tf_op jit(solution)/shard_map/grtu,tgrd->ugd/dot_general | solution.py:107
  156.4 1.8 copy.231
  158.1 1.7 add.96
  159.8 1.9 %collective-permute-start.11 = (f32[256,256]{1,0:T(8,128)}, f32[256,256]{1,0:T(8,128)}, u32[]{:S(2)}, u32[]{:S(2)}) collective-permute-start(f32[256,256]{1,0:T(8,128)} %add.96), channel_id=1, source_target_pairs={{4,0},{8,4},{12,8},{16,12},{20,16},{24,20},{28,24},{5,1},{9,5},{13... | collective-permute-start | bytes 786440 | tf_op jit(solution)/shard_map/ppermute | solution.py:16
  161.8 1.8 add.93
  163.5 1.9 %collective-permute-start.8 = (f32[256,256]{1,0:T(8,128)}, f32[256,256]{1,0:T(8,128)}, u32[]{:S(2)}, u32[]{:S(2)}) collective-permute-start(f32[256,256]{1,0:T(8,128)} %add.93), channel_id=1, source_target_pairs={{4,0},{8,4},{12,8},{16,12},{20,16},{24,20},{28,24},{5,1},{9,5},{13... | collective-permute-start | bytes 786440 | tf_op jit(solution)/shard_map/ppermute | solution.py:16
  166.3 1.1 copy.245
  167.5 2.1 %collective-permute-done.11 = f32[256,256]{1,0:T(8,128)} collective-permute-done((f32[256,256]{1,0:T(8,128)}, f32[256,256]{1,0:T(8,128)}, u32[]{:S(2)}, u32[]{:S(2)}) %collective-permute-start.11) | collective-permute-done | bytes 262176 | tf_op jit(solution)/shard_map/ppermute | solution.py:16
  169.6 1.6 add_convert_fusion
  171.2 4.9 %all-to-all-start.7 = ((bf16[4,64,256]{2,1,0:T(8,128)(2,1)}), bf16[4,64,256]{2,1,0:T(8,128)(2,1)S(1)}, u32[]{:S(2)}, u32[]{:S(2)}) async-start(bf16[4,64,256]{2,1,0:T(8,128)(2,1)} %bitcast.91), calls=%async_computation.7 | async-start | bytes 262144 | tf_op jit(solution)/shard_map/all_to_all | solution.py:132
  176.1 1.6 add_convert_fusion.1
  177.8 1.1 all-to-all-done.7
  178.9 5.2 %all-to-all-start.6 = ((bf16[4,64,256]{2,1,0:T(8,128)(2,1)}), bf16[4,64,256]{2,1,0:T(8,128)(2,1)S(1)}, u32[]{:S(2)}, u32[]{:S(2)}) async-start(bf16[4,64,256]{2,1,0:T(8,128)(2,1)} %bitcast.73), calls=%async_computation.6 | async-start | bytes 262144 | tf_op jit(solution)/shard_map/all_to_all | solution.py:129
  184.1 2.3 %copy.318 = bf16[4,8,8,2048]{3,2,0,1:T(8,128)(2,1)} copy(bf16[4,8,8,2048]{3,2,1,0:T(8,128)(2,1)} %bitcast.136) | data formatting | bytes 2097152 | tf_op jit(solution)/shard_map/all_to_all | solution.py:128
  186.4 2.3 %copy.317 = bf16[4,8,8,2048]{3,2,0,1:T(8,128)(2,1)} copy(bf16[4,8,8,2048]{3,2,1,0:T(8,128)(2,1)} %bitcast.134) | data formatting | bytes 2097152 | tf_op jit(solution)/shard_map/all_to_all | solution.py:127
  (124 shorter events, 23.2 us)
Async XLA Ops:
  0.6 35.9 %copy-start.18 = (bf16[64,8192]{1,0:T(8,128)(2,1)S(1)}, bf16[64,8192]{1,0:T(8,128)(2,1)}, u32[]{:S(2)}) copy-start(bf16[64,8192]{1,0:T(8,128)(2,1)} %param.7) | copy-start | bytes 3145732
  2.3 6.8 %all-to-all-start = ((bf16[64,4,256]{2,0,1:T(8,128)(2,1)}), bf16[64,4,256]{2,0,1:T(8,128)(2,1)S(1)}, u32[]{:S(2)}, u32[]{:S(2)}) async-start(bf16[64,4,256]{2,0,1:T(8,128)(2,1)} %bitcast.395), calls=%async_computation | async-start | bytes 262144 | tf_op jit(solution)/shard_map/all_to_all | solution.py:30
  9.1 7.9 %all-to-all-start.2 = ((bf16[64,4,256]{2,0,1:T(8,128)(2,1)}), bf16[64,4,256]{2,0,1:T(8,128)(2,1)S(1)}, u32[]{:S(2)}, u32[]{:S(2)}) async-start(bf16[64,4,256]{2,0,1:T(8,128)(2,1)} %bitcast.394), calls=%async_computation.2 | async-start | bytes 262144 | tf_op jit(solution)/shard_map/all_to_all | solution.py:31
  17.1 26.2 %all-to-all-start.1 = ((bf16[64,4,2048]{2,0,1:T(8,128)(2,1)}), bf16[64,4,2048]{2,0,1:T(8,128)(2,1)S(1)}, u32[]{:S(2)}, u32[]{:S(2)}) async-start(bf16[64,4,2048]{2,0,1:T(8,128)(2,1)} %bitcast.393), calls=%async_computation.1 | async-start | bytes 2097152 | tf_op jit(solution)/shard_map/all_to_all | solution.py:28
  22.5 11.0 %collective-permute-start.5 = (bf16[256,256]{1,0:T(8,128)(2,1)S(1)}, bf16[256,256]{1,0:T(8,128)(2,1)S(1)}, u32[]{:S(2)}, u32[]{:S(2)}) collective-permute-start(bf16[256,256]{1,0:T(8,128)(2,1)S(1)} %bitcast.420), channel_id=1, source_target_pairs={{0,16},{4,20},{8,24},{12,28},{1,17},{5,21},{9,25},{13,29},{2,18},{... | collective-permute-start | bytes 393224 | tf_op jit(solution)/shard_map/ppermute | solution.py:16
  23.8 16.1 %collective-permute-start.4 = (bf16[256,256]{1,0:T(8,128)(2,1)S(1)}, bf16[256,256]{1,0:T(8,128)(2,1)S(1)}, u32[]{:S(2)}, u32[]{:S(2)}) collective-permute-start(bf16[256,256]{1,0:T(8,128)(2,1)S(1)} %bitcast.421), channel_id=1, source_target_pairs={{0,8},{4,12},{8,16},{12,20},{16,24},{20,28},{1,9},{5,13},{9,17},{1... | collective-permute-start | bytes 393224 | tf_op jit(solution)/shard_map/ppermute | solution.py:16
  25.1 15.6 %collective-permute-start.3 = (bf16[256,256]{1,0:T(8,128)(2,1)S(1)}, bf16[256,256]{1,0:T(8,128)(2,1)S(1)}, u32[]{:S(2)}, u32[]{:S(2)}) collective-permute-start(bf16[256,256]{1,0:T(8,128)(2,1)S(1)} %bitcast.422), channel_id=1, source_target_pairs={{0,4},{4,8},{8,12},{12,16},{16,20},{20,24},{24,28},{1,5},{5,9},{9,... | collective-permute-start | bytes 393224 | tf_op jit(solution)/shard_map/ppermute | solution.py:16
  28.2 13.7 %collective-permute-start.2 = (bf16[256,256]{1,0:T(8,128)(2,1)S(1)}, bf16[256,256]{1,0:T(8,128)(2,1)S(1)}, u32[]{:S(2)}, u32[]{:S(2)}) collective-permute-start(bf16[256,256]{1,0:T(8,128)(2,1)S(1)} %bitcast.416), channel_id=1, source_target_pairs={{0,16},{4,20},{8,24},{12,28},{1,17},{5,21},{9,25},{13,29},{2,18},{... | collective-permute-start | bytes 393224 | tf_op jit(solution)/shard_map/ppermute | solution.py:16
  29.5 12.5 %collective-permute-start.1 = (bf16[256,256]{1,0:T(8,128)(2,1)S(1)}, bf16[256,256]{1,0:T(8,128)(2,1)S(1)}, u32[]{:S(2)}, u32[]{:S(2)}) collective-permute-start(bf16[256,256]{1,0:T(8,128)(2,1)S(1)} %bitcast.417), channel_id=1, source_target_pairs={{0,8},{4,12},{8,16},{12,20},{16,24},{20,28},{1,9},{5,13},{9,17},{1... | collective-permute-start | bytes 393224 | tf_op jit(solution)/shard_map/ppermute | solution.py:16
  33.4 9.1 %collective-permute-start = (bf16[256,256]{1,0:T(8,128)(2,1)S(1)}, bf16[256,256]{1,0:T(8,128)(2,1)S(1)}, u32[]{:S(2)}, u32[]{:S(2)}) collective-permute-start(bf16[256,256]{1,0:T(8,128)(2,1)S(1)} %bitcast.418), channel_id=1, source_target_pairs={{0,4},{4,8},{8,12},{12,16},{16,20},{20,24},{24,28},{1,5},{5,9},{9,... | collective-permute-start | bytes 393224 | tf_op jit(solution)/shard_map/ppermute | solution.py:16
  43.3 20.0 %all-to-all-start.4 = ((bf16[64,4,2048]{2,0,1:T(8,128)(2,1)}), bf16[64,4,2048]{2,0,1:T(8,128)(2,1)S(1)}, u32[]{:S(2)}, u32[]{:S(2)}) async-start(bf16[64,4,2048]{2,0,1:T(8,128)(2,1)} %bitcast.392), calls=%async_computation.4 | async-start | bytes 2097152 | tf_op jit(solution)/shard_map/all_to_all | solution.py:29
  51.8 0.9 copy-start.10
  52.6 6.2 %copy-start = (f32[2,256,256,8]{2,1,3,0:T(8,128)}, f32[2,256,256,8]{2,1,3,0:T(8,128)S(1)}, u32[]{:S(2)}) copy-start(f32[2,256,256,8]{2,1,3,0:T(8,128)S(1)} %get-tuple-element.18) | copy-start | bytes 12582916
  52.7 1.6 copy-start.12
  53.5 3.0 %copy-start.6 = (f32[2,256,256,8]{2,1,3,0:T(8,128)}, f32[2,256,256,8]{2,1,3,0:T(8,128)S(1)}, u32[]{:S(2)}) copy-start(f32[2,256,256,8]{2,1,3,0:T(8,128)S(1)} %get-tuple-element.14) | copy-start | bytes 12582916
  53.5 7.9 %copy-start.21 = (f32[2,8,256]{2,1,0:T(8,128)}, f32[2,8,256]{2,1,0:T(8,128)S(1)}, u32[]{:S(2)}) copy-start(f32[2,8,256]{2,1,0:T(8,128)S(1)} %get-tuple-element.13) | copy-start | bytes 49156
  54.3 4.5 %copy-start.2 = (f32[2,256,256,8]{2,1,3,0:T(8,128)}, f32[2,256,256,8]{2,1,3,0:T(8,128)S(1)}, u32[]{:S(2)}) copy-start(f32[2,256,256,8]{2,1,3,0:T(8,128)S(1)} %get-tuple-element.12) | copy-start | bytes 12582916
  54.3 7.1 %copy-start.23 = (f32[2,8,256]{2,1,0:T(8,128)}, f32[2,8,256]{2,1,0:T(8,128)S(1)}, u32[]{:S(2)}) copy-start(f32[2,8,256]{2,1,0:T(8,128)S(1)} %get-tuple-element.11) | copy-start | bytes 49156
  55.2 3.6 %copy-start.4 = (f32[2,256,256,8]{2,1,3,0:T(8,128)}, f32[2,256,256,8]{2,1,3,0:T(8,128)S(1)}, u32[]{:S(2)}) copy-start(f32[2,256,256,8]{2,1,3,0:T(8,128)S(1)} %get-tuple-element.16) | copy-start | bytes 12582916
  55.2 6.3 %copy-start.25 = (f32[2,8,256]{2,1,0:T(8,128)}, f32[2,8,256]{2,1,0:T(8,128)S(1)}, u32[]{:S(2)}) copy-start(f32[2,8,256]{2,1,0:T(8,128)S(1)} %get-tuple-element.15) | copy-start | bytes 49156
  64.3 13.4 %copy-start.19 = (bf16[256,2,8,128]{0,3,2,1:T(8,128)(2,1)}, bf16[256,2,8,128]{0,3,2,1:T(8,128)(2,1)S(1)}, u32[]{:S(2)}) copy-start(bf16[256,2,8,128]{0,3,2,1:T(8,128)(2,1)S(1)} %copy.204) | copy-start | bytes 3145732
  64.3 4.3 %copy-start.3 = (f32[2,256,256,8]{2,1,3,0:T(8,128)S(1)}, f32[2,256,256,8]{2,1,3,0:T(8,128)}, u32[]{:S(2)}) copy-start(f32[2,256,256,8]{2,1,3,0:T(8,128)} %copy-done.2) | copy-start | bytes 12582916
  64.4 4.3 %copy-start.31 = (f32[2,8,256]{2,1,0:T(8,128)S(1)}, f32[2,8,256]{2,1,0:T(8,128)}, u32[]{:S(2)}) copy-start(f32[2,8,256]{2,1,0:T(8,128)} %log_add_fusion) | copy-start | bytes 49156
  68.6 2.3 %copy-start.1 = (f32[2,256,256,8]{2,1,3,0:T(8,128)S(1)}, f32[2,256,256,8]{2,1,3,0:T(8,128)}, u32[]{:S(2)}) copy-start(f32[2,256,256,8]{2,1,3,0:T(8,128)} %copy-done) | copy-start | bytes 12582916
  70.9 2.3 %copy-start.7 = (f32[2,256,256,8]{2,1,3,0:T(8,128)S(1)}, f32[2,256,256,8]{2,1,3,0:T(8,128)}, u32[]{:S(2)}) copy-start(f32[2,256,256,8]{2,1,3,0:T(8,128)} %copy-done.6) | copy-start | bytes 12582916
  70.9 2.3 %copy-start.22 = (f32[2,8,256]{2,1,0:T(8,128)S(1)}, f32[2,8,256]{2,1,0:T(8,128)}, u32[]{:S(2)}) copy-start(f32[2,8,256]{2,1,0:T(8,128)} %copy-done.21) | copy-start | bytes 49156
  70.9 2.3 %copy-start.30 = (bf16[256,256]{0,1:T(8,128)(2,1)S(1)}, bf16[256,256]{0,1:T(8,128)(2,1)}, u32[]{:S(2)}) copy-start(bf16[256,256]{0,1:T(8,128)(2,1)} %copy.193) | copy-start | bytes 393220
  72.6 1.7 copy-start.24
  72.6 1.7 copy-start.29
  74.3 2.2 %copy-start.5 = (f32[2,256,256,8]{2,1,3,0:T(8,128)S(1)}, f32[2,256,256,8]{2,1,3,0:T(8,128)}, u32[]{:S(2)}) copy-start(f32[2,256,256,8]{2,1,3,0:T(8,128)} %copy-done.4) | copy-start | bytes 12582916
  74.3 2.2 %copy-start.13 = (pred[256,256]{0,1:T(8,128)(4,1)S(1)}, pred[256,256]{0,1:T(8,128)(4,1)}, u32[]{:S(2)}) copy-start(pred[256,256]{0,1:T(8,128)(4,1)} %iota_compare_fusion) | copy-start | bytes 196612
  74.3 2.2 %copy-start.26 = (f32[2,8,256]{2,1,0:T(8,128)S(1)}, f32[2,8,256]{2,1,0:T(8,128)}, u32[]{:S(2)}) copy-start(f32[2,8,256]{2,1,0:T(8,128)} %copy-done.25) | copy-start | bytes 49156
  74.3 2.2 %copy-start.28 = (bf16[256,2,128,1]{0,2,3,1:T(8,128)(2,1)S(1)}, bf16[256,2,128,1]{0,2,3,1:T(8,128)(2,1)}, u32[]{:S(2)}) copy-start(bf16[256,2,128,1]{0,2,3,1:T(8,128)(2,1)} %copy.252) | copy-start | bytes 393220
  76.5 1.3 copy-start.27
  76.5 1.3 copy-start.33
  76.5 1.3 copy-start.34
  76.5 1.3 copy-start.35
  76.5 1.3 copy-start.36
  76.5 1.3 copy-start.37
  76.5 1.3 copy-start.38
  76.6 1.3 copy-start.39
  80.8 2.8 %copy-start.20 = (bf16[256,2,8,128]{0,3,2,1:T(8,128)(2,1)S(1)}, bf16[256,2,8,128]{0,3,2,1:T(8,128)(2,1)}, u32[]{:S(2)}) copy-start(bf16[256,2,8,128]{0,3,2,1:T(8,128)(2,1)} %copy-done.19) | copy-start | bytes 3145732
  97.3 43.5 %collective-permute-start.9 = (f32[256,256]{1,0:T(8,128)}, f32[256,256]{1,0:T(8,128)}, u32[]{:S(2)}, u32[]{:S(2)}) collective-permute-start(f32[256,256]{1,0:T(8,128)} %copy.238), channel_id=1, source_target_pairs={{8,0},{12,4},{16,8},{20,12},{24,16},{28,20},{9,1},{13,5},{17,9},{2... | collective-permute-start | bytes 786440 | tf_op jit(solution)/shard_map/ppermute | solution.py:16
  110.2 3.6 %copy-start.8 = (bf16[2,8,256,256]{2,3,1,0:T(8,128)(2,1)S(1)}, bf16[2,8,256,256]{2,3,1,0:T(8,128)(2,1)}, u32[]{:S(2)}) copy-start(bf16[2,8,256,256]{2,3,1,0:T(8,128)(2,1)} %fusion.5) | copy-start | bytes 6291460
  110.2 3.6 %copy-start.11 = (bf16[256,256]{0,1:T(8,128)(2,1)S(1)}, bf16[256,256]{0,1:T(8,128)(2,1)}, u32[]{:S(2)}) copy-start(bf16[256,256]{0,1:T(8,128)(2,1)} %copy.181) | copy-start | bytes 393220
  112.9 1.9 copy-start.9
  119.8 28.4 %all-to-all-start.5 = ((bf16[4,64,2048]{2,1,0:T(8,128)(2,1)}), bf16[4,64,2048]{2,1,0:T(8,128)(2,1)}, u32[]{:S(2)}, u32[]{:S(2)}) async-start(bf16[4,64,2048]{2,1,0:T(8,128)(2,1)} %all_to_all.126), calls=%async_computation.5 | async-start | bytes 2097152 | tf_op jit(solution)/shard_map/all_to_all | solution.py:128
  126.2 10.2 %copy-start.14 = (pred[256,256]{0,1:T(8,128)(4,1)S(1)}, pred[256,256]{0,1:T(8,128)(4,1)}, u32[]{:S(2)}) copy-start(pred[256,256]{0,1:T(8,128)(4,1)} %iota_compare_fusion) | copy-start | bytes 196612
  126.2 10.2 %copy-start.32 = (f32[2,8,256]{2,1,0:T(8,128)S(1)}, f32[2,8,256]{2,1,0:T(8,128)}, u32[]{:S(2)}) copy-start(f32[2,8,256]{2,1,0:T(8,128)} %log_add_fusion) | copy-start | bytes 49156
  129.5 14.9 %collective-permute-start.6 = (f32[256,256]{1,0:T(8,128)}, f32[256,256]{1,0:T(8,128)}, u32[]{:S(2)}, u32[]{:S(2)}) collective-permute-start(f32[256,256]{1,0:T(8,128)} %copy.225), channel_id=1, source_target_pairs={{8,0},{12,4},{16,8},{20,12},{24,16},{28,20},{9,1},{13,5},{17,9},{2... | collective-permute-start | bytes 786440 | tf_op jit(solution)/shard_map/ppermute | solution.py:16
  136.4 4.4 %copy-start.16 = (f32[256,256]{1,0:T(8,128)S(1)}, f32[256,256]{1,0:T(8,128)}, u32[]{:S(2)}) copy-start(f32[256,256]{1,0:T(8,128)} %copy.241) | copy-start | bytes 786436
  136.4 8.0 %copy-start.17 = (f32[256,256]{1,0:T(8,128)S(1)}, f32[256,256]{1,0:T(8,128)}, u32[]{:S(2)}) copy-start(f32[256,256]{1,0:T(8,128)} %copy.228) | copy-start | bytes 786436
  140.7 17.4 %copy-start.15 = (f32[256,256]{1,0:T(8,128)S(1)}, f32[256,256]{1,0:T(8,128)}, u32[]{:S(2)}) copy-start(f32[256,256]{1,0:T(8,128)} %copy.244) | copy-start | bytes 786436
  142.5 15.7 %collective-permute-start.10 = (f32[256,256]{1,0:T(8,128)}, f32[256,256]{1,0:T(8,128)}, u32[]{:S(2)}, u32[]{:S(2)}) collective-permute-start(f32[256,256]{1,0:T(8,128)} %add.95), channel_id=1, source_target_pairs={{4,0},{8,4},{12,8},{16,12},{20,16},{24,20},{28,24},{5,1},{9,5},{13... | collective-permute-start | bytes 786440 | tf_op jit(solution)/shard_map/ppermute | solution.py:16
  146.1 15.7 %collective-permute-start.7 = (f32[256,256]{1,0:T(8,128)}, f32[256,256]{1,0:T(8,128)}, u32[]{:S(2)}, u32[]{:S(2)}) collective-permute-start(f32[256,256]{1,0:T(8,128)} %add.92), channel_id=1, source_target_pairs={{4,0},{8,4},{12,8},{16,12},{20,16},{24,20},{28,24},{5,1},{9,5},{13... | collective-permute-start | bytes 786440 | tf_op jit(solution)/shard_map/ppermute | solution.py:16
  148.2 23.0 %all-to-all-start.3 = ((bf16[4,64,2048]{2,1,0:T(8,128)(2,1)}), bf16[4,64,2048]{2,1,0:T(8,128)(2,1)}, u32[]{:S(2)}, u32[]{:S(2)}) async-start(bf16[4,64,2048]{2,1,0:T(8,128)(2,1)} %all_to_all.119), calls=%async_computation.3 | async-start | bytes 2097152 | tf_op jit(solution)/shard_map/all_to_all | solution.py:127
  159.8 9.7 %collective-permute-start.11 = (f32[256,256]{1,0:T(8,128)}, f32[256,256]{1,0:T(8,128)}, u32[]{:S(2)}, u32[]{:S(2)}) collective-permute-start(f32[256,256]{1,0:T(8,128)} %add.96), channel_id=1, source_target_pairs={{4,0},{8,4},{12,8},{16,12},{20,16},{24,20},{28,24},{5,1},{9,5},{13... | collective-permute-start | bytes 786440 | tf_op jit(solution)/shard_map/ppermute | solution.py:16
  163.5 12.6 %collective-permute-start.8 = (f32[256,256]{1,0:T(8,128)}, f32[256,256]{1,0:T(8,128)}, u32[]{:S(2)}, u32[]{:S(2)}) collective-permute-start(f32[256,256]{1,0:T(8,128)} %add.93), channel_id=1, source_target_pairs={{4,0},{8,4},{12,8},{16,12},{20,16},{24,20},{28,24},{5,1},{9,5},{13... | collective-permute-start | bytes 786440 | tf_op jit(solution)/shard_map/ppermute | solution.py:16
  171.2 7.6 %all-to-all-start.7 = ((bf16[4,64,256]{2,1,0:T(8,128)(2,1)}), bf16[4,64,256]{2,1,0:T(8,128)(2,1)S(1)}, u32[]{:S(2)}, u32[]{:S(2)}) async-start(bf16[4,64,256]{2,1,0:T(8,128)(2,1)} %bitcast.91), calls=%async_computation.7 | async-start | bytes 262144 | tf_op jit(solution)/shard_map/all_to_all | solution.py:132
  178.9 10.5 %all-to-all-start.6 = ((bf16[4,64,256]{2,1,0:T(8,128)(2,1)}), bf16[4,64,256]{2,1,0:T(8,128)(2,1)S(1)}, u32[]{:S(2)}, u32[]{:S(2)}) async-start(bf16[4,64,256]{2,1,0:T(8,128)(2,1)} %bitcast.73), calls=%async_computation.6 | async-start | bytes 262144 | tf_op jit(solution)/shard_map/all_to_all | solution.py:129
where the time goes:
time: 192 us; the launch traced here: 190 us
  starting transfers between devices  73 us (38%)
  matrix products  47.4 us (25%)
  local copies, waits for them, and re-layouts  42.3 us (22%)
  other arithmetic  16.3 us (8%)
  waiting for transfers between devices  9.61 us (5%)
    ppermute x12, starting transfers between devices, shifted(): return lax.ppermute(array, axis, pairs)  29.3 us
    dot_general x4, matrix products, shards(): jnp.einsum('grtu,tgrd->ugd', probs.astype(jnp.bfloat16), grad_rows, prefe...  12 us
    dot_general x4, matrix products, shards(): jnp.einsum('tgrd,ugd->grtu', grad_rows, value_rows, preferred_element_typ...  11.1 us
    dot_general x4, matrix products, shards(): jnp.einsum('grtu,tgrd->ugd', grad_scores, queries, preferred_element_type...  9.43 us
    all_to_all x1, starting transfers between devices, shards(): lax.all_to_all(grad_out, 'kvh', split_axis=1, concat_axis=0, tiled=True)  7.42 us
    add x4, other arithmetic, shards(): carried = (carried[0] + partial_terms[0], carried[1] + partial_terms[1])  6.88 us
    reshape x4, local copies, waits for them, and re-layouts, shards(): grad_val.reshape(block_len, groups * HD)  6.41 us
    all_to_all x1, starting transfers between devices, shards(): lax.all_to_all(grad_flat, 'kvh', split_axis=0, concat_axis=1, tiled=True)  6.41 us
  transfers between devices with their start and end apart: 20, of which 8 were waited for; matrix products, arithmetic and copies ran while one was open for 34% of the time, Pallas kernels for 0%

commit v1 on v0

v1 whole, which is shorter than its diff:
```python
import jax
import jax.numpy as jnp
from jax import lax
from jax.experimental import pallas as pl
from jax.experimental.pallas import tpu as pltpu
from jax.sharding import PartitionSpec as P

HD = 128
LOG2E = 1.4426950408889634
LOW = -1e30

NT = (((1,), (1,)), ((), ()))
NN = (((1,), (0,)), ((), ()))
TN = (((0,), (0,)), ((), ()))


def mm(a, b, dims):
    return lax.dot_general(a, b, dims, preferred_element_type=jnp.float32)


def attention_kernel(levels, peers, group, *refs):
    count = levels * peers
    q_ref, g_ref = refs[:2]
    kv_refs = refs[2 : 2 + count]
    o_ref, dq_ref = refs[2 + count : 4 + count]
    dkv_refs = refs[4 + count :]
    rows = q_ref.shape[0]
    heads = kv_refs[0].shape[1] // (2 * HD)
    width = heads * HD
    wide = group * rows
    scale = HD ** (-0.5)
    factor = scale * LOG2E
    ctx = lax.axis_index("ctx")
    kvh = lax.axis_index("kvh")
    valid = []
    for level in range(levels):
        for j in range(peers):
            if level == 0:
                valid.append(None if j == 0 else lax.bitwise_xor(kvh, j) < kvh)
            else:
                valid.append(ctx >= (1 << (level - 1)))

    def stack(ref, g):
        return jnp.concatenate(
            [ref[:, pl.ds(pl.multiple_of((g * group + r) * HD, HD), HD)] for r in range(group)], axis=0
        )

    def unstack(ref, g, value):
        for r in range(group):
            ref[:, pl.ds(pl.multiple_of((g * group + r) * HD, HD), HD)] = value[r * rows : (r + 1) * rows]

    def head(g, carry):
        queries = stack(q_ref, g)
        grads = stack(g_ref, g)
        at_k = pl.ds(pl.multiple_of(g * HD, HD), HD)
        at_v = pl.ds(pl.multiple_of(g * HD + width, HD), HD)
        keys, values, scores = [], [], []
        top = None
        key_pos = lax.broadcasted_iota(jnp.int32, (rows, wide), 0)
        query_pos = lax.broadcasted_iota(jnp.int32, (rows, wide), 1) % rows
        causal = key_pos <= query_pos
        for level in range(levels):
            part = kv_refs[level * peers : (level + 1) * peers]
            keys.append(jnp.concatenate([ref[:, at_k] for ref in part], axis=0))
            values.append(jnp.concatenate([ref[:, at_v] for ref in part], axis=0))
            raw = mm(keys[level], queries, NT)
            for j in range(peers):
                piece = raw[j * rows : (j + 1) * rows]
                ok = valid[level * peers + j]
                if ok is None:
                    piece = jnp.where(causal, piece, LOW)
                best = jnp.max(piece, axis=0, keepdims=True)
                if ok is not None:
                    best = jnp.where(ok, best, LOW)
                top = best if top is None else jnp.maximum(top, best)
                scores.append(piece)
        top = top * factor
        total = None
        expo = []
        for index in range(levels * peers):
            ok = valid[index]
            shift = top if ok is None else jnp.where(ok, top, -LOW)
            weight = jnp.exp2(scores[index] * factor - shift)
            part = jnp.sum(weight, axis=0, keepdims=True)
            total = part if total is None else total + part
            expo.append(weight)
        inverse = 1.0 / total
        probs, low, out_t = [], [], None
        for level in range(levels):
            prob = jnp.concatenate(expo[level * peers : (level + 1) * peers], axis=0) * inverse
            probs.append(prob)
            low.append(prob.astype(jnp.bfloat16))
            part = mm(values[level], low[level], TN)
            out_t = part if out_t is None else out_t + part
        out = out_t.T.astype(jnp.bfloat16)
        unstack(o_ref, g, out)
        delta = jnp.sum(
            grads.astype(jnp.float32).T * out_t.astype(jnp.bfloat16).astype(jnp.float32), axis=0, keepdims=True
        )
        dq_t = None
        for level in range(levels):
            grad_prob = mm(values[level], grads, NT)
            grad_scores = (probs[level] * (grad_prob - delta)).astype(jnp.bfloat16)
            part = mm(keys[level], grad_scores, TN)
            dq_t = part if dq_t is None else dq_t + part
            grad_k = (mm(grad_scores, queries, NN) * scale).astype(jnp.bfloat16)
            grad_v = mm(low[level], grads, NN).astype(jnp.bfloat16)
            for j in range(peers):
                ref = dkv_refs[level * peers + j]
                ref[:, at_k] = grad_k[j * rows : (j + 1) * rows]
                ref[:, at_v] = grad_v[j * rows : (j + 1) * rows]
        unstack(dq_ref, g, (dq_t * scale).T.astype(jnp.bfloat16))
        return carry

    lax.fori_loop(0, heads, head, 0)


def attention(query, grad, shards, levels, peers):
    rows, q_width = query.shape
    kv_width = shards[0].shape[1]
    group = 2 * q_width // kv_width
    spec = pl.BlockSpec(memory_space=pltpu.VMEM)
    q_shape = jax.ShapeDtypeStruct(query.shape, jnp.bfloat16)
    kv_shape = jax.ShapeDtypeStruct((rows, kv_width), jnp.bfloat16)
    keys = levels * peers * rows
    return pl.pallas_call(
        lambda *refs: attention_kernel(levels, peers, group, *refs),
        out_shape=[q_shape] * 2 + [kv_shape] * (levels * peers),
        in_specs=[spec] * (2 + levels * peers),
        out_specs=[spec] * (2 + levels * peers),
        compiler_params=pltpu.CompilerParams(vmem_limit_bytes=48 * 2**20),
        cost_estimate=pl.CostEstimate(
            flops=12 * rows * q_width * keys, bytes_accessed=8 * rows * q_width, transcendentals=0
        ),
        name="attention",
    )(query, grad, *shards)


AXES = ("ctx", "kvh")


def permute(array, target):
    blocks, peers = lax.axis_size("ctx"), lax.axis_size("kvh")
    pairs = []
    for c in range(blocks):
        for k in range(peers):
            to_c, to_k = target(c, k)
            if 0 <= to_c < blocks:
                pairs.append((c * peers + k, to_c * peers + to_k))
    return lax.ppermute(array, AXES, pairs)


def along(array, by):
    return permute(array, lambda c, k: (c + by, k))


def pair_swap(array):
    return permute(array, lambda c, k: (c ^ 1, k))


def across(array, bit):
    return permute(array, lambda c, k: (c, k ^ bit))


def add(*terms):
    total = terms[0].astype(jnp.float32)
    for term in terms[1:]:
        total = total + term.astype(jnp.float32)
    return total


def low(array):
    return array.astype(jnp.bfloat16)


def shards(query_act, key_act, value_act, grad_out):
    blocks, peers = lax.axis_size("ctx"), lax.axis_size("kvh")
    far = (blocks - 1).bit_length()
    levels = far + 1
    odd = lax.axis_index("ctx") % 2 == 1
    own = jnp.concatenate([key_act, value_act], axis=1)
    held = {(0, 0): own}
    half = peers // 2
    held[2, 0] = along(own, 2)
    held[0, half] = across(own, half)
    held[1, 0] = pair_swap(jnp.where(odd, held[2, 0], own))
    held[2, half] = across(held[2, 0], half)
    for level in range(3, levels):
        held[level, 0] = along(held[level - 1, 0], 1 << (level - 2))
        held[level, half] = along(held[level - 1, half], 1 << (level - 2))
    held[1, half] = across(held[1, 0], half)
    bit = half // 2
    while bit:
        for level in range(levels):
            for j in range(0, peers, 2 * bit):
                held[level, j + bit] = across(held[level, j], bit)
        bit //= 2
    order = [(level, j) for level in range(levels) for j in range(peers)]
    out, grad_query, *parts = attention(query_act, grad_out, [held[at] for at in order], levels, peers)
    sums = dict(zip(order, parts))
    bit = 1
    while bit < half:
        for level in range(levels):
            for j in range(0, peers, 2 * bit):
                sums[level, j] = low(add(sums[level, j], across(sums[level, j + bit], bit)))
        bit *= 2
    for level in range(levels - 1, 2, -1):
        moved = along(sums[level, half], -(1 << (level - 2)))
        sums[level - 1, half] = low(add(sums[level - 1, half], moved))
        moved = along(sums[level, 0], -(1 << (level - 2)))
        sums[level - 1, 0] = low(add(sums[level - 1, 0], moved))
    sums[1, 0] = low(add(sums[1, 0], across(sums[1, half], half)))
    swapped = pair_swap(sums[1, 0])
    nothing = jnp.zeros_like(swapped)
    sums[2, 0] = low(add(sums[2, 0], across(sums[2, half], half), jnp.where(odd, swapped, nothing)))
    total = add(
        sums[0, 0],
        across(sums[0, half], half),
        jnp.where(odd, nothing, swapped),
        along(sums[2, 0], -2),
    )
    total = low(total)
    width = key_act.shape[1]
    return out, grad_query, total[:, :width], total[:, width:]


def solution(mesh):
    spec = P(AXES, None)
    return jax.shard_map(
        shards, mesh=mesh, in_specs=(spec,) * 4, out_specs=(spec,) * 4, check_vma=False
    )
```

time: 192 us -> 100 us (0.52)
  the two profiles are of different devices: /device:TPU:29 before, /device:TPU:0 now
where the time goes in v1:
time: 100 us
  waiting for transfers between devices  40.9 us (41%)
  starting transfers between devices  30.3 us (30%)
  Pallas kernels  24.7 us (25%)
  local copies, waits for them, and re-layouts  2.41 us (2%)
    ppermute x30, waiting for transfers between devices, permute(): return lax.ppermute(array, AXES, pairs)  40.9 us
    ppermute x30, starting transfers between devices, permute(): return lax.ppermute(array, AXES, pairs)  30.3 us
    pallas_call x1, Pallas kernels, attention(): pl.pallas_call(lambda *refs: attention_kernel(levels, peers, group, *refs...  24.7 us
  transfers between devices with their start and end apart: 30, of which 15 were waited for; matrix products, arithmetic and copies ran while one was open for 1% of the time, Pallas kernels for 0%

profile of v1, /device:TPU:0, one launch (start us, length us, event | category | flops | bytes accessed | tf_op | source)
XLA Modules:
  0.0 100.0 jit_solution(17679295823121631560)
XLA Ops:
  0.6 0.9 constant_dynamic-update-slice_fusion.1
  1.6 0.0 copy-done.1
  1.6 4.9 %collective-permute-start.3 = (bf16[64,2048]{1,0:T(8,128)(2,1)S(1)}, bf16[64,2048]{1,0:T(8,128)(2,1)S(1)}, u32[]{:S(2)}, u32[]{:S(2)}) collective-permute-start(bf16[64,2048]{1,0:T(8,128)(2,1)S(1)} %constant_dynamic-update-slice_fusion.refs_2_), channel_id=1, source_target_pairs={{0,8},{1,9},{2,10},{3,11},{4,12},{5,13},{6,14},{7,15},{8,16},{9,17... | collective-permute-start | bytes 786440 | tf_op jit(solution)/shard_map/ppermute | solution.py:150
  6.6 1.6 %collective-permute-start.1 = (bf16[64,2048]{1,0:T(8,128)(2,1)S(1)}, bf16[64,2048]{1,0:T(8,128)(2,1)S(1)}, u32[]{:S(2)}, u32[]{:S(2)}) collective-permute-start(bf16[64,2048]{1,0:T(8,128)(2,1)S(1)} %constant_dynamic-update-slice_fusion.refs_2_), channel_id=1, source_target_pairs={{0,2},{1,3},{2,0},{3,1},{4,6},{5,7},{6,4},{7,5},{8,10},{9,11},{10,... | collective-permute-start | bytes 786440 | tf_op jit(solution)/shard_map/ppermute | solution.py:150
  8.2 0.0 collective-permute-start
  8.2 3.9 %collective-permute-done.3.refs_10_ = bf16[64,2048]{1,0:T(8,128)(2,1)S(1)} collective-permute-done((bf16[64,2048]{1,0:T(8,128)(2,1)S(1)}, bf16[64,2048]{1,0:T(8,128)(2,1)S(1)}, u32[]{:S(2)}, u32[]{:S(2)}) %collective-permute-start.3) | collective-permute-done | bytes 262176 | tf_op jit(solution)/shard_map/ppermute | solution.py:150
  12.1 1.6 %collective-permute-start.4 = (bf16[64,2048]{1,0:T(8,128)(2,1)S(1)}, bf16[64,2048]{1,0:T(8,128)(2,1)S(1)}, u32[]{:S(2)}, u32[]{:S(2)}) collective-permute-start(bf16[64,2048]{1,0:T(8,128)(2,1)S(1)} %broadcast_select_fusion), channel_id=1, source_target_pairs={{0,4},{1,5},{2,6},{3,7},{4,0},{5,1},{6,2},{7,3},{8,12},{9,13},{10,... | collective-permute-start | bytes 786440 | tf_op jit(solution)/shard_map/ppermute | solution.py:150
  13.7 1.5 %collective-permute-start.9 = (bf16[64,2048]{1,0:T(8,128)(2,1)S(1)}, bf16[64,2048]{1,0:T(8,128)(2,1)S(1)}, u32[]{:S(2)}, u32[]{:S(2)}) collective-permute-start(bf16[64,2048]{1,0:T(8,128)(2,1)S(1)} %collective-permute-done.3.refs_10_), channel_id=1, source_target_pairs={{0,2},{1,3},{2,0},{3,1},{4,6},{5,7},{6,4},{7,5},{8,10},{9,11},{10,... | collective-permute-start | bytes 786440 | tf_op jit(solution)/shard_map/ppermute | solution.py:150
  15.2 4.4 %collective-permute-start.11 = (bf16[64,2048]{1,0:T(8,128)(2,1)S(1)}, bf16[64,2048]{1,0:T(8,128)(2,1)S(1)}, u32[]{:S(2)}, u32[]{:S(2)}) collective-permute-start(bf16[64,2048]{1,0:T(8,128)(2,1)S(1)} %collective-permute-done.3.refs_10_), channel_id=1, source_target_pairs={{0,8},{1,9},{2,10},{3,11},{4,12},{5,13},{6,14},{7,15},{8,16},{9,17... | collective-permute-start | bytes 786440 | tf_op jit(solution)/shard_map/ppermute | solution.py:150
  19.6 0.1 collective-permute-start.8
  19.7 0.0 collective-permute-done.refs_3_
  19.7 0.5 collective-permute-start.2
  20.2 0.0 collective-permute-done.4.refs_6_
  20.2 0.7 collective-permute-start.6
  20.9 4.4 %collective-permute-start.13 = (bf16[64,2048]{1,0:T(8,128)(2,1)S(1)}, bf16[64,2048]{1,0:T(8,128)(2,1)S(1)}, u32[]{:S(2)}, u32[]{:S(2)}) collective-permute-start(bf16[64,2048]{1,0:T(8,128)(2,1)S(1)} %collective-permute-done.9.refs_12_), channel_id=1, source_target_pairs={{0,8},{1,9},{2,10},{3,11},{4,12},{5,13},{6,14},{7,15},{8,16},{9,17... | collective-permute-start | bytes 786440 | tf_op jit(solution)/shard_map/ppermute | solution.py:150
  25.3 0.0 collective-permute-done.11.refs_14_
  25.3 0.1 collective-permute-start.5
  25.4 0.0 collective-permute-done.8.refs_11_
  25.4 0.5 collective-permute-start.10
  25.9 0.1 collective-permute-start.12
  26.0 2.5 %collective-permute-done.6.refs_8_ = bf16[64,2048]{1,0:T(8,128)(2,1)S(1)} collective-permute-done((bf16[64,2048]{1,0:T(8,128)(2,1)S(1)}, bf16[64,2048]{1,0:T(8,128)(2,1)S(1)}, u32[]{:S(2)}, u32[]{:S(2)}) %collective-permute-start.6) | collective-permute-done | bytes 262176 | tf_op jit(solution)/shard_map/ppermute | solution.py:150
  28.5 0.0 collective-permute-start.7
  28.5 1.2 %collective-permute-done.13.refs_16_ = bf16[64,2048]{1,0:T(8,128)(2,1)S(1)} collective-permute-done((bf16[64,2048]{1,0:T(8,128)(2,1)S(1)}, bf16[64,2048]{1,0:T(8,128)(2,1)S(1)}, u32[]{:S(2)}, u32[]{:S(2)}) %collective-permute-start.13) | collective-permute-done | bytes 262176 | tf_op jit(solution)/shard_map/ppermute | solution.py:150
  29.7 0.0 collective-permute-done.5.refs_7_
  29.7 0.0 collective-permute-done.12.refs_15_
  29.8 0.3 collective-permute-done.7.refs_9_
  30.1 1.2 %collective-permute-done.14.refs_17_ = bf16[64,2048]{1,0:T(8,128)(2,1)S(1)} collective-permute-done((bf16[64,2048]{1,0:T(8,128)(2,1)S(1)}, bf16[64,2048]{1,0:T(8,128)(2,1)S(1)}, u32[]{:S(2)}, u32[]{:S(2)}) %collective-permute-start.14) | collective-permute-done | bytes 262176 | tf_op jit(solution)/shard_map/ppermute | solution.py:150
  31.3 0.7 copy-done.9
  32.0 24.7 %attention.1 = (bf16[64,8192]{1,0:T(8,128)(2,1)}, bf16[64,8192]{1,0:T(8,128)(2,1)}, bf16[64,2048]{1,0:T(8,128)(2,1)S(1)}, bf16[64,2048]{1,0:T(8,128)(2,1)S(1)}, ...) custom-call(bf16[64,8192]{1,0:T(8,128)(2,1)} %refs_0_.1, ...), custom_call_target="tpu_custom_call" | custom-call | flops 6442450944 | bytes 4194304 | tf_op jit(solution)/shard_map/attention/pallas_call | solution.py:126
  56.7 0.1 collective-permute-start.19
  56.8 0.4 collective-permute-start.15
  57.2 0.1 collective-permute-start.16
  57.3 0.4 collective-permute-start.18
  57.7 0.1 collective-permute-start.22
  57.8 0.4 collective-permute-done.19
  58.2 0.1 collective-permute-start.23
  58.4 0.1 add_convert_fusion.9
  58.4 1.7 %collective-permute-done.23 = bf16[64,2048]{1,0:T(8,128)(2,1)S(1)} collective-permute-done((bf16[64,2048]{1,0:T(8,128)(2,1)S(1)}, bf16[64,2048]{1,0:T(8,128)(2,1)S(1)}, u32[]{:S(2)}, u32[]{:S(2)}) %collective-permute-start.23) | collective-permute-done | bytes 262176 | tf_op jit(solution)/shard_map/ppermute | solution.py:150
  60.1 0.1 collective-permute-start.26
  60.2 0.1 add_convert_fusion.6
  60.3 1.3 %collective-permute-done.26 = bf16[64,2048]{1,0:T(8,128)(2,1)S(1)} collective-permute-done((bf16[64,2048]{1,0:T(8,128)(2,1)S(1)}, bf16[64,2048]{1,0:T(8,128)(2,1)S(1)}, u32[]{:S(2)}, u32[]{:S(2)}) %collective-permute-start.26) | collective-permute-done | bytes 262176 | tf_op jit(solution)/shard_map/ppermute | solution.py:150
  61.6 1.5 %collective-permute-start.20 = (bf16[64,2048]{1,0:T(8,128)(2,1)S(1)}, bf16[64,2048]{1,0:T(8,128)(2,1)S(1)}, u32[]{:S(2)}, u32[]{:S(2)}) collective-permute-start(bf16[64,2048]{1,0:T(8,128)(2,1)S(1)} %add_convert_fusion.9), channel_id=1, source_target_pairs={{0,2},{1,3},{2,0},{3,1},{4,6},{5,7},{6,4},{7,5},{8,10},{9,11},{10,... | collective-permute-start | bytes 786440 | tf_op jit(solution)/shard_map/ppermute | solution.py:150
  63.1 0.1 add_convert_fusion.3
  63.2 0.0 collective-permute-done.18
  63.2 0.1 collective-permute-start.25
  63.3 6.7 %collective-permute-done.20 = bf16[64,2048]{1,0:T(8,128)(2,1)S(1)} collective-permute-done((bf16[64,2048]{1,0:T(8,128)(2,1)S(1)}, bf16[64,2048]{1,0:T(8,128)(2,1)S(1)}, u32[]{:S(2)}, u32[]{:S(2)}) %collective-permute-start.20) | collective-permute-done | bytes 262176 | tf_op jit(solution)/shard_map/ppermute | solution.py:150
  70.0 1.3 %collective-permute-start.27 = (bf16[64,2048]{1,0:T(8,128)(2,1)S(1)}, bf16[64,2048]{1,0:T(8,128)(2,1)S(1)}, u32[]{:S(2)}, u32[]{:S(2)}) collective-permute-start(bf16[64,2048]{1,0:T(8,128)(2,1)S(1)} %add_convert_fusion.3), channel_id=1, source_target_pairs={{8,0},{9,1},{10,2},{11,3},{12,4},{13,5},{14,6},{15,7},{16,8},{17,9... | collective-permute-start | bytes 786440 | tf_op jit(solution)/shard_map/ppermute | solution.py:150
  71.3 0.1 add_convert_fusion.8
  71.4 1.3 %collective-permute-start.24 = (bf16[64,2048]{1,0:T(8,128)(2,1)S(1)}, bf16[64,2048]{1,0:T(8,128)(2,1)S(1)}, u32[]{:S(2)}, u32[]{:S(2)}) collective-permute-start(bf16[64,2048]{1,0:T(8,128)(2,1)S(1)} %add_convert_fusion.6), channel_id=1, source_target_pairs={{8,0},{9,1},{10,2},{11,3},{12,4},{13,5},{14,6},{15,7},{16,8},{17,9... | collective-permute-start | bytes 786440 | tf_op jit(solution)/shard_map/ppermute | solution.py:150
  72.7 8.9 %collective-permute-done.27 = bf16[64,2048]{1,0:T(8,128)(2,1)S(1)} collective-permute-done((bf16[64,2048]{1,0:T(8,128)(2,1)S(1)}, bf16[64,2048]{1,0:T(8,128)(2,1)S(1)}, u32[]{:S(2)}, u32[]{:S(2)}) %collective-permute-start.27) | collective-permute-done | bytes 262176 | tf_op jit(solution)/shard_map/ppermute | solution.py:150
  81.5 0.9 collective-permute-start.21
  82.5 0.1 add_convert_fusion.2
  82.6 1.2 %collective-permute-start.28 = (bf16[64,2048]{1,0:T(8,128)(2,1)S(1)}, bf16[64,2048]{1,0:T(8,128)(2,1)S(1)}, u32[]{:S(2)}, u32[]{:S(2)}) collective-permute-start(bf16[64,2048]{1,0:T(8,128)(2,1)S(1)} %add_convert_fusion.2), channel_id=1, source_target_pairs={{0,2},{1,3},{2,0},{3,1},{4,6},{5,7},{6,4},{7,5},{8,10},{9,11},{10,... | collective-permute-start | bytes 786440 | tf_op jit(solution)/shard_map/ppermute | solution.py:150
  83.8 0.1 add_convert_fusion.11
  83.9 1.0 collective-permute-start.17
  84.8 0.9 collective-permute-done.24
  85.7 2.2 %collective-permute-done.21 = bf16[64,2048]{1,0:T(8,128)(2,1)S(1)} collective-permute-done((bf16[64,2048]{1,0:T(8,128)(2,1)S(1)}, bf16[64,2048]{1,0:T(8,128)(2,1)S(1)}, u32[]{:S(2)}, u32[]{:S(2)}) %collective-permute-start.21) | collective-permute-done | bytes 262176 | tf_op jit(solution)/shard_map/ppermute | solution.py:150
  87.9 2.7 %collective-permute-done.28 = bf16[64,2048]{1,0:T(8,128)(2,1)S(1)} collective-permute-done((bf16[64,2048]{1,0:T(8,128)(2,1)S(1)}, bf16[64,2048]{1,0:T(8,128)(2,1)S(1)}, u32[]{:S(2)}, u32[]{:S(2)}) %collective-permute-start.28) | collective-permute-done | bytes 262176 | tf_op jit(solution)/shard_map/ppermute | solution.py:150
  90.7 0.2 add_convert_fusion.1
  90.9 1.3 %collective-permute-start.29 = (bf16[64,2048]{1,0:T(8,128)(2,1)S(1)}, bf16[64,2048]{1,0:T(8,128)(2,1)S(1)}, u32[]{:S(2)}, u32[]{:S(2)}) collective-permute-start(bf16[64,2048]{1,0:T(8,128)(2,1)S(1)} %add_convert_fusion.1), channel_id=1, source_target_pairs={{8,0},{9,1},{10,2},{11,3},{12,4},{13,5},{14,6},{15,7},{16,8},{17,9... | collective-permute-start | bytes 786440 | tf_op jit(solution)/shard_map/ppermute | solution.py:150
  92.2 1.3 %collective-permute-done.17 = bf16[64,2048]{1,0:T(8,128)(2,1)S(1)} collective-permute-done((bf16[64,2048]{1,0:T(8,128)(2,1)S(1)}, bf16[64,2048]{1,0:T(8,128)(2,1)S(1)}, u32[]{:S(2)}, u32[]{:S(2)}) %collective-permute-start.17) | collective-permute-done | bytes 262176 | tf_op jit(solution)/shard_map/ppermute | solution.py:150
  93.5 5.6 %collective-permute-done.29 = bf16[64,2048]{1,0:T(8,128)(2,1)S(1)} collective-permute-done((bf16[64,2048]{1,0:T(8,128)(2,1)S(1)}, bf16[64,2048]{1,0:T(8,128)(2,1)S(1)}, u32[]{:S(2)}, u32[]{:S(2)}) %collective-permute-start.29) | collective-permute-done | bytes 262176 | tf_op jit(solution)/shard_map/ppermute | solution.py:150
  99.1 0.2 add_convert_fusion
  99.3 0.7 fusion
  (29 shorter events, 0.1 us)
Async XLA Ops:
  0.6 1.0 copy-start.1
  1.6 10.5 %collective-permute-start.3 = (bf16[64,2048]{1,0:T(8,128)(2,1)S(1)}, bf16[64,2048]{1,0:T(8,128)(2,1)S(1)}, u32[]{:S(2)}, u32[]{:S(2)}) collective-permute-start(bf16[64,2048]{1,0:T(8,128)(2,1)S(1)} %constant_dynamic-update-slice_fusion.refs_2_), channel_id=1, source_target_pairs={{0,8},{1,9},{2,10},{3,11},{4,12},{5,13},{6,14},{7,15},{8,16},{9,17... | collective-permute-start | bytes 786440 | tf_op jit(solution)/shard_map/ppermute | solution.py:150
  6.6 13.0 %collective-permute-start.1 = (bf16[64,2048]{1,0:T(8,128)(2,1)S(1)}, bf16[64,2048]{1,0:T(8,128)(2,1)S(1)}, u32[]{:S(2)}, u32[]{:S(2)}) collective-permute-start(bf16[64,2048]{1,0:T(8,128)(2,1)S(1)} %constant_dynamic-update-slice_fusion.refs_2_), channel_id=1, source_target_pairs={{0,2},{1,3},{2,0},{3,1},{4,6},{5,7},{6,4},{7,5},{8,10},{9,11},{10,... | collective-permute-start | bytes 786440 | tf_op jit(solution)/shard_map/ppermute | solution.py:150
  8.2 11.6 %collective-permute-start = (bf16[64,2048]{1,0:T(8,128)(2,1)S(1)}, bf16[64,2048]{1,0:T(8,128)(2,1)S(1)}, u32[]{:S(2)}, u32[]{:S(2)}) collective-permute-start(bf16[64,2048]{1,0:T(8,128)(2,1)S(1)} %constant_dynamic-update-slice_fusion.refs_2_), channel_id=1, source_target_pairs={{0,1},{1,0},{2,3},{3,2},{4,5},{5,4},{6,7},{7,6},{8,9},{9,8},{10,11... | collective-permute-start | bytes 786440 | tf_op jit(solution)/shard_map/ppermute | solution.py:150
  12.1 7.5 %copy-start = (bf16[64,2048]{1,0:T(8,128)(2,1)}, bf16[64,2048]{1,0:T(8,128)(2,1)S(1)}, u32[]{:S(2)}) copy-start(bf16[64,2048]{1,0:T(8,128)(2,1)S(1)} %collective-permute-done.3.refs_10_) | copy-start | bytes 786436
  12.1 8.1 %collective-permute-start.4 = (bf16[64,2048]{1,0:T(8,128)(2,1)S(1)}, bf16[64,2048]{1,0:T(8,128)(2,1)S(1)}, u32[]{:S(2)}, u32[]{:S(2)}) collective-permute-start(bf16[64,2048]{1,0:T(8,128)(2,1)S(1)} %broadcast_select_fusion), channel_id=1, source_target_pairs={{0,4},{1,5},{2,6},{3,7},{4,0},{5,1},{6,2},{7,3},{8,12},{9,13},{10,... | collective-permute-start | bytes 786440 | tf_op jit(solution)/shard_map/ppermute | solution.py:150
  13.7 7.2 %collective-permute-start.9 = (bf16[64,2048]{1,0:T(8,128)(2,1)S(1)}, bf16[64,2048]{1,0:T(8,128)(2,1)S(1)}, u32[]{:S(2)}, u32[]{:S(2)}) collective-permute-start(bf16[64,2048]{1,0:T(8,128)(2,1)S(1)} %collective-permute-done.3.refs_10_), channel_id=1, source_target_pairs={{0,2},{1,3},{2,0},{3,1},{4,6},{5,7},{6,4},{7,5},{8,10},{9,11},{10,... | collective-permute-start | bytes 786440 | tf_op jit(solution)/shard_map/ppermute | solution.py:150
  15.2 10.1 %collective-permute-start.11 = (bf16[64,2048]{1,0:T(8,128)(2,1)S(1)}, bf16[64,2048]{1,0:T(8,128)(2,1)S(1)}, u32[]{:S(2)}, u32[]{:S(2)}) collective-permute-start(bf16[64,2048]{1,0:T(8,128)(2,1)S(1)} %collective-permute-done.3.refs_10_), channel_id=1, source_target_pairs={{0,8},{1,9},{2,10},{3,11},{4,12},{5,13},{6,14},{7,15},{8,16},{9,17... | collective-permute-start | bytes 786440 | tf_op jit(solution)/shard_map/ppermute | solution.py:150
  19.6 5.8 %collective-permute-start.8 = (bf16[64,2048]{1,0:T(8,128)(2,1)S(1)}, bf16[64,2048]{1,0:T(8,128)(2,1)S(1)}, u32[]{:S(2)}, u32[]{:S(2)}) collective-permute-start(bf16[64,2048]{1,0:T(8,128)(2,1)S(1)} %collective-permute-done.3.refs_10_), channel_id=1, source_target_pairs={{0,1},{1,0},{2,3},{3,2},{4,5},{5,4},{6,7},{7,6},{8,9},{9,8},{10,11... | collective-permute-start | bytes 786440 | tf_op jit(solution)/shard_map/ppermute | solution.py:150
  19.7 6.2 %collective-permute-start.2 = (bf16[64,2048]{1,0:T(8,128)(2,1)S(1)}, bf16[64,2048]{1,0:T(8,128)(2,1)S(1)}, u32[]{:S(2)}, u32[]{:S(2)}) collective-permute-start(bf16[64,2048]{1,0:T(8,128)(2,1)S(1)} %collective-permute-done.1.refs_4_), channel_id=1, source_target_pairs={{0,1},{1,0},{2,3},{3,2},{4,5},{5,4},{6,7},{7,6},{8,9},{9,8},{10,11... | collective-permute-start | bytes 786440 | tf_op jit(solution)/shard_map/ppermute | solution.py:150
  20.2 8.3 %collective-permute-start.6 = (bf16[64,2048]{1,0:T(8,128)(2,1)S(1)}, bf16[64,2048]{1,0:T(8,128)(2,1)S(1)}, u32[]{:S(2)}, u32[]{:S(2)}) collective-permute-start(bf16[64,2048]{1,0:T(8,128)(2,1)S(1)} %collective-permute-done.4.refs_6_), channel_id=1, source_target_pairs={{0,2},{1,3},{2,0},{3,1},{4,6},{5,7},{6,4},{7,5},{8,10},{9,11},{10,... | collective-permute-start | bytes 786440 | tf_op jit(solution)/shard_map/ppermute | solution.py:150
  20.9 10.3 %copy-start.2 = (bf16[64,2048]{1,0:T(8,128)(2,1)}, bf16[64,2048]{1,0:T(8,128)(2,1)S(1)}, u32[]{:S(2)}) copy-start(bf16[64,2048]{1,0:T(8,128)(2,1)S(1)} %collective-permute-done.9.refs_12_) | copy-start | bytes 786436
  20.9 8.8 %collective-permute-start.13 = (bf16[64,2048]{1,0:T(8,128)(2,1)S(1)}, bf16[64,2048]{1,0:T(8,128)(2,1)S(1)}, u32[]{:S(2)}, u32[]{:S(2)}) collective-permute-start(bf16[64,2048]{1,0:T(8,128)(2,1)S(1)} %collective-permute-done.9.refs_12_), channel_id=1, source_target_pairs={{0,8},{1,9},{2,10},{3,11},{4,12},{5,13},{6,14},{7,15},{8,16},{9,17... | collective-permute-start | bytes 786440 | tf_op jit(solution)/shard_map/ppermute | solution.py:150
  25.3 5.9 %copy-start.3 = (bf16[64,2048]{1,0:T(8,128)(2,1)}, bf16[64,2048]{1,0:T(8,128)(2,1)S(1)}, u32[]{:S(2)}) copy-start(bf16[64,2048]{1,0:T(8,128)(2,1)S(1)} %collective-permute-done.11.refs_14_) | copy-start | bytes 786436
  25.3 4.4 %collective-permute-start.5 = (bf16[64,2048]{1,0:T(8,128)(2,1)S(1)}, bf16[64,2048]{1,0:T(8,128)(2,1)S(1)}, u32[]{:S(2)}, u32[]{:S(2)}) collective-permute-start(bf16[64,2048]{1,0:T(8,128)(2,1)S(1)} %collective-permute-done.4.refs_6_), channel_id=1, source_target_pairs={{0,1},{1,0},{2,3},{3,2},{4,5},{5,4},{6,7},{7,6},{8,9},{9,8},{10,11... | collective-permute-start | bytes 786440 | tf_op jit(solution)/shard_map/ppermute | solution.py:150
  25.4 5.8 %copy-start.4 = (bf16[64,2048]{1,0:T(8,128)(2,1)}, bf16[64,2048]{1,0:T(8,128)(2,1)S(1)}, u32[]{:S(2)}) copy-start(bf16[64,2048]{1,0:T(8,128)(2,1)S(1)} %collective-permute-done.8.refs_11_) | copy-start | bytes 786436
  25.4 4.3 %collective-permute-start.10 = (bf16[64,2048]{1,0:T(8,128)(2,1)S(1)}, bf16[64,2048]{1,0:T(8,128)(2,1)S(1)}, u32[]{:S(2)}, u32[]{:S(2)}) collective-permute-start(bf16[64,2048]{1,0:T(8,128)(2,1)S(1)} %collective-permute-done.9.refs_12_), channel_id=1, source_target_pairs={{0,1},{1,0},{2,3},{3,2},{4,5},{5,4},{6,7},{7,6},{8,9},{9,8},{10,11... | collective-permute-start | bytes 786440 | tf_op jit(solution)/shard_map/ppermute | solution.py:150
  25.9 3.8 %collective-permute-start.12 = (bf16[64,2048]{1,0:T(8,128)(2,1)S(1)}, bf16[64,2048]{1,0:T(8,128)(2,1)S(1)}, u32[]{:S(2)}, u32[]{:S(2)}) collective-permute-start(bf16[64,2048]{1,0:T(8,128)(2,1)S(1)} %collective-permute-done.11.refs_14_), channel_id=1, source_target_pairs={{0,1},{1,0},{2,3},{3,2},{4,5},{5,4},{6,7},{7,6},{8,9},{9,8},{10,11... | collective-permute-start | bytes 786440 | tf_op jit(solution)/shard_map/ppermute | solution.py:150
  28.5 1.5 %collective-permute-start.7 = (bf16[64,2048]{1,0:T(8,128)(2,1)S(1)}, bf16[64,2048]{1,0:T(8,128)(2,1)S(1)}, u32[]{:S(2)}, u32[]{:S(2)}) collective-permute-start(bf16[64,2048]{1,0:T(8,128)(2,1)S(1)} %collective-permute-done.6.refs_8_), channel_id=1, source_target_pairs={{0,1},{1,0},{2,3},{3,2},{4,5},{5,4},{6,7},{7,6},{8,9},{9,8},{10,11... | collective-permute-start | bytes 786440 | tf_op jit(solution)/shard_map/ppermute | solution.py:150
  29.7 1.6 %copy-start.5 = (bf16[64,2048]{1,0:T(8,128)(2,1)}, bf16[64,2048]{1,0:T(8,128)(2,1)S(1)}, u32[]{:S(2)}) copy-start(bf16[64,2048]{1,0:T(8,128)(2,1)S(1)} %collective-permute-done.13.refs_16_) | copy-start | bytes 786436
  29.7 1.5 %collective-permute-start.14 = (bf16[64,2048]{1,0:T(8,128)(2,1)S(1)}, bf16[64,2048]{1,0:T(8,128)(2,1)S(1)}, u32[]{:S(2)}, u32[]{:S(2)}) collective-permute-start(bf16[64,2048]{1,0:T(8,128)(2,1)S(1)} %collective-permute-done.13.refs_16_), channel_id=1, source_target_pairs={{0,1},{1,0},{2,3},{3,2},{4,5},{5,4},{6,7},{7,6},{8,9},{9,8},{10,11... | collective-permute-start | bytes 786440 | tf_op jit(solution)/shard_map/ppermute | solution.py:150
  29.7 1.5 %copy-start.7 = (bf16[64,2048]{1,0:T(8,128)(2,1)}, bf16[64,2048]{1,0:T(8,128)(2,1)S(1)}, u32[]{:S(2)}) copy-start(bf16[64,2048]{1,0:T(8,128)(2,1)S(1)} %collective-permute-done.12.refs_15_) | copy-start | bytes 786436
  29.7 1.5 %copy-start.6 = (bf16[64,2048]{1,0:T(8,128)(2,1)}, bf16[64,2048]{1,0:T(8,128)(2,1)S(1)}, u32[]{:S(2)}) copy-start(bf16[64,2048]{1,0:T(8,128)(2,1)S(1)} %collective-permute-done.10.refs_13_) | copy-start | bytes 786436
  30.1 1.2 %copy-start.8 = (bf16[64,2048]{1,0:T(8,128)(2,1)}, bf16[64,2048]{1,0:T(8,128)(2,1)S(1)}, u32[]{:S(2)}) copy-start(bf16[64,2048]{1,0:T(8,128)(2,1)S(1)} %collective-permute-done.7.refs_9_) | copy-start | bytes 786436
  31.3 0.7 copy-start.9
  56.7 1.5 %collective-permute-start.19 = (bf16[64,2048]{1,0:T(8,128)(2,1)S(1)}, bf16[64,2048]{1,0:T(8,128)(2,1)S(1)}, u32[]{:S(2)}, u32[]{:S(2)}) collective-permute-start(bf16[64,2048]{1,0:T(8,128)(2,1)S(1)} %get-tuple-element.31), channel_id=1, source_target_pairs={{0,1},{1,0},{2,3},{3,2},{4,5},{5,4},{6,7},{7,6},{8,9},{9,8},{10,11... | collective-permute-start | bytes 786440 | tf_op jit(solution)/shard_map/ppermute | solution.py:150
  56.8 35.3 %collective-permute-start.15 = (bf16[64,2048]{1,0:T(8,128)(2,1)S(1)}, bf16[64,2048]{1,0:T(8,128)(2,1)S(1)}, u32[]{:S(2)}, u32[]{:S(2)}) collective-permute-start(bf16[64,2048]{1,0:T(8,128)(2,1)S(1)} %get-tuple-element.25), channel_id=1, source_target_pairs={{0,1},{1,0},{2,3},{3,2},{4,5},{5,4},{6,7},{7,6},{8,9},{9,8},{10,11... | collective-permute-start | bytes 786440 | tf_op jit(solution)/shard_map/ppermute | solution.py:150
  57.2 25.4 %collective-permute-start.16 = (bf16[64,2048]{1,0:T(8,128)(2,1)S(1)}, bf16[64,2048]{1,0:T(8,128)(2,1)S(1)}, u32[]{:S(2)}, u32[]{:S(2)}) collective-permute-start(bf16[64,2048]{1,0:T(8,128)(2,1)S(1)} %get-tuple-element.27), channel_id=1, source_target_pairs={{0,1},{1,0},{2,3},{3,2},{4,5},{5,4},{6,7},{7,6},{8,9},{9,8},{10,11... | collective-permute-start | bytes 786440 | tf_op jit(solution)/shard_map/ppermute | solution.py:150
  57.3 5.9 %collective-permute-start.18 = (bf16[64,2048]{1,0:T(8,128)(2,1)S(1)}, bf16[64,2048]{1,0:T(8,128)(2,1)S(1)}, u32[]{:S(2)}, u32[]{:S(2)}) collective-permute-start(bf16[64,2048]{1,0:T(8,128)(2,1)S(1)} %get-tuple-element.29), channel_id=1, source_target_pairs={{0,1},{1,0},{2,3},{3,2},{4,5},{5,4},{6,7},{7,6},{8,9},{9,8},{10,11... | collective-permute-start | bytes 786440 | tf_op jit(solution)/shard_map/ppermute | solution.py:150
  57.7 26.1 %collective-permute-start.22 = (bf16[64,2048]{1,0:T(8,128)(2,1)S(1)}, bf16[64,2048]{1,0:T(8,128)(2,1)S(1)}, u32[]{:S(2)}, u32[]{:S(2)}) collective-permute-start(bf16[64,2048]{1,0:T(8,128)(2,1)S(1)} %get-tuple-element.33), channel_id=1, source_target_pairs={{0,1},{1,0},{2,3},{3,2},{4,5},{5,4},{6,7},{7,6},{8,9},{9,8},{10,11... | collective-permute-start | bytes 786440 | tf_op jit(solution)/shard_map/ppermute | solution.py:150
  58.2 1.9 %collective-permute-start.23 = (bf16[64,2048]{1,0:T(8,128)(2,1)S(1)}, bf16[64,2048]{1,0:T(8,128)(2,1)S(1)}, u32[]{:S(2)}, u32[]{:S(2)}) collective-permute-start(bf16[64,2048]{1,0:T(8,128)(2,1)S(1)} %get-tuple-element.35), channel_id=1, source_target_pairs={{0,1},{1,0},{2,3},{3,2},{4,5},{5,4},{6,7},{7,6},{8,9},{9,8},{10,11... | collective-permute-start | bytes 786440 | tf_op jit(solution)/shard_map/ppermute | solution.py:150
  60.1 1.5 %collective-permute-start.26 = (bf16[64,2048]{1,0:T(8,128)(2,1)S(1)}, bf16[64,2048]{1,0:T(8,128)(2,1)S(1)}, u32[]{:S(2)}, u32[]{:S(2)}) collective-permute-start(bf16[64,2048]{1,0:T(8,128)(2,1)S(1)} %get-tuple-element.39), channel_id=1, source_target_pairs={{0,1},{1,0},{2,3},{3,2},{4,5},{5,4},{6,7},{7,6},{8,9},{9,8},{10,11... | collective-permute-start | bytes 786440 | tf_op jit(solution)/shard_map/ppermute | solution.py:150
  61.6 8.3 %collective-permute-start.20 = (bf16[64,2048]{1,0:T(8,128)(2,1)S(1)}, bf16[64,2048]{1,0:T(8,128)(2,1)S(1)}, u32[]{:S(2)}, u32[]{:S(2)}) collective-permute-start(bf16[64,2048]{1,0:T(8,128)(2,1)S(1)} %add_convert_fusion.9), channel_id=1, source_target_pairs={{0,2},{1,3},{2,0},{3,1},{4,6},{5,7},{6,4},{7,5},{8,10},{9,11},{10,... | collective-permute-start | bytes 786440 | tf_op jit(solution)/shard_map/ppermute | solution.py:150
  63.2 8.2 %collective-permute-start.25 = (bf16[64,2048]{1,0:T(8,128)(2,1)S(1)}, bf16[64,2048]{1,0:T(8,128)(2,1)S(1)}, u32[]{:S(2)}, u32[]{:S(2)}) collective-permute-start(bf16[64,2048]{1,0:T(8,128)(2,1)S(1)} %get-tuple-element.37), channel_id=1, source_target_pairs={{0,1},{1,0},{2,3},{3,2},{4,5},{5,4},{6,7},{7,6},{8,9},{9,8},{10,11... | collective-permute-start | bytes 786440 | tf_op jit(solution)/shard_map/ppermute | solution.py:150
  70.0 11.6 %collective-permute-start.27 = (bf16[64,2048]{1,0:T(8,128)(2,1)S(1)}, bf16[64,2048]{1,0:T(8,128)(2,1)S(1)}, u32[]{:S(2)}, u32[]{:S(2)}) collective-permute-start(bf16[64,2048]{1,0:T(8,128)(2,1)S(1)} %add_convert_fusion.3), channel_id=1, source_target_pairs={{8,0},{9,1},{10,2},{11,3},{12,4},{13,5},{14,6},{15,7},{16,8},{17,9... | collective-permute-start | bytes 786440 | tf_op jit(solution)/shard_map/ppermute | solution.py:150
  71.4 14.4 %collective-permute-start.24 = (bf16[64,2048]{1,0:T(8,128)(2,1)S(1)}, bf16[64,2048]{1,0:T(8,128)(2,1)S(1)}, u32[]{:S(2)}, u32[]{:S(2)}) collective-permute-start(bf16[64,2048]{1,0:T(8,128)(2,1)S(1)} %add_convert_fusion.6), channel_id=1, source_target_pairs={{8,0},{9,1},{10,2},{11,3},{12,4},{13,5},{14,6},{15,7},{16,8},{17,9... | collective-permute-start | bytes 786440 | tf_op jit(solution)/shard_map/ppermute | solution.py:150
  81.5 6.4 %collective-permute-start.21 = (bf16[64,2048]{1,0:T(8,128)(2,1)S(1)}, bf16[64,2048]{1,0:T(8,128)(2,1)S(1)}, u32[]{:S(2)}, u32[]{:S(2)}) collective-permute-start(bf16[64,2048]{1,0:T(8,128)(2,1)S(1)} %add_convert_fusion.8), channel_id=1, source_target_pairs={{0,4},{1,5},{2,6},{3,7},{4,0},{5,1},{6,2},{7,3},{8,12},{9,13},{10,... | collective-permute-start | bytes 786440 | tf_op jit(solution)/shard_map/ppermute | solution.py:150
  82.6 8.1 %collective-permute-start.28 = (bf16[64,2048]{1,0:T(8,128)(2,1)S(1)}, bf16[64,2048]{1,0:T(8,128)(2,1)S(1)}, u32[]{:S(2)}, u32[]{:S(2)}) collective-permute-start(bf16[64,2048]{1,0:T(8,128)(2,1)S(1)} %add_convert_fusion.2), channel_id=1, source_target_pairs={{0,2},{1,3},{2,0},{3,1},{4,6},{5,7},{6,4},{7,5},{8,10},{9,11},{10,... | collective-permute-start | bytes 786440 | tf_op jit(solution)/shard_map/ppermute | solution.py:150
  83.9 9.6 %collective-permute-start.17 = (bf16[64,2048]{1,0:T(8,128)(2,1)S(1)}, bf16[64,2048]{1,0:T(8,128)(2,1)S(1)}, u32[]{:S(2)}, u32[]{:S(2)}) collective-permute-start(bf16[64,2048]{1,0:T(8,128)(2,1)S(1)} %add_convert_fusion.11), channel_id=1, source_target_pairs={{0,2},{1,3},{2,0},{3,1},{4,6},{5,7},{6,4},{7,5},{8,10},{9,11},{10,... | collective-permute-start | bytes 786440 | tf_op jit(solution)/shard_map/ppermute | solution.py:150
  90.9 8.3 %collective-permute-start.29 = (bf16[64,2048]{1,0:T(8,128)(2,1)S(1)}, bf16[64,2048]{1,0:T(8,128)(2,1)S(1)}, u32[]{:S(2)}, u32[]{:S(2)}) collective-permute-start(bf16[64,2048]{1,0:T(8,128)(2,1)S(1)} %add_convert_fusion.1), channel_id=1, source_target_pairs={{8,0},{9,1},{10,2},{11,3},{12,4},{13,5},{14,6},{15,7},{16,8},{17,9... | collective-permute-start | bytes 786440 | tf_op jit(solution)/shard_map/ppermute | solution.py:150

commit v2 on v1

v2 whole, which is shorter than its diff:
```python
import jax
import jax.numpy as jnp
from jax import lax
from jax.experimental import pallas as pl
from jax.experimental.pallas import tpu as pltpu
from jax.sharding import PartitionSpec as P

HD = 128
LOG2E = 1.4426950408889634
LOW = -1e30

NT = (((1,), (1,)), ((), ()))
NN = (((1,), (0,)), ((), ()))
TN = (((0,), (0,)), ((), ()))


def mm(a, b, dims):
    return lax.dot_general(a, b, dims, preferred_element_type=jnp.float32)


def attention_kernel(levels, peers, group, per, homes, *refs):
    count = levels * peers
    q_ref, g_ref = refs[:2]
    kv_refs = refs[2 : 2 + count]
    o_ref, dq_ref = refs[2 + count : 4 + count]
    dkv_refs = refs[4 + count :]
    homes = {at: (dkv_refs[place], pl.ds(index * q_ref.shape[0], q_ref.shape[0])) for at, (place, index) in homes.items()}
    rows = q_ref.shape[0]
    width = kv_refs[0].shape[1] // 2
    wide = group * rows
    scale = HD ** (-0.5)
    factor = scale * LOG2E
    ctx = lax.axis_index("ctx")
    kvh = lax.axis_index("kvh")
    key_pos = lax.broadcasted_iota(jnp.int32, (rows, wide), 0)
    query_pos = lax.broadcasted_iota(jnp.int32, (rows, wide), 1) % rows
    causal = key_pos <= query_pos

    def counts(level, j):
        if level == 0:
            return lax.bitwise_xor(kvh, j) < kvh
        return ctx >= (1 << (level - 1))

    class Head:
        def __init__(self, index):
            self.first = index * group * HD
            self.head = pl.program_id(0) * per + index
            self.at_k = pl.ds(pl.multiple_of(self.head * HD, HD), HD)
            self.at_v = pl.ds(pl.multiple_of(self.head * HD + width, HD), HD)

        def stack(self, ref):
            return jnp.concatenate(
                [ref[:, self.first + r * HD : self.first + (r + 1) * HD] for r in range(group)], axis=0
            )

        def unstack(self, ref, value):
            for r in range(group):
                ref[:, self.first + r * HD : self.first + (r + 1) * HD] = value[r * rows : (r + 1) * rows]

        def keys(self, level):
            return jnp.concatenate([ref[:, self.at_k] for ref in kv_refs[level * peers : (level + 1) * peers]], axis=0)

        def values(self, level):
            return jnp.concatenate([ref[:, self.at_v] for ref in kv_refs[level * peers : (level + 1) * peers]], axis=0)

        def start(self):
            self.queries = self.stack(q_ref)
            self.grads = self.stack(g_ref)
            self.queries_t, self.grads_t = self.queries.T, self.grads.T
            self.top, self.total, self.out_t, self.dq_t = None, None, None, None
            self.scores, self.weights, self.grad_prob = [], [], []

        def score(self, level):
            raw = mm(self.keys(level), self.queries_t, NN)
            for j in range(peers):
                piece = raw[j * rows : (j + 1) * rows]
                if level == 0 and j == 0:
                    piece = jnp.where(causal, piece, LOW)
                best = jnp.max(piece, axis=0, keepdims=True)
                if level or j:
                    best = jnp.where(counts(level, j), best, LOW)
                self.top = best if self.top is None else jnp.maximum(self.top, best)
                self.scores.append(piece)

        def weigh(self, level):
            top = self.top * factor
            pieces = []
            for j in range(peers):
                shift = jnp.where(counts(level, j), top, -LOW) if level or j else top
                weight = jnp.exp2(self.scores[level * peers + j] * factor - shift)
                part = jnp.sum(weight, axis=0, keepdims=True)
                self.total = part if self.total is None else self.total + part
                pieces.append(weight.astype(jnp.bfloat16))
            self.weights.append(jnp.concatenate(pieces, axis=0))
            part = mm(self.values(level), self.weights[level], TN)
            self.out_t = part if self.out_t is None else self.out_t + part

        def finish(self):
            self.inverse = 1.0 / self.total
            out_t = (self.out_t * self.inverse).astype(jnp.bfloat16)
            self.unstack(o_ref, out_t.T)
            self.delta = jnp.sum(
                self.grads_t.astype(jnp.float32) * out_t.astype(jnp.float32), axis=0, keepdims=True
            )
            spread = jnp.broadcast_to(self.inverse, (HD, wide)).T
            self.queries_low = (self.queries.astype(jnp.float32) * (spread * scale)).astype(jnp.bfloat16)
            self.grads_low = (self.grads.astype(jnp.float32) * spread).astype(jnp.bfloat16)

        def back(self, level):
            grad_prob = mm(self.values(level), self.grads_t, NN) - self.delta
            grad_scores = self.weights[level] * grad_prob.astype(jnp.bfloat16)
            part = mm(self.keys(level), grad_scores, TN)
            self.dq_t = part if self.dq_t is None else self.dq_t + part
            grad_k = mm(grad_scores, self.queries_low, NN).astype(jnp.bfloat16)
            grad_v = mm(self.weights[level], self.grads_low, NN).astype(jnp.bfloat16)
            for j in range(peers):
                ref, at = homes[level, j]
                ref[at, self.at_k] = grad_k[j * rows : (j + 1) * rows]
                ref[at, self.at_v] = grad_v[j * rows : (j + 1) * rows]

        def end(self):
            self.unstack(dq_ref, (self.dq_t * (self.inverse * scale)).T.astype(jnp.bfloat16))

    heads = [Head(index) for index in range(per)]
    first = heads[0]
    first.start()
    for level in range(levels):
        first.score(level)
    for index, head in enumerate(heads):
        after = heads[index + 1] if index + 1 < per else None
        if after:
            after.start()
        for level in range(levels):
            head.weigh(level)
            if after:
                after.score(level)
        head.finish()
        for level in range(levels):
            head.back(level)
        head.end()


def attention(query, grad, shards, levels, peers, parts):
    rows, q_width = query.shape
    kv_width = shards[0].shape[1]
    heads = kv_width // (2 * HD)
    group = q_width // (heads * HD)
    per = 4
    whole = pl.BlockSpec(memory_space=pltpu.VMEM)
    block = pl.BlockSpec((rows, per * group * HD), lambda step: (0, step))
    q_shape = jax.ShapeDtypeStruct(query.shape, jnp.bfloat16)
    kv_shapes = [jax.ShapeDtypeStruct((rows * len(part), kv_width), jnp.bfloat16) for part in parts]
    homes = {at: (place, index) for place, part in enumerate(parts) for index, at in enumerate(part)}
    count = levels * peers
    return pl.pallas_call(
        lambda *refs: attention_kernel(levels, peers, group, per, homes, *refs),
        grid=(heads // per,),
        out_shape=[q_shape] * 2 + kv_shapes,
        in_specs=[block] * 2 + [whole] * count,
        out_specs=[block] * 2 + [whole] * len(parts),
        compiler_params=pltpu.CompilerParams(vmem_limit_bytes=32 * 2**20),
        cost_estimate=pl.CostEstimate(
            flops=12 * rows * q_width * count * rows, bytes_accessed=8 * rows * q_width, transcendentals=0
        ),
        name="attention",
    )(query, grad, *shards)


def merge(body, inputs, shapes, name):
    def kernel(*refs):
        body(refs[: len(inputs)], refs[len(inputs) :])

    whole = pl.BlockSpec(memory_space=pltpu.VMEM)
    return pl.pallas_call(
        kernel,
        out_shape=[jax.ShapeDtypeStruct(shape, jnp.bfloat16) for shape in shapes],
        in_specs=[whole] * len(inputs),
        out_specs=[whole] * len(shapes),
        compiler_params=pltpu.CompilerParams(vmem_limit_bytes=12 * 2**20),
        name=name,
    )(*inputs)


AXES = ("ctx", "kvh")


def permute(array, target):
    blocks, peers = lax.axis_size("ctx"), lax.axis_size("kvh")
    pairs = []
    for c in range(blocks):
        for k in range(peers):
            to_c, to_k = target(c, k)
            pairs.append((c * peers + k, to_c % blocks * peers + to_k))
    return lax.ppermute(array, AXES, pairs)


def along(array, by):
    return permute(array, lambda c, k: (c + by, k))


def pair_swap(array):
    return permute(array, lambda c, k: (c ^ 1, k))


def across(array):
    return permute(array, lambda c, k: (c, k ^ 2))


def sibling(array):
    return permute(array, lambda c, k: (c, k ^ 1))


def wide(value):
    return value.astype(jnp.float32)


def low(value):
    return value.astype(jnp.bfloat16)


def gather(own, levels, odd):
    held = {(0, 0): own}
    held[2, 0] = along(own, 2)
    held[0, 2] = across(own)
    held[0, 1] = sibling(own)
    for level in range(3, levels):
        held[level, 0] = along(held[level - 1, 0], 1 << (level - 2))
    held[2, 2] = across(held[2, 0])
    held[1, 0] = pair_swap(jnp.where(odd, held[2, 0], own))
    held[0, 3] = sibling(held[0, 2])
    held[2, 1] = sibling(held[2, 0])
    for level in range(3, levels):
        held[level, 2] = across(held[level, 0])
    held[1, 2] = pair_swap(jnp.where(odd, held[2, 2], held[0, 2]))
    held[2, 3] = sibling(held[2, 2])
    held[1, 1] = sibling(held[1, 0])
    held[1, 3] = sibling(held[1, 2])
    for level in range(3, levels):
        held[level, 1] = sibling(held[level, 0])
        held[level, 3] = sibling(held[level, 2])
    return held


def scatter(parts, levels, rows, width):
    keep_a, keep_b, keep_c, send_a, send_b, send_c = parts
    tall = 2 * width
    shape = (rows, tall)
    far = levels - 1

    def at(ref, index):
        return wide(ref[index * rows : (index + 1) * rows])

    def is_odd():
        return lax.axis_index("ctx") % 2 == 1

    got_a = sibling(send_a)
    got_b = sibling(send_b)
    got_c = sibling(send_c)

    def first(ins, outs):
        keep, got = ins
        for index, out in enumerate(outs):
            out[...] = low(at(keep, index) + at(got, index))

    *far_2, near_2 = merge(first, [keep_a, got_a], [shape] * (far - 1), "first")
    got_far = [across(array) for array in far_2]
    got_near = pair_swap(near_2)

    def second(ins, outs):
        keep, got, swapped, *crossed = ins
        from_pair = wide(swapped[...])
        odd = is_odd()
        none = jnp.zeros_like(from_pair)
        outs[0][...] = low(at(keep, 0) + at(got, 0) + jnp.where(odd, from_pair, none))
        outs[1][...] = low(at(keep, 1) + at(got, 1) + jnp.where(odd, none, from_pair))
        outs[2][...] = low(at(keep, 2) + at(got, 2))
        for index, other in enumerate(crossed):
            outs[3 + index][...] = low(at(keep, 3 + index) + at(got, 3 + index) + wide(other[...]))

    two_2, zero_2, one_0, *far_0 = merge(
        second, [keep_b, got_b, got_near] + got_far, [shape] * (far + 1), "second"
    )
    chain = far_0[-1]
    for level in range(far, 3, -1):
        chain = low(wide(far_0[level - 4]) + wide(along(chain, -(1 << (level - 2)))))
    got_chain = along(chain, -2)
    got_two = across(two_2)
    got_one = pair_swap(one_0)

    def third(ins, outs):
        keep, got, chain, two, one = ins
        from_pair = wide(one[...])
        terms = jnp.where(is_odd(), from_pair, jnp.zeros_like(from_pair))
        outs[0][...] = low(at(keep, 0) + at(got, 0) + wide(chain[...]) + wide(two[...]) + terms)

    (two_0,) = merge(third, [keep_c, got_c, got_chain, got_two, got_one], [shape], "third")
    got_chain = along(two_0, -2)
    got_zero = across(zero_2)

    def fourth(ins, outs):
        keep, got, one, zero, chain = ins
        from_pair = wide(one[...])
        terms = jnp.where(is_odd(), jnp.zeros_like(from_pair), from_pair)
        total = at(keep, 1) + at(got, 1) + wide(chain[...]) + wide(zero[...]) + terms
        outs[0][...] = low(total[:, :width])
        outs[1][...] = low(total[:, width:])

    return merge(fourth, [keep_c, got_c, got_one, got_zero, got_chain], [(rows, width)] * 2, "fourth")


def shards(query_act, key_act, value_act, grad_out):
    blocks, peers = lax.axis_size("ctx"), lax.axis_size("kvh")
    levels = (blocks - 1).bit_length() + 1
    odd = lax.axis_index("ctx") % 2 == 1
    rows, width = key_act.shape

    def join(ins, outs):
        outs[0][:, :width] = ins[0][...]
        outs[0][:, width:] = ins[1][...]

    (own,) = merge(join, [key_act, value_act], [(rows, 2 * width)], "join")
    held = gather(own, levels, odd)
    ordered = [held[level, j] for level in range(levels) for j in range(peers)]
    later = list(range(3, levels))
    kept = [
        [(level, 2) for level in later] + [(1, 2)],
        [(2, 2), (0, 2), (1, 0)] + [(level, 0) for level in later],
        [(2, 0), (0, 0)],
    ]
    sent = [[(level, j + 1) for level, j in part] for part in kept]
    out, grad_query, *parts = attention(query_act, grad_out, ordered, levels, peers, kept + sent)
    grad_key, grad_value = scatter(parts, levels, rows, width)
    return out, grad_query, grad_key, grad_value


def solution(mesh):
    spec = P(AXES, None)
    return jax.shard_map(
        shards, mesh=mesh, in_specs=(spec,) * 4, out_specs=(spec,) * 4, check_vma=False
    )
```

time: 100 us -> 85.6 us (0.86)
  starting transfers between devices: 30.3 us -> 16.7 us
  waiting for transfers between devices: 40.9 us -> 44.6 us
  Pallas kernels: 24.7 us -> 21.6 us
    ppermute x30 -> x25, starting transfers between devices: 30.3 us -> 16.7 us  [permute(): return lax.ppermute(array, AXES, pairs)]
    ppermute x30 -> x25, waiting for transfers between devices: 40.9 us -> 44.6 us  [permute(): return lax.ppermute(array, AXES, pairs)]
    pallas_call x1 -> x6, Pallas kernels: 24.7 us -> 21.6 us  [the longest x1 20.1 us: attention(): pl.pallas_call(lambda *refs: attention_kernel(levels, peers, group, per,...]
  transfers between devices with their start and end apart: 30 -> 25, of which waited for: 15 -> 14; matrix products, arithmetic and copies ran while one was open for 1% -> 0% of each run, Pallas kernels for 0% -> 1%
where the time goes in v2:
time: 85.6 us; the launch traced here: 85.5 us
  waiting for transfers between devices  44.6 us (52%)
  Pallas kernels  21.6 us (25%)
  starting transfers between devices  16.7 us (20%)
  local copies, waits for them, and re-layouts  1.81 us (2%)
    ppermute x25, waiting for transfers between devices, permute(): return lax.ppermute(array, AXES, pairs)  44.6 us
    pallas_call x1, Pallas kernels, attention(): pl.pallas_call(lambda *refs: attention_kernel(levels, peers, group, per,...  20.1 us
    ppermute x25, starting transfers between devices, permute(): return lax.ppermute(array, AXES, pairs)  16.7 us
    unnamed x8, local copies, waits for them, and re-layouts  1.81 us
  transfers between devices with their start and end apart: 25, of which 14 were waited for; matrix products, arithmetic and copies ran while one was open for 0% of the time, Pallas kernels for 1%

profile of v2, /device:TPU:0, one launch (start us, length us, event | category | flops | bytes accessed | tf_op | source)
XLA Modules:
  0.0 85.5 jit_solution(16007518921039095731)
XLA Ops:
  0.6 0.0 copy-start
  0.6 0.9 %copy-done = bf16[64,1024]{1,0:T(8,128)(2,1)S(1)} copy-done((bf16[64,1024]{1,0:T(8,128)(2,1)S(1)}, bf16[64,1024]{1,0:T(8,128)(2,1)}, u32[]{:S(2)}) %copy-start) | copy-done | bytes 131096
  1.5 0.0 copy-start.1
  1.5 0.9 %copy-done.1 = bf16[64,1024]{1,0:T(8,128)(2,1)S(1)} copy-done((bf16[64,1024]{1,0:T(8,128)(2,1)S(1)}, bf16[64,1024]{1,0:T(8,128)(2,1)}, u32[]{:S(2)}) %copy-start.1) | copy-done | bytes 131096
  2.4 0.0 copy-start.2
  2.4 0.0 copy-start.3
  2.5 3.1 %collective-permute-start.3 = (bf16[64,2048]{1,0:T(8,128)(2,1)S(1)}, bf16[64,2048]{1,0:T(8,128)(2,1)S(1)}, u32[]{:S(2)}, u32[]{:S(2)}) collective-permute-start(bf16[64,2048]{1,0:T(8,128)(2,1)S(1)} %join.1.refs_2_), channel_id=1, source_target_pairs={{0,8},{1,9},{2,10},{3,11},{4,12},{5,13},{6,14},{7,15},{8,16},{9,17... | collective-permute-start | bytes 786440 | tf_op jit(solution)/shard_map/ppermute | solution.py:194
  5.5 1.5 %collective-permute-start.1 = (bf16[64,2048]{1,0:T(8,128)(2,1)S(1)}, bf16[64,2048]{1,0:T(8,128)(2,1)S(1)}, u32[]{:S(2)}, u32[]{:S(2)}) collective-permute-start(bf16[64,2048]{1,0:T(8,128)(2,1)S(1)} %join.1.refs_2_), channel_id=1, source_target_pairs={{0,2},{1,3},{2,0},{3,1},{4,6},{5,7},{6,4},{7,5},{8,10},{9,11},{10,... | collective-permute-start | bytes 786440 | tf_op jit(solution)/shard_map/ppermute | solution.py:194
  7.1 0.0 collective-permute-start
  7.1 6.8 %collective-permute-done.3.refs_10_ = bf16[64,2048]{1,0:T(8,128)(2,1)S(1)} collective-permute-done((bf16[64,2048]{1,0:T(8,128)(2,1)S(1)}, bf16[64,2048]{1,0:T(8,128)(2,1)S(1)}, u32[]{:S(2)}, u32[]{:S(2)}) %collective-permute-start.3) | collective-permute-done | bytes 262176 | tf_op jit(solution)/shard_map/ppermute | solution.py:194
  13.9 0.0 collective-permute-start.11
  13.9 1.5 %collective-permute-start.6 = (bf16[64,2048]{1,0:T(8,128)(2,1)S(1)}, bf16[64,2048]{1,0:T(8,128)(2,1)S(1)}, u32[]{:S(2)}, u32[]{:S(2)}) collective-permute-start(bf16[64,2048]{1,0:T(8,128)(2,1)S(1)} %collective-permute-done.3.refs_10_), channel_id=1, source_target_pairs={{0,2},{1,3},{2,0},{3,1},{4,6},{5,7},{6,4},{7,5},{8,10},{9,11},{10,... | collective-permute-start | bytes 786440 | tf_op jit(solution)/shard_map/ppermute | solution.py:194
  15.4 1.6 %collective-permute-start.4 = (bf16[64,2048]{1,0:T(8,128)(2,1)S(1)}, bf16[64,2048]{1,0:T(8,128)(2,1)S(1)}, u32[]{:S(2)}, u32[]{:S(2)}) collective-permute-start(bf16[64,2048]{1,0:T(8,128)(2,1)S(1)} %broadcast_select_fusion.1), channel_id=1, source_target_pairs={{0,4},{1,5},{2,6},{3,7},{4,0},{5,1},{6,2},{7,3},{8,12},{9,13},{10,... | collective-permute-start | bytes 786440 | tf_op jit(solution)/shard_map/ppermute | solution.py:194
  17.0 0.0 collective-permute-done.1.refs_4_
  17.0 0.0 collective-permute-start.9
  17.0 6.2 %collective-permute-done.11.refs_14_ = bf16[64,2048]{1,0:T(8,128)(2,1)S(1)} collective-permute-done((bf16[64,2048]{1,0:T(8,128)(2,1)S(1)}, bf16[64,2048]{1,0:T(8,128)(2,1)S(1)}, u32[]{:S(2)}, u32[]{:S(2)}) %collective-permute-start.11) | collective-permute-done | bytes 262176 | tf_op jit(solution)/shard_map/ppermute | solution.py:194
  23.2 0.0 collective-permute-start.2
  23.2 0.0 collective-permute-done.6.refs_12_
  23.2 1.3 %collective-permute-start.13 = (bf16[64,2048]{1,0:T(8,128)(2,1)S(1)}, bf16[64,2048]{1,0:T(8,128)(2,1)S(1)}, u32[]{:S(2)}, u32[]{:S(2)}) collective-permute-start(bf16[64,2048]{1,0:T(8,128)(2,1)S(1)} %collective-permute-done.11.refs_14_), channel_id=1, source_target_pairs={{0,2},{1,3},{2,0},{3,1},{4,6},{5,7},{6,4},{7,5},{8,10},{9,11},{10,... | collective-permute-start | bytes 786440 | tf_op jit(solution)/shard_map/ppermute | solution.py:194
  24.5 0.0 collective-permute-done.refs_3_
  24.5 1.6 %collective-permute-start.7 = (bf16[64,2048]{1,0:T(8,128)(2,1)S(1)}, bf16[64,2048]{1,0:T(8,128)(2,1)S(1)}, u32[]{:S(2)}, u32[]{:S(2)}) collective-permute-start(bf16[64,2048]{1,0:T(8,128)(2,1)S(1)} %broadcast_select_fusion), channel_id=1, source_target_pairs={{0,4},{1,5},{2,6},{3,7},{4,0},{5,1},{6,2},{7,3},{8,12},{9,13},{10,... | collective-permute-start | bytes 786440 | tf_op jit(solution)/shard_map/ppermute | solution.py:194
  26.0 0.0 collective-permute-done.4.refs_6_
  26.0 0.0 collective-permute-start.12
  26.1 0.0 collective-permute-done.9.refs_11_
  26.1 0.5 collective-permute-start.10
  26.6 0.0 collective-permute-done.2.refs_5_
  26.6 0.1 collective-permute-start.5
  26.6 5.3 %collective-permute-done.13.refs_16_ = bf16[64,2048]{1,0:T(8,128)(2,1)S(1)} collective-permute-done((bf16[64,2048]{1,0:T(8,128)(2,1)S(1)}, bf16[64,2048]{1,0:T(8,128)(2,1)S(1)}, u32[]{:S(2)}, u32[]{:S(2)}) %collective-permute-start.13) | collective-permute-done | bytes 262176 | tf_op jit(solution)/shard_map/ppermute | solution.py:194
  31.9 0.0 collective-permute-start.14
  31.9 1.1 %collective-permute-done.7.refs_8_ = bf16[64,2048]{1,0:T(8,128)(2,1)S(1)} collective-permute-done((bf16[64,2048]{1,0:T(8,128)(2,1)S(1)}, bf16[64,2048]{1,0:T(8,128)(2,1)S(1)}, u32[]{:S(2)}, u32[]{:S(2)}) %collective-permute-start.7) | collective-permute-done | bytes 262176 | tf_op jit(solution)/shard_map/ppermute | solution.py:194
  33.0 0.0 collective-permute-start.8
  33.0 0.0 collective-permute-done.5.refs_7_
  33.0 0.0 collective-permute-done.12.refs_15_
  33.0 0.0 collective-permute-done.10.refs_13_
  33.0 0.4 collective-permute-done.14.refs_17_
  33.4 1.1 %collective-permute-done.8.refs_9_ = bf16[64,2048]{1,0:T(8,128)(2,1)S(1)} collective-permute-done((bf16[64,2048]{1,0:T(8,128)(2,1)S(1)}, bf16[64,2048]{1,0:T(8,128)(2,1)S(1)}, u32[]{:S(2)}, u32[]{:S(2)}) %collective-permute-start.8) | collective-permute-done | bytes 262176 | tf_op jit(solution)/shard_map/ppermute | solution.py:194
  34.5 0.0 copy-done.2
  34.5 0.0 copy-done.3
  34.5 20.1 %attention.1 = (bf16[64,8192]{1,0:T(8,128)(2,1)}, bf16[64,8192]{1,0:T(8,128)(2,1)}, bf16[128,2048]{1,0:T(8,128)(2,1)S(1)}, bf16[256,2048]{1,0:T(8,128)(2,1)S(1)}...) custom-call(bf16[64,8192]{1,0:T(8,128)(2,1)S(1)} %copy-done.2, ...), custom_call_target="tpu_custom_call" | custom-call | flops 6442450944 | bytes 4194304 | tf_op jit(solution)/shard_map/attention/pallas_call | solution.py:155
  54.6 0.1 collective-permute-start.16
  54.7 0.4 collective-permute-start.17
  55.1 2.9 %collective-permute-done.17.refs_1_ = bf16[128,2048]{1,0:T(8,128)(2,1)S(1)} collective-permute-done((bf16[128,2048]{1,0:T(8,128)(2,1)S(1)}, bf16[128,2048]{1,0:T(8,128)(2,1)S(1)}, u32[]{:S(2)}, u32[]{:S(2)}) %collective-permute-start.17) | collective-permute-done | bytes 524320 | tf_op jit(solution)/shard_map/ppermute | solution.py:194
  58.0 0.1 first.1
  58.2 1.6 %collective-permute-start.18 = (bf16[64,2048]{1,0:T(8,128)(2,1)S(1)}, bf16[64,2048]{1,0:T(8,128)(2,1)S(1)}, u32[]{:S(2)}, u32[]{:S(2)}) collective-permute-start(bf16[64,2048]{1,0:T(8,128)(2,1)S(1)} %get-tuple-element.28), channel_id=1, source_target_pairs={{0,4},{1,5},{2,6},{3,7},{4,0},{5,1},{6,2},{7,3},{8,12},{9,13},{10,... | collective-permute-start | bytes 786440 | tf_op jit(solution)/shard_map/ppermute | solution.py:194
  59.7 0.5 collective-permute-start.19
  60.3 0.0 collective-permute-start.15
  60.3 6.3 %collective-permute-done.18.refs_2_ = bf16[64,2048]{1,0:T(8,128)(2,1)S(1)} collective-permute-done((bf16[64,2048]{1,0:T(8,128)(2,1)S(1)}, bf16[64,2048]{1,0:T(8,128)(2,1)S(1)}, u32[]{:S(2)}, u32[]{:S(2)}) %collective-permute-start.18) | collective-permute-done | bytes 262176 | tf_op jit(solution)/shard_map/ppermute | solution.py:194
  66.6 1.2 %collective-permute-done.19.refs_3_ = bf16[64,2048]{1,0:T(8,128)(2,1)S(1)} collective-permute-done((bf16[64,2048]{1,0:T(8,128)(2,1)S(1)}, bf16[64,2048]{1,0:T(8,128)(2,1)S(1)}, u32[]{:S(2)}, u32[]{:S(2)}) %collective-permute-start.19) | collective-permute-done | bytes 262176 | tf_op jit(solution)/shard_map/ppermute | solution.py:194
  67.8 0.0 collective-permute-done.16.refs_1_
  67.8 0.4 second.1
  68.2 0.6 collective-permute-start.20
  68.8 0.0 collective-permute-start.22
  68.8 0.8 collective-permute-start.23
  69.5 1.3 %collective-permute-start.21 = (bf16[64,2048]{1,0:T(8,128)(2,1)S(1)}, bf16[64,2048]{1,0:T(8,128)(2,1)S(1)}, u32[]{:S(2)}, u32[]{:S(2)}) collective-permute-start(bf16[64,2048]{1,0:T(8,128)(2,1)S(1)} %get-tuple-element.31), channel_id=1, source_target_pairs={{0,2},{1,3},{2,0},{3,1},{4,6},{5,7},{6,4},{7,5},{8,10},{9,11},{10,... | collective-permute-start | bytes 786440 | tf_op jit(solution)/shard_map/ppermute | solution.py:194
  70.8 0.0 collective-permute-done.15.refs_1_
  70.8 4.6 %collective-permute-done.20.refs_4_.refs_2_ = bf16[64,2048]{1,0:T(8,128)(2,1)S(1)} collective-permute-done((bf16[64,2048]{1,0:T(8,128)(2,1)S(1)}, bf16[64,2048]{1,0:T(8,128)(2,1)S(1)}, u32[]{:S(2)}, u32[]{:S(2)}) %collective-permute-start.20) | collective-permute-done | bytes 262176 | tf_op jit(solution)/shard_map/ppermute | solution.py:194
  75.4 0.3 collective-permute-done.22.refs_2_
  75.8 2.3 %collective-permute-done.23.refs_3_ = bf16[64,2048]{1,0:T(8,128)(2,1)S(1)} collective-permute-done((bf16[64,2048]{1,0:T(8,128)(2,1)S(1)}, bf16[64,2048]{1,0:T(8,128)(2,1)S(1)}, u32[]{:S(2)}, u32[]{:S(2)}) %collective-permute-start.23) | collective-permute-done | bytes 262176 | tf_op jit(solution)/shard_map/ppermute | solution.py:194
  78.0 0.2 third.1
  78.2 0.4 collective-permute-start.24
  78.6 2.8 %collective-permute-done.21.refs_3_ = bf16[64,2048]{1,0:T(8,128)(2,1)S(1)} collective-permute-done((bf16[64,2048]{1,0:T(8,128)(2,1)S(1)}, bf16[64,2048]{1,0:T(8,128)(2,1)S(1)}, u32[]{:S(2)}, u32[]{:S(2)}) %collective-permute-start.21) | collective-permute-done | bytes 262176 | tf_op jit(solution)/shard_map/ppermute | solution.py:194
  81.4 3.2 %collective-permute-done.24.refs_4_ = bf16[64,2048]{1,0:T(8,128)(2,1)S(1)} collective-permute-done((bf16[64,2048]{1,0:T(8,128)(2,1)S(1)}, bf16[64,2048]{1,0:T(8,128)(2,1)S(1)}, u32[]{:S(2)}, u32[]{:S(2)}) %collective-permute-start.24) | collective-permute-done | bytes 262176 | tf_op jit(solution)/shard_map/ppermute | solution.py:194
  84.6 0.8 fourth.1
  (3 shorter events, 0.1 us)
Async XLA Ops:
  0.6 0.9 %copy-start = (bf16[64,1024]{1,0:T(8,128)(2,1)S(1)}, bf16[64,1024]{1,0:T(8,128)(2,1)}, u32[]{:S(2)}) copy-start(bf16[64,1024]{1,0:T(8,128)(2,1)} %refs_0_.2) | copy-start | bytes 393220
  1.5 0.9 %copy-start.1 = (bf16[64,1024]{1,0:T(8,128)(2,1)S(1)}, bf16[64,1024]{1,0:T(8,128)(2,1)}, u32[]{:S(2)}) copy-start(bf16[64,1024]{1,0:T(8,128)(2,1)} %refs_1_.2) | copy-start | bytes 393220
  2.4 32.1 %copy-start.2 = (bf16[64,8192]{1,0:T(8,128)(2,1)S(1)}, bf16[64,8192]{1,0:T(8,128)(2,1)}, u32[]{:S(2)}) copy-start(bf16[64,8192]{1,0:T(8,128)(2,1)} %refs_0_.3) | copy-start | bytes 3145732
  2.4 32.1 %copy-start.3 = (bf16[64,8192]{1,0:T(8,128)(2,1)S(1)}, bf16[64,8192]{1,0:T(8,128)(2,1)}, u32[]{:S(2)}) copy-start(bf16[64,8192]{1,0:T(8,128)(2,1)} %refs_1_.3) | copy-start | bytes 3145732
  2.5 11.4 %collective-permute-start.3 = (bf16[64,2048]{1,0:T(8,128)(2,1)S(1)}, bf16[64,2048]{1,0:T(8,128)(2,1)S(1)}, u32[]{:S(2)}, u32[]{:S(2)}) collective-permute-start(bf16[64,2048]{1,0:T(8,128)(2,1)S(1)} %join.1.refs_2_), channel_id=1, source_target_pairs={{0,8},{1,9},{2,10},{3,11},{4,12},{5,13},{6,14},{7,15},{8,16},{9,17... | collective-permute-start | bytes 786440 | tf_op jit(solution)/shard_map/ppermute | solution.py:194
  5.5 11.4 %collective-permute-start.1 = (bf16[64,2048]{1,0:T(8,128)(2,1)S(1)}, bf16[64,2048]{1,0:T(8,128)(2,1)S(1)}, u32[]{:S(2)}, u32[]{:S(2)}) collective-permute-start(bf16[64,2048]{1,0:T(8,128)(2,1)S(1)} %join.1.refs_2_), channel_id=1, source_target_pairs={{0,2},{1,3},{2,0},{3,1},{4,6},{5,7},{6,4},{7,5},{8,10},{9,11},{10,... | collective-permute-start | bytes 786440 | tf_op jit(solution)/shard_map/ppermute | solution.py:194
  7.1 17.4 %collective-permute-start = (bf16[64,2048]{1,0:T(8,128)(2,1)S(1)}, bf16[64,2048]{1,0:T(8,128)(2,1)S(1)}, u32[]{:S(2)}, u32[]{:S(2)}) collective-permute-start(bf16[64,2048]{1,0:T(8,128)(2,1)S(1)} %join.1.refs_2_), channel_id=1, source_target_pairs={{0,1},{1,0},{2,3},{3,2},{4,5},{5,4},{6,7},{7,6},{8,9},{9,8},{10,11... | collective-permute-start | bytes 786440 | tf_op jit(solution)/shard_map/ppermute | solution.py:194
  13.9 9.3 %collective-permute-start.11 = (bf16[64,2048]{1,0:T(8,128)(2,1)S(1)}, bf16[64,2048]{1,0:T(8,128)(2,1)S(1)}, u32[]{:S(2)}, u32[]{:S(2)}) collective-permute-start(bf16[64,2048]{1,0:T(8,128)(2,1)S(1)} %collective-permute-done.3.refs_10_), channel_id=1, source_target_pairs={{0,8},{1,9},{2,10},{3,11},{4,12},{5,13},{6,14},{7,15},{8,16},{9,17... | collective-permute-start | bytes 786440 | tf_op jit(solution)/shard_map/ppermute | solution.py:194
  13.9 9.3 %collective-permute-start.6 = (bf16[64,2048]{1,0:T(8,128)(2,1)S(1)}, bf16[64,2048]{1,0:T(8,128)(2,1)S(1)}, u32[]{:S(2)}, u32[]{:S(2)}) collective-permute-start(bf16[64,2048]{1,0:T(8,128)(2,1)S(1)} %collective-permute-done.3.refs_10_), channel_id=1, source_target_pairs={{0,2},{1,3},{2,0},{3,1},{4,6},{5,7},{6,4},{7,5},{8,10},{9,11},{10,... | collective-permute-start | bytes 786440 | tf_op jit(solution)/shard_map/ppermute | solution.py:194
  15.4 10.6 %collective-permute-start.4 = (bf16[64,2048]{1,0:T(8,128)(2,1)S(1)}, bf16[64,2048]{1,0:T(8,128)(2,1)S(1)}, u32[]{:S(2)}, u32[]{:S(2)}) collective-permute-start(bf16[64,2048]{1,0:T(8,128)(2,1)S(1)} %broadcast_select_fusion.1), channel_id=1, source_target_pairs={{0,4},{1,5},{2,6},{3,7},{4,0},{5,1},{6,2},{7,3},{8,12},{9,13},{10,... | collective-permute-start | bytes 786440 | tf_op jit(solution)/shard_map/ppermute | solution.py:194
  17.0 9.1 %collective-permute-start.9 = (bf16[64,2048]{1,0:T(8,128)(2,1)S(1)}, bf16[64,2048]{1,0:T(8,128)(2,1)S(1)}, u32[]{:S(2)}, u32[]{:S(2)}) collective-permute-start(bf16[64,2048]{1,0:T(8,128)(2,1)S(1)} %collective-permute-done.3.refs_10_), channel_id=1, source_target_pairs={{0,1},{1,0},{2,3},{3,2},{4,5},{5,4},{6,7},{7,6},{8,9},{9,8},{10,11... | collective-permute-start | bytes 786440 | tf_op jit(solution)/shard_map/ppermute | solution.py:194
  23.2 3.4 %collective-permute-start.2 = (bf16[64,2048]{1,0:T(8,128)(2,1)S(1)}, bf16[64,2048]{1,0:T(8,128)(2,1)S(1)}, u32[]{:S(2)}, u32[]{:S(2)}) collective-permute-start(bf16[64,2048]{1,0:T(8,128)(2,1)S(1)} %collective-permute-done.1.refs_4_), channel_id=1, source_target_pairs={{0,1},{1,0},{2,3},{3,2},{4,5},{5,4},{6,7},{7,6},{8,9},{9,8},{10,11... | collective-permute-start | bytes 786440 | tf_op jit(solution)/shard_map/ppermute | solution.py:194
  23.2 8.7 %collective-permute-start.13 = (bf16[64,2048]{1,0:T(8,128)(2,1)S(1)}, bf16[64,2048]{1,0:T(8,128)(2,1)S(1)}, u32[]{:S(2)}, u32[]{:S(2)}) collective-permute-start(bf16[64,2048]{1,0:T(8,128)(2,1)S(1)} %collective-permute-done.11.refs_14_), channel_id=1, source_target_pairs={{0,2},{1,3},{2,0},{3,1},{4,6},{5,7},{6,4},{7,5},{8,10},{9,11},{10,... | collective-permute-start | bytes 786440 | tf_op jit(solution)/shard_map/ppermute | solution.py:194
  24.5 8.5 %collective-permute-start.7 = (bf16[64,2048]{1,0:T(8,128)(2,1)S(1)}, bf16[64,2048]{1,0:T(8,128)(2,1)S(1)}, u32[]{:S(2)}, u32[]{:S(2)}) collective-permute-start(bf16[64,2048]{1,0:T(8,128)(2,1)S(1)} %broadcast_select_fusion), channel_id=1, source_target_pairs={{0,4},{1,5},{2,6},{3,7},{4,0},{5,1},{6,2},{7,3},{8,12},{9,13},{10,... | collective-permute-start | bytes 786440 | tf_op jit(solution)/shard_map/ppermute | solution.py:194
  26.0 7.0 %collective-permute-start.12 = (bf16[64,2048]{1,0:T(8,128)(2,1)S(1)}, bf16[64,2048]{1,0:T(8,128)(2,1)S(1)}, u32[]{:S(2)}, u32[]{:S(2)}) collective-permute-start(bf16[64,2048]{1,0:T(8,128)(2,1)S(1)} %collective-permute-done.11.refs_14_), channel_id=1, source_target_pairs={{0,1},{1,0},{2,3},{3,2},{4,5},{5,4},{6,7},{7,6},{8,9},{9,8},{10,11... | collective-permute-start | bytes 786440 | tf_op jit(solution)/shard_map/ppermute | solution.py:194
  26.1 6.9 %collective-permute-start.10 = (bf16[64,2048]{1,0:T(8,128)(2,1)S(1)}, bf16[64,2048]{1,0:T(8,128)(2,1)S(1)}, u32[]{:S(2)}, u32[]{:S(2)}) collective-permute-start(bf16[64,2048]{1,0:T(8,128)(2,1)S(1)} %collective-permute-done.6.refs_12_), channel_id=1, source_target_pairs={{0,1},{1,0},{2,3},{3,2},{4,5},{5,4},{6,7},{7,6},{8,9},{9,8},{10,11... | collective-permute-start | bytes 786440 | tf_op jit(solution)/shard_map/ppermute | solution.py:194
  26.6 6.4 %collective-permute-start.5 = (bf16[64,2048]{1,0:T(8,128)(2,1)S(1)}, bf16[64,2048]{1,0:T(8,128)(2,1)S(1)}, u32[]{:S(2)}, u32[]{:S(2)}) collective-permute-start(bf16[64,2048]{1,0:T(8,128)(2,1)S(1)} %collective-permute-done.4.refs_6_), channel_id=1, source_target_pairs={{0,1},{1,0},{2,3},{3,2},{4,5},{5,4},{6,7},{7,6},{8,9},{9,8},{10,11... | collective-permute-start | bytes 786440 | tf_op jit(solution)/shard_map/ppermute | solution.py:194
  31.9 1.5 %collective-permute-start.14 = (bf16[64,2048]{1,0:T(8,128)(2,1)S(1)}, bf16[64,2048]{1,0:T(8,128)(2,1)S(1)}, u32[]{:S(2)}, u32[]{:S(2)}) collective-permute-start(bf16[64,2048]{1,0:T(8,128)(2,1)S(1)} %collective-permute-done.13.refs_16_), channel_id=1, source_target_pairs={{0,1},{1,0},{2,3},{3,2},{4,5},{5,4},{6,7},{7,6},{8,9},{9,8},{10,11... | collective-permute-start | bytes 786440 | tf_op jit(solution)/shard_map/ppermute | solution.py:194
  33.0 1.5 %collective-permute-start.8 = (bf16[64,2048]{1,0:T(8,128)(2,1)S(1)}, bf16[64,2048]{1,0:T(8,128)(2,1)S(1)}, u32[]{:S(2)}, u32[]{:S(2)}) collective-permute-start(bf16[64,2048]{1,0:T(8,128)(2,1)S(1)} %collective-permute-done.7.refs_8_), channel_id=1, source_target_pairs={{0,1},{1,0},{2,3},{3,2},{4,5},{5,4},{6,7},{7,6},{8,9},{9,8},{10,11... | collective-permute-start | bytes 786440 | tf_op jit(solution)/shard_map/ppermute | solution.py:194
  54.6 13.2 %collective-permute-start.16 = (bf16[256,2048]{1,0:T(8,128)(2,1)S(1)}, bf16[256,2048]{1,0:T(8,128)(2,1)S(1)}, u32[]{:S(2)}, u32[]{:S(2)}) collective-permute-start(bf16[256,2048]{1,0:T(8,128)(2,1)S(1)} %get-tuple-element.25), channel_id=1, source_target_pairs={{0,1},{1,0},{2,3},{3,2},{4,5},{5,4},{6,7},{7,6},{8,9},{9,8},{10,11... | collective-permute-start | bytes 3145736 | tf_op jit(solution)/shard_map/ppermute | solution.py:194
  54.7 3.3 %collective-permute-start.17 = (bf16[128,2048]{1,0:T(8,128)(2,1)S(1)}, bf16[128,2048]{1,0:T(8,128)(2,1)S(1)}, u32[]{:S(2)}, u32[]{:S(2)}) collective-permute-start(bf16[128,2048]{1,0:T(8,128)(2,1)S(1)} %get-tuple-element.27), channel_id=1, source_target_pairs={{0,1},{1,0},{2,3},{3,2},{4,5},{5,4},{6,7},{7,6},{8,9},{9,8},{10,11... | collective-permute-start | bytes 1572872 | tf_op jit(solution)/shard_map/ppermute | solution.py:194
  58.2 8.4 %collective-permute-start.18 = (bf16[64,2048]{1,0:T(8,128)(2,1)S(1)}, bf16[64,2048]{1,0:T(8,128)(2,1)S(1)}, u32[]{:S(2)}, u32[]{:S(2)}) collective-permute-start(bf16[64,2048]{1,0:T(8,128)(2,1)S(1)} %get-tuple-element.28), channel_id=1, source_target_pairs={{0,4},{1,5},{2,6},{3,7},{4,0},{5,1},{6,2},{7,3},{8,12},{9,13},{10,... | collective-permute-start | bytes 786440 | tf_op jit(solution)/shard_map/ppermute | solution.py:194
  59.7 8.1 %collective-permute-start.19 = (bf16[64,2048]{1,0:T(8,128)(2,1)S(1)}, bf16[64,2048]{1,0:T(8,128)(2,1)S(1)}, u32[]{:S(2)}, u32[]{:S(2)}) collective-permute-start(bf16[64,2048]{1,0:T(8,128)(2,1)S(1)} %get-tuple-element.29), channel_id=1, source_target_pairs={{0,2},{1,3},{2,0},{3,1},{4,6},{5,7},{6,4},{7,5},{8,10},{9,11},{10,... | collective-permute-start | bytes 786440 | tf_op jit(solution)/shard_map/ppermute | solution.py:194
  60.3 10.5 %collective-permute-start.15 = (bf16[128,2048]{1,0:T(8,128)(2,1)S(1)}, bf16[128,2048]{1,0:T(8,128)(2,1)S(1)}, u32[]{:S(2)}, u32[]{:S(2)}) collective-permute-start(bf16[128,2048]{1,0:T(8,128)(2,1)S(1)} %get-tuple-element.23), channel_id=1, source_target_pairs={{0,1},{1,0},{2,3},{3,2},{4,5},{5,4},{6,7},{7,6},{8,9},{9,8},{10,11... | collective-permute-start | bytes 1572872 | tf_op jit(solution)/shard_map/ppermute | solution.py:194
  68.2 7.3 %collective-permute-start.20 = (bf16[64,2048]{1,0:T(8,128)(2,1)S(1)}, bf16[64,2048]{1,0:T(8,128)(2,1)S(1)}, u32[]{:S(2)}, u32[]{:S(2)}) collective-permute-start(bf16[64,2048]{1,0:T(8,128)(2,1)S(1)} %get-tuple-element.30), channel_id=1, source_target_pairs={{0,4},{1,5},{2,6},{3,7},{4,0},{5,1},{6,2},{7,3},{8,12},{9,13},{10,... | collective-permute-start | bytes 786440 | tf_op jit(solution)/shard_map/ppermute | solution.py:194
  68.8 7.0 %collective-permute-start.22 = (bf16[64,2048]{1,0:T(8,128)(2,1)S(1)}, bf16[64,2048]{1,0:T(8,128)(2,1)S(1)}, u32[]{:S(2)}, u32[]{:S(2)}) collective-permute-start(bf16[64,2048]{1,0:T(8,128)(2,1)S(1)} %get-tuple-element.32), channel_id=1, source_target_pairs={{0,24},{1,25},{2,26},{3,27},{4,28},{5,29},{6,30},{7,31},{8,0},{9,1... | collective-permute-start | bytes 786440 | tf_op jit(solution)/shard_map/ppermute | solution.py:194
  68.8 9.2 %collective-permute-start.23 = (bf16[64,2048]{1,0:T(8,128)(2,1)S(1)}, bf16[64,2048]{1,0:T(8,128)(2,1)S(1)}, u32[]{:S(2)}, u32[]{:S(2)}) collective-permute-start(bf16[64,2048]{1,0:T(8,128)(2,1)S(1)} %get-tuple-element.33), channel_id=1, source_target_pairs={{0,2},{1,3},{2,0},{3,1},{4,6},{5,7},{6,4},{7,5},{8,10},{9,11},{10,... | collective-permute-start | bytes 786440 | tf_op jit(solution)/shard_map/ppermute | solution.py:194
  69.5 11.9 %collective-permute-start.21 = (bf16[64,2048]{1,0:T(8,128)(2,1)S(1)}, bf16[64,2048]{1,0:T(8,128)(2,1)S(1)}, u32[]{:S(2)}, u32[]{:S(2)}) collective-permute-start(bf16[64,2048]{1,0:T(8,128)(2,1)S(1)} %get-tuple-element.31), channel_id=1, source_target_pairs={{0,2},{1,3},{2,0},{3,1},{4,6},{5,7},{6,4},{7,5},{8,10},{9,11},{10,... | collective-permute-start | bytes 786440 | tf_op jit(solution)/shard_map/ppermute | solution.py:194
  78.2 6.4 %collective-permute-start.24 = (bf16[64,2048]{1,0:T(8,128)(2,1)S(1)}, bf16[64,2048]{1,0:T(8,128)(2,1)S(1)}, u32[]{:S(2)}, u32[]{:S(2)}) collective-permute-start(bf16[64,2048]{1,0:T(8,128)(2,1)S(1)} %third.1), channel_id=1, source_target_pairs={{0,24},{1,25},{2,26},{3,27},{4,28},{5,29},{6,30},{7,31},{8,0},{9,1... | collective-permute-start | bytes 786440 | tf_op jit(solution)/shard_map/ppermute | solution.py:194

commit v3 on v0

v3 whole, which is shorter than its diff:
```python
import jax
import jax.numpy as jnp
from jax import lax
from jax.experimental import pallas as pl
from jax.experimental.pallas import tpu as pltpu
from jax.sharding import PartitionSpec as P

HD = 128
LOG2E = 1.4426950408889634
LOW = -1e30

NN = (((1,), (0,)), ((), ()))
TN = (((0,), (0,)), ((), ()))

MIB = 2**20
AXES = ("ctx", "kvh")
WHOLE = pl.BlockSpec(memory_space=pltpu.VMEM)
HBM = pl.BlockSpec(memory_space=pltpu.HBM)


def mm(a, b, dims):
    return lax.dot_general(a, b, dims, preferred_element_type=jnp.float32)


def wide(value):
    return value.astype(jnp.float32)


def low(value):
    return value.astype(jnp.bfloat16)


def like(shape, dtype=jnp.bfloat16):
    return jax.ShapeDtypeStruct(shape, dtype)


def is_odd():
    return lax.axis_index("ctx") % 2 == 1


class Head:
    def __init__(self, index, per, group, width):
        self.index = index
        self.number = pl.program_id(0) * per + index
        self.group = group
        self.first = self.number * group * HD
        self.at_k = pl.ds(pl.multiple_of(self.number * HD, HD), HD)
        self.at_v = pl.ds(pl.multiple_of(self.number * HD + width, HD), HD)

    def column(self, r):
        return pl.ds(pl.multiple_of(self.first + r * HD, HD), HD)

    def keys(self, shards):
        return jnp.concatenate([ref[:, self.at_k] for ref in shards], axis=0)

    def values(self, shards):
        return jnp.concatenate([ref[:, self.at_v] for ref in shards], axis=0)

    def stack(self, mine, other, at):
        base = self.index * self.group
        blocks = [mine[:, (base + r) * HD : (base + r + 1) * HD] for r in range(self.group)]
        blocks += [other[at, r * HD : (r + 1) * HD] for r in range(self.group)]
        return jnp.concatenate(blocks, axis=0)

    def unstack(self, refs, value):
        rows = refs[0].shape[0]
        for side, ref in enumerate(refs):
            for r in range(self.group):
                at = (side * self.group + r) * rows
                ref[:, self.column(r)] = value[at : at + rows]

    def back(self, shards, weights, grads_t, delta, queries_low, grads_low, homes):
        rows = shards[0].shape[0]
        grad_prob = mm(self.values(shards), grads_t, NN) - delta
        grad_scores = weights * low(grad_prob)
        term = mm(self.keys(shards), grad_scores, TN)
        grad_k = low(mm(grad_scores, queries_low, NN))
        grad_v = low(mm(weights, grads_low, NN))
        for index, ref in enumerate(homes):
            part = slice(index * rows, (index + 1) * rows)
            ref[:, self.at_k] = grad_k[part]
            ref[:, self.at_v] = grad_v[part]
        return term


def split(refs, groups):
    parts = []
    for part in groups:
        parts.append(refs[: len(part)])
        refs = refs[len(part) :]
    return parts, refs


def forward_kernel(groups, group, per, *refs):
    q_ref, g_ref = refs[:2]
    others, refs = refs[2 : 2 + per], refs[2 + per :]
    shards, refs = split(refs, groups)
    outs, refs = refs[:2], refs[2:]
    homes, refs = refs[: len(groups[0])], refs[len(groups[0]) :]
    weight_refs, refs = refs[: len(groups) - 1], refs[len(groups) - 1 :]
    gt_ref, ql_ref, gl_ref, delta_ref, factor_ref, dq_ref = refs
    rows = q_ref.shape[0]
    width = shards[0][0].shape[1] // 2
    half = group * rows
    span = 2 * half
    scale = HD ** (-0.5)
    factor = scale * LOG2E
    ctx = lax.axis_index("ctx")
    kvh = lax.axis_index("kvh")
    key_pos = lax.broadcasted_iota(jnp.int32, (rows, span), 0)
    column = lax.broadcasted_iota(jnp.int32, (rows, span), 1)
    causal = key_pos <= column % rows
    own = lax.broadcasted_iota(jnp.int32, (1, span), 1) < half
    diagonal = [causal | (column >= half), causal | (column < half)]

    def choose(level, hi, j, value, other):
        if level:
            return jnp.where(ctx >= (1 << (level - 1)), value, other)
        sides = []
        for i in range(2):
            if hi == 0 and i == j:
                sides.append(value)
            else:
                before = lax.bitwise_xor(kvh, hi ^ j) < lax.bitwise_xor(kvh, i)
                sides.append(jnp.where(before, value, other))
        return jnp.where(own, sides[0], sides[1])

    class Forward(Head):
        def start(self):
            self.queries = self.stack(q_ref, others[self.index], slice(0, rows))
            self.grads = self.stack(g_ref, others[self.index], slice(rows, 2 * rows))
            self.queries_t, self.grads_t = self.queries.T, self.grads.T
            self.top, self.total, self.out_t = None, None, None
            self.scores, self.weights = [], []

        def score(self, place):
            raw = mm(self.keys(shards[place]), self.queries_t, NN)
            pieces = []
            for index, (level, hi) in enumerate(groups[place]):
                for j in range(2):
                    at = (2 * index + j) * rows
                    piece = raw[at : at + rows]
                    if level == 0 and hi == 0:
                        piece = jnp.where(diagonal[j], piece, LOW)
                    best = choose(level, hi, j, jnp.max(piece, axis=0, keepdims=True), LOW)
                    self.top = best if self.top is None else jnp.maximum(self.top, best)
                    pieces.append(piece)
            self.scores.append(pieces)

        def weigh(self, place):
            top = self.top * factor
            pieces = []
            for index, (level, hi) in enumerate(groups[place]):
                for j in range(2):
                    shift = choose(level, hi, j, top, -LOW)
                    weight = jnp.exp2(self.scores[place][2 * index + j] * factor - shift)
                    part = jnp.sum(weight, axis=0, keepdims=True)
                    self.total = part if self.total is None else self.total + part
                    pieces.append(low(weight))
            weights = jnp.concatenate(pieces, axis=0)
            self.weights.append(weights)
            if place:
                weight_refs[place - 1][self.number] = weights
            part = mm(self.values(shards[place]), weights, TN)
            self.out_t = part if self.out_t is None else self.out_t + part

        def finish(self):
            inverse = 1.0 / self.total
            out_t = low(self.out_t * inverse)
            self.unstack(outs, out_t.T)
            delta = jnp.sum(wide(self.grads_t) * wide(out_t), axis=0, keepdims=True)
            spread = jnp.broadcast_to(inverse, (HD, span)).T
            queries_low = low(wide(self.queries) * (spread * scale))
            grads_low = low(wide(self.grads) * spread)
            gt_ref[self.number] = self.grads_t
            ql_ref[self.number] = queries_low
            gl_ref[self.number] = grads_low
            delta_ref[self.number] = delta
            factor_ref[self.number] = inverse * scale
            dq_ref[self.number] = self.back(
                shards[0], self.weights[0], self.grads_t, delta, queries_low, grads_low, homes
            )

    heads = [Forward(index, per, group, width) for index in range(per)]
    places = range(len(groups))
    heads[0].start()
    for place in places:
        heads[0].score(place)
    for index, head in enumerate(heads):
        after = heads[index + 1] if index + 1 < per else None
        if after:
            after.start()
        for place in places:
            head.weigh(place)
            if after:
                after.score(place)
        head.finish()


def backward_kernel(groups, group, per, last, *refs):
    shards, refs = split(refs, groups)
    weight_refs, refs = refs[: len(groups)], refs[len(groups) :]
    gt_ref, ql_ref, gl_ref, delta_ref, factor_ref, dq_ref, *refs = refs
    dq_outs, refs = (refs[:2], refs[2:]) if last else (refs[:1], refs[1:])
    homes, refs = split(refs, groups)
    width = shards[0][0].shape[1] // 2
    for index in range(per):
        head = Head(index, per, group, width)
        at = head.number
        term = dq_ref[at]
        for place in range(len(groups)):
            term = term + head.back(
                shards[place],
                weight_refs[place][at],
                gt_ref[at],
                delta_ref[at],
                ql_ref[at],
                gl_ref[at],
                homes[place],
            )
        if last:
            head.unstack(dq_outs, low(term * factor_ref[at]).T)
        else:
            dq_outs[0][at] = term


def call(kernel, inputs, shapes, name, limit=12, grid=(), cost=None, in_spec=WHOLE, out_spec=WHOLE, scratch=()):
    return pl.pallas_call(
        kernel,
        grid=grid,
        out_shape=shapes,
        in_specs=in_spec if isinstance(in_spec, list) else [in_spec] * len(inputs),
        out_specs=[out_spec] * len(shapes),
        scratch_shapes=scratch,
        compiler_params=pltpu.CompilerParams(vmem_limit_bytes=limit * MIB),
        cost_estimate=cost,
        name=name,
    )(*inputs)


FREE = pl.CostEstimate(flops=0, bytes_accessed=0, transcendentals=0)


def merge(body, inputs, shapes, name):
    def kernel(*refs):
        body(refs[: len(inputs)], refs[len(inputs) :])

    return call(kernel, inputs, [like(shape) for shape in shapes], name)


def cost(keys, span, heads, matmuls):
    return pl.CostEstimate(flops=2 * keys * span * HD * heads * matmuls, bytes_accessed=0, transcendentals=0)


def sizes(others):
    return others[0].shape[0] // 2, len(others), others[0].shape[1] // HD


def forward(query, grad, others, held, groups):
    rows, heads, group = sizes(others)
    span = 2 * group * rows
    shards = [held[at] for part in groups for at in part]
    keys = shards[0].shape[0]
    per = heads
    steps = heads // per
    block = pl.BlockSpec((rows, per * group * HD), lambda step: (0, side() * steps + step))
    shapes = [like((rows, heads * group * HD))] * 2
    shapes += [like(shards[0].shape)] * len(groups[0])
    shapes += [like((heads, len(part) * keys, span)) for part in groups[1:]]
    shapes += [like((heads, HD, span)), like((heads, span, HD)), like((heads, span, HD))]
    shapes += [like((heads, 1, span), jnp.float32)] * 2 + [like((heads, HD, span), jnp.float32)]
    rest = call(
        lambda *refs: forward_kernel(groups, group, per, *refs),
        [query, grad, *others] + shards,
        shapes,
        "forward",
        limit=28,
        grid=(steps,),
        cost=cost(keys, span, heads, 2 * len(shards) + 4 * len(groups[0])),
        in_spec=[block] * 2 + [WHOLE] * (heads + len(shards)),
    )
    outs, rest = rest[:2], rest[2:]
    sums, rest = rest[: len(groups[0])], rest[len(groups[0]) :]
    return outs, sums, list(rest[: len(groups) - 1]), list(rest[len(groups) - 1 :])


def backward(others, held, groups, weights, state, last, after=()):
    rows, heads, group = sizes(others)
    span = 2 * group * rows
    shards = [held[at] for part in groups for at in part]
    keys = shards[0].shape[0]
    per = 2
    shapes = [like((rows, heads * group * HD))] * 2 if last else [like(state[-1].shape, state[-1].dtype)]
    heading = len(shapes)
    shapes += [like(shards[0].shape)] * len(shards)
    result = call(
        lambda *refs: backward_kernel(groups, group, per, last, *refs[len(after) :]),
        list(after) + shards + list(weights) + list(state),
        shapes,
        "backward",
        limit=14,
        grid=(heads // per,),
        cost=cost(keys, span, heads, 4 * len(shards)),
    )
    sums = dict(zip([at for part in groups for at in part], result[heading:]))
    return result[:heading], sums


def side():
    return lax.axis_index("kvh") % 2


def halves(array, place):
    rows, width = array.shape
    return pl.BlockSpec((rows, width // 2), lambda step: (0, side() ^ place))


def deal(key, value):
    rows, width = key.shape
    half = width // 2

    def kernel(key_kept, value_kept, key_sent, value_sent, kept, sent):
        kept[:, :half] = key_kept[...]
        kept[:, half:] = value_kept[...]
        sent[:, :half] = key_sent[...]
        sent[:, half:] = value_sent[...]

    specs = [halves(array, place) for place in range(2) for array in (key, value)]
    return call(kernel, [key, value] * 2, [like((rows, width))] * 2, "deal", grid=(1,), in_spec=specs, cost=FREE)


def pack(query, grad, after, heads):
    rows, width = query.shape
    share = width // 2 // heads

    def kernel(query_ref, grad_ref, after_ref, *outs):
        for index, out in enumerate(outs):
            out[:rows] = query_ref[:, index * share : (index + 1) * share]
            out[rows:] = grad_ref[:, index * share : (index + 1) * share]

    specs = [halves(query, 1), halves(grad, 1), WHOLE]
    shapes = [like((2 * rows, share))] * heads
    return call(kernel, [query, grad, after], shapes, "pack", grid=(1,), in_spec=specs, cost=FREE)


def assemble(pairs):
    rows, half = pairs[0][0].shape
    inputs = [array for pair in pairs for array in pair]

    def kernel(*refs):
        outs, sems = refs[len(inputs) : -1], refs[-1]
        copies = []
        for index, ref in enumerate(refs[: len(inputs)]):
            start = pl.multiple_of((side() ^ (index % 2)) * half, half)
            target = outs[index // 2].at[:, pl.ds(start, half)]
            copies.append(pltpu.make_async_copy(ref, target, sems.at[index]))
        for copy in copies:
            copy.start()
        for copy in copies:
            copy.wait()

    return call(
        kernel,
        inputs,
        [like((rows, 2 * half))] * len(pairs),
        "assemble",
        out_spec=HBM,
        scratch=[pltpu.SemaphoreType.DMA((len(inputs),))],
    )


def permute(array, target):
    blocks, peers = lax.axis_size("ctx"), lax.axis_size("kvh")
    pairs = []
    for c in range(blocks):
        for k in range(peers):
            to_c, to_k = target(c, k)
            pairs.append((c * peers + k, to_c % blocks * peers + to_k))
    return lax.ppermute(array, AXES, pairs)


def along(array, by):
    return permute(array, lambda c, k: (c + by, k))


def pair_swap(array):
    return permute(array, lambda c, k: (c ^ 1, k))


def across(array):
    return permute(array, lambda c, k: (c, k ^ 2))


def sibling(array):
    return permute(array, lambda c, k: (c, k ^ 1))


def gather(own, levels):
    odd = is_odd()
    held = {(0, 0): own}
    held[2, 0] = along(own, 2)
    held[0, 2] = across(own)
    for level in range(3, levels):
        held[level, 0] = along(held[level - 1, 0], 1 << (level - 2))
    held[2, 2] = across(held[2, 0])
    held[1, 0] = pair_swap(jnp.where(odd, held[2, 0], own))
    for level in range(3, levels):
        held[level, 2] = across(held[level, 0])
    held[1, 2] = pair_swap(jnp.where(odd, held[2, 2], held[0, 2]))
    return held


def shards(query_act, key_act, value_act, grad_out):
    blocks, peers = lax.axis_size("ctx"), lax.axis_size("kvh")
    assert peers == 4, peers
    levels = (blocks - 1).bit_length() + 1
    later = range(3, levels)
    rows, width = key_act.shape
    shape = (2 * rows, width)

    kept, sent = deal(key_act, value_act)

    def stack(ins, outs):
        outs[0][:rows] = ins[0][...]
        outs[0][rows:] = ins[1][...]

    (own,) = merge(stack, [kept, sibling(sent)], [shape], "stack")
    held = gather(own, levels)
    heads = width // (2 * HD)
    others = [sibling(array) for array in pack(query_act, grad_out, held[0, 2], heads)]

    group_a = [(level, 2) for level in later] + [(1, 2)]
    group_b = [(2, 2), (0, 2)]
    group_c = [(level, 0) for level in later] + [(1, 0)]
    group_d = [(2, 0), (0, 0)]
    outs, sums_a, weights, state = forward(query_act, grad_out, others, held, [group_a, group_b, group_c, group_d])
    *far_2, near_2 = sums_a
    got_far = [across(array) for array in far_2]
    got_near = pair_swap(near_2)
    (dq_t,), sums = backward(others, held, [group_b, group_c], weights[:2], state, False)
    got_out = sibling(outs[1])

    def second(ins, outs):
        two, zero, swapped, *rest = ins
        from_pair = wide(swapped[...])
        odd = is_odd()
        none = jnp.zeros_like(from_pair)
        outs[0][...] = low(wide(two[...]) + jnp.where(odd, from_pair, none))
        outs[1][...] = low(wide(zero[...]) + jnp.where(odd, none, from_pair))
        for index in range(len(later)):
            outs[2 + index][...] = low(wide(rest[2 * index][...]) + wide(rest[2 * index + 1][...]))

    far_0 = [array for pair in zip([sums[level, 0] for level in later], got_far) for array in pair]
    two_2, zero_2, *far_0 = merge(
        second, [sums[2, 2], sums[0, 2], got_near] + far_0, [shape] * (len(later) + 2), "second"
    )
    chain = far_0[-1]
    for level in range(levels - 1, 3, -1):
        chain = low(wide(far_0[level - 4]) + wide(along(chain, -(1 << (level - 2)))))
    got_chain = along(chain, -2)
    got_two = across(two_2)
    got_one = pair_swap(sums[1, 0])
    dqs, last_sums = backward(others, held, [group_d], weights[2:], state[:-1] + [dq_t], True, [two_2])
    got_dq = sibling(dqs[1])

    def third(ins, outs):
        base, chain, two, one = ins
        from_pair = wide(one[...])
        terms = jnp.where(is_odd(), from_pair, jnp.zeros_like(from_pair))
        outs[0][...] = low(wide(base[...]) + wide(chain[...]) + wide(two[...]) + terms)

    (two_0,) = merge(third, [last_sums[2, 0], got_chain, got_two, got_one], [shape], "third")
    got_chain = along(two_0, -2)
    got_zero = across(zero_2)
    out, grad_query = assemble([(outs[0], got_out), (dqs[0], got_dq)])

    def fourth(ins, outs):
        base, one, zero, chain = ins[:4]
        from_pair = wide(one[...])
        terms = jnp.where(is_odd(), jnp.zeros_like(from_pair), from_pair)
        total = low(wide(base[...]) + wide(chain[...]) + wide(zero[...]) + terms)
        outs[0][...] = total[:rows]
        outs[1][...] = total[rows:]

    kept, sent = merge(
        fourth,
        [last_sums[0, 0], got_one, got_zero, got_chain],
        [(rows, width)] * 2,
        "fourth",
    )

    def fifth(ins, outs):
        half = width // 2
        for place, ref in enumerate(ins):
            at = pl.ds(pl.multiple_of((side() ^ place) * half, half), half)
            outs[0][:, at] = ref[:, :half]
            outs[1][:, at] = ref[:, half:]

    grad_key, grad_value = merge(fifth, [kept, sibling(sent)], [(rows, width)] * 2, "fifth")
    return out, grad_query, grad_key, grad_value


def solution(mesh):
    spec = P(AXES, None)
    return jax.shard_map(
        shards, mesh=mesh, in_specs=(spec,) * 4, out_specs=(spec,) * 4, check_vma=False
    )
```

time: 192 us -> 70.7 us (0.37)
  the two profiles are of different devices: /device:TPU:29 before, /device:TPU:0 now
where the time goes in v3:
time: 70.7 us; the launch traced here: 70.5 us
  waiting for transfers between devices  26.8 us (38%)
  Pallas kernels  20.9 us (30%)
  starting transfers between devices  18.9 us (27%)
  local copies, waits for them, and re-layouts  3.03 us (4%)
  between operations  0.77 us (1%)
    ppermute x22, waiting for transfers between devices, permute(): return lax.ppermute(array, AXES, pairs)  26.8 us
    pallas_call x11, Pallas kernels, call(): pl.pallas_call(kernel, grid=grid, out_shape=shapes, in_specs=in_spec if i...  20.9 us
    ppermute x22, starting transfers between devices, permute(): return lax.ppermute(array, AXES, pairs)  18.9 us
    unnamed x10, local copies, waits for them, and re-layouts  3.03 us
  transfers between devices with their start and end apart: 22, of which 11 were waited for; matrix products, arithmetic and copies ran while one was open for 0% of the time, Pallas kernels for 14%

profile of v3, /device:TPU:0, one launch (start us, length us, event | category | flops | bytes accessed | tf_op | source)
XLA Modules:
  0.0 70.5 jit_solution(18372309538234527959)
XLA Ops:
  0.6 0.0 copy-start.3
  0.6 0.9 %copy-done.3 = bf16[64,1024]{1,0:T(8,128)(2,1)S(1)} copy-done((bf16[64,1024]{1,0:T(8,128)(2,1)S(1)}, bf16[64,1024]{1,0:T(8,128)(2,1)}, u32[]{:S(2)}) %copy-start.3) | copy-done | bytes 131096
  1.5 0.0 copy-start.4
  1.5 0.9 %copy-done.4 = bf16[64,1024]{1,0:T(8,128)(2,1)S(1)} copy-done((bf16[64,1024]{1,0:T(8,128)(2,1)S(1)}, bf16[64,1024]{1,0:T(8,128)(2,1)}, u32[]{:S(2)}) %copy-start.4) | copy-done | bytes 131096
  2.4 0.0 copy-start
  2.5 0.5 collective-permute-start
  3.0 1.0 %collective-permute-done.refs_1_ = bf16[64,1024]{1,0:T(8,128)(2,1)S(1)} collective-permute-done((bf16[64,1024]{1,0:T(8,128)(2,1)S(1)}, bf16[64,1024]{1,0:T(8,128)(2,1)S(1)}, u32[]{:S(2)}, u32[]{:S(2)}) %collective-permute-start) | collective-permute-done | bytes 131104 | tf_op jit(solution)/shard_map/ppermute | solution.py:379
  4.0 3.0 %collective-permute-start.6 = (bf16[128,1024]{1,0:T(8,128)(2,1)S(1)}, bf16[128,1024]{1,0:T(8,128)(2,1)S(1)}, u32[]{:S(2)}, u32[]{:S(2)}) collective-permute-start(bf16[128,1024]{1,0:T(8,128)(2,1)S(1)} %stack.1.refs_13_.refs_2_), channel_id=1, source_target_pairs={{0,8},{1,9},{2,10},{3,11},{4,12},{5,13},{6,14},{7,15},{8,16},{9,17... | collective-permute-start | bytes 786440 | tf_op jit(solution)/shard_map/ppermute | solution.py:379
  7.0 1.5 %collective-permute-start.1 = (bf16[128,1024]{1,0:T(8,128)(2,1)S(1)}, bf16[128,1024]{1,0:T(8,128)(2,1)S(1)}, u32[]{:S(2)}, u32[]{:S(2)}) collective-permute-start(bf16[128,1024]{1,0:T(8,128)(2,1)S(1)} %stack.1.refs_13_.refs_2_), channel_id=1, source_target_pairs={{0,2},{1,3},{2,0},{3,1},{4,6},{5,7},{6,4},{7,5},{8,10},{9,11},{10,... | collective-permute-start | bytes 786440 | tf_op jit(solution)/shard_map/ppermute | solution.py:379
  8.5 7.1 %collective-permute-done.6.refs_12_.refs_1_ = bf16[128,1024]{1,0:T(8,128)(2,1)S(1)} collective-permute-done((bf16[128,1024]{1,0:T(8,128)(2,1)S(1)}, bf16[128,1024]{1,0:T(8,128)(2,1)S(1)}, u32[]{:S(2)}, u32[]{:S(2)}) %collective-permute-start.6) | collective-permute-done | bytes 262176 | tf_op jit(solution)/shard_map/ppermute | solution.py:379
  15.6 1.5 %collective-permute-start.9 = (bf16[128,1024]{1,0:T(8,128)(2,1)S(1)}, bf16[128,1024]{1,0:T(8,128)(2,1)S(1)}, u32[]{:S(2)}, u32[]{:S(2)}) collective-permute-start(bf16[128,1024]{1,0:T(8,128)(2,1)S(1)} %collective-permute-done.6.refs_12_.refs_1_), channel_id=1, source_target_pairs={{0,2},{1,3},{2,0},{3,1},{4,6},{5,7},{6,4},{7,5},{8,10},{9,11},{10,... | collective-permute-start | bytes 786440 | tf_op jit(solution)/shard_map/ppermute | solution.py:379
  17.2 1.6 %collective-permute-start.11 = (bf16[128,1024]{1,0:T(8,128)(2,1)S(1)}, bf16[128,1024]{1,0:T(8,128)(2,1)S(1)}, u32[]{:S(2)}, u32[]{:S(2)}) collective-permute-start(bf16[128,1024]{1,0:T(8,128)(2,1)S(1)} %broadcast_select_fusion), channel_id=1, source_target_pairs={{0,4},{1,5},{2,6},{3,7},{4,0},{5,1},{6,2},{7,3},{8,12},{9,13},{10,... | collective-permute-start | bytes 786440 | tf_op jit(solution)/shard_map/ppermute | solution.py:379
  18.7 0.0 collective-permute-start.7
  18.7 0.0 collective-permute-done.1.after_ref.refs_9_.refs_1_
  18.7 0.0 copy-done
  18.7 0.0 copy-start.1
  18.8 1.2 %copy-done.1 = bf16[64,8192]{1,0:T(8,128)(2,1)S(1)} copy-done((bf16[64,8192]{1,0:T(8,128)(2,1)S(1)}, bf16[64,8192]{1,0:T(8,128)(2,1)}, u32[]{:S(2)}) %copy-start.1) | copy-done | bytes 1048600
  20.0 0.0 copy-start.2
  20.0 0.1 pack.1
  20.0 0.1 collective-permute-start.2
  20.1 0.5 collective-permute-start.3
  20.6 2.9 %collective-permute-done.9.refs_8_.refs_0_ = bf16[128,1024]{1,0:T(8,128)(2,1)S(1)} collective-permute-done((bf16[128,1024]{1,0:T(8,128)(2,1)S(1)}, bf16[128,1024]{1,0:T(8,128)(2,1)S(1)}, u32[]{:S(2)}, u32[]{:S(2)}) %collective-permute-start.9) | collective-permute-done | bytes 262176 | tf_op jit(solution)/shard_map/ppermute | solution.py:379
  23.5 0.0 collective-permute-start.4
  23.5 1.1 %collective-permute-done.11.refs_11_.refs_3_ = bf16[128,1024]{1,0:T(8,128)(2,1)S(1)} collective-permute-done((bf16[128,1024]{1,0:T(8,128)(2,1)S(1)}, bf16[128,1024]{1,0:T(8,128)(2,1)S(1)}, u32[]{:S(2)}, u32[]{:S(2)}) %collective-permute-start.11) | collective-permute-done | bytes 262176 | tf_op jit(solution)/shard_map/ppermute | solution.py:379
  24.6 0.0 collective-permute-start.5
  24.6 3.0 %collective-permute-done.7.refs_10_.refs_2_ = bf16[128,1024]{1,0:T(8,128)(2,1)S(1)} collective-permute-done((bf16[128,1024]{1,0:T(8,128)(2,1)S(1)}, bf16[128,1024]{1,0:T(8,128)(2,1)S(1)}, u32[]{:S(2)}, u32[]{:S(2)}) %collective-permute-start.7) | collective-permute-done | bytes 262176 | tf_op jit(solution)/shard_map/ppermute | solution.py:379
  27.6 0.5 collective-permute-start.8
  28.1 0.0 collective-permute-done.2.refs_2_
  28.1 0.8 %collective-permute-start.10 = (bf16[128,1024]{1,0:T(8,128)(2,1)S(1)}, bf16[128,1024]{1,0:T(8,128)(2,1)S(1)}, u32[]{:S(2)}, u32[]{:S(2)}) collective-permute-start(bf16[128,1024]{1,0:T(8,128)(2,1)S(1)} %broadcast_select_fusion.1), channel_id=1, source_target_pairs={{0,4},{1,5},{2,6},{3,7},{4,0},{5,1},{6,2},{7,3},{8,12},{9,13},{10,... | collective-permute-start | bytes 786440 | tf_op jit(solution)/shard_map/ppermute | solution.py:379
  28.9 0.0 collective-permute-done.3.refs_3_
  28.9 0.0 collective-permute-done.4.refs_4_
  28.9 0.0 collective-permute-done.5.refs_5_
  28.9 5.1 %collective-permute-done.8.refs_6_ = bf16[128,1024]{1,0:T(8,128)(2,1)S(1)} collective-permute-done((bf16[128,1024]{1,0:T(8,128)(2,1)S(1)}, bf16[128,1024]{1,0:T(8,128)(2,1)S(1)}, u32[]{:S(2)}, u32[]{:S(2)}) %collective-permute-start.8) | collective-permute-done | bytes 262176 | tf_op jit(solution)/shard_map/ppermute | solution.py:379
  33.9 0.5 collective-permute-done.10.refs_7_
  34.5 0.0 copy-done.2
  34.5 10.3 %forward.1 = (bf16[64,4096]{1,0:T(8,128)(2,1)S(1)}, bf16[64,4096]{1,0:T(8,128)(2,1)S(1)}, bf16[128,1024]{1,0:T(8,128)(2,1)S(1)}, bf16[128,1024]{1,0:T(8,128)(2,1...) custom-call(bf16[64,8192]{1,0:T(8,128)(2,1)S(1)} %copy-done, ...), custom_call_target="tpu_custom_call" | custom-call | flops 3221225472 | tf_op jit(solution)/shard_map/forward/pallas_call | solution.py:228
  44.7 0.8 %collective-permute-start.13 = (bf16[128,1024]{1,0:T(8,128)(2,1)S(1)}, bf16[128,1024]{1,0:T(8,128)(2,1)S(1)}, u32[]{:S(2)}, u32[]{:S(2)}) collective-permute-start(bf16[128,1024]{1,0:T(8,128)(2,1)S(1)} %get-tuple-element.59), channel_id=1, source_target_pairs={{0,4},{1,5},{2,6},{3,7},{4,0},{5,1},{6,2},{7,3},{8,12},{9,13},{10,... | collective-permute-start | bytes 786440 | tf_op jit(solution)/shard_map/ppermute | solution.py:379
  45.6 1.3 %collective-permute-start.14 = (bf16[128,1024]{1,0:T(8,128)(2,1)S(1)}, bf16[128,1024]{1,0:T(8,128)(2,1)S(1)}, u32[]{:S(2)}, u32[]{:S(2)}) collective-permute-start(bf16[128,1024]{1,0:T(8,128)(2,1)S(1)} %get-tuple-element.61), channel_id=1, source_target_pairs={{0,2},{1,3},{2,0},{3,1},{4,6},{5,7},{6,4},{7,5},{8,10},{9,11},{10,... | collective-permute-start | bytes 786440 | tf_op jit(solution)/shard_map/ppermute | solution.py:379
  46.9 5.1 %backward.2 = (f32[4,128,1024]{2,1,0:T(8,128)S(1)}, bf16[128,1024]{1,0:T(8,128)(2,1)S(1)}, bf16[128,1024]{1,0:T(8,128)(2,1)S(1)}, bf16[128,1024]{1,0:T(8,128)(2,1)S(1)}, bf16[128,1024]{1,0:T(8,128)(2,1)S(1)}) custom-call(bf16[128,1024]{1,0:T(8,128)(2,1)S(1)} %collective-permute-done.9.refs_8_.refs_0_, ...), custom_call_target="tpu_custom_call" | custom-call | flops 2147483648 | tf_op jit(solution)/shard_map/backward/pallas_call | solution.py:228
  52.0 1.5 %collective-permute-start.16 = (bf16[128,1024]{1,0:T(8,128)(2,1)S(1)}, bf16[128,1024]{1,0:T(8,128)(2,1)S(1)}, u32[]{:S(2)}, u32[]{:S(2)}) collective-permute-start(bf16[128,1024]{1,0:T(8,128)(2,1)S(1)} %get-tuple-element.70), channel_id=1, source_target_pairs={{0,4},{1,5},{2,6},{3,7},{4,0},{5,1},{6,2},{7,3},{8,12},{9,13},{10,... | collective-permute-start | bytes 786440 | tf_op jit(solution)/shard_map/ppermute | solution.py:379
  53.5 0.0 collective-permute-done.13.refs_2_
  53.5 0.0 collective-permute-done.14.refs_4_
  53.6 0.2 second.1
  53.8 0.8 %collective-permute-start.18 = (bf16[128,1024]{1,0:T(8,128)(2,1)S(1)}, bf16[128,1024]{1,0:T(8,128)(2,1)S(1)}, u32[]{:S(2)}, u32[]{:S(2)}) collective-permute-start(bf16[128,1024]{1,0:T(8,128)(2,1)S(1)} %get-tuple-element.73), channel_id=1, source_target_pairs={{0,24},{1,25},{2,26},{3,27},{4,28},{5,29},{6,30},{7,31},{8,0},{9,1... | collective-permute-start | bytes 786440 | tf_op jit(solution)/shard_map/ppermute | solution.py:379
  54.6 1.3 %collective-permute-start.19 = (bf16[128,1024]{1,0:T(8,128)(2,1)S(1)}, bf16[128,1024]{1,0:T(8,128)(2,1)S(1)}, u32[]{:S(2)}, u32[]{:S(2)}) collective-permute-start(bf16[128,1024]{1,0:T(8,128)(2,1)S(1)} %get-tuple-element.62.refs_0_), channel_id=1, source_target_pairs={{0,2},{1,3},{2,0},{3,1},{4,6},{5,7},{6,4},{7,5},{8,10},{9,11},{10,... | collective-permute-start | bytes 786440 | tf_op jit(solution)/shard_map/ppermute | solution.py:379
  55.9 0.0 collective-permute-start.12
  55.9 2.8 %backward.3 = (bf16[64,4096]{1,0:T(8,128)(2,1)S(1)}, bf16[64,4096]{1,0:T(8,128)(2,1)S(1)}, bf16[128,1024]{1,0:T(8,128)(2,1)S(1)}, bf16[128,1024]{1,0:T(8,128)(2,1)S(1)}) custom-call(bf16[128,1024]{1,0:T(8,128)(2,1)S(1)} %get-tuple-element.62.refs_0_, bf16[128,1024]{1,0:T(8,128)(2,1)S(1)} %collective-permute-done.6.refs_12_.refs_1_, ...), custom_call_target="tpu_custom_call" | custom-call | flops 1073741824 | tf_op jit(solution)/shard_map/backward/pallas_call | solution.py:228
  58.6 0.6 collective-permute-start.15
  59.2 0.0 collective-permute-done.16.refs_3_.refs_1_
  59.2 0.7 %collective-permute-start.17 = (bf16[128,1024]{1,0:T(8,128)(2,1)S(1)}, bf16[128,1024]{1,0:T(8,128)(2,1)S(1)}, u32[]{:S(2)}, u32[]{:S(2)}) collective-permute-start(bf16[128,1024]{1,0:T(8,128)(2,1)S(1)} %get-tuple-element.71), channel_id=1, source_target_pairs={{0,2},{1,3},{2,0},{3,1},{4,6},{5,7},{6,4},{7,5},{8,10},{9,11},{10,... | collective-permute-start | bytes 786440 | tf_op jit(solution)/shard_map/ppermute | solution.py:379
  59.9 0.3 collective-permute-done.18.refs_1_
  60.2 0.7 %collective-permute-done.19.refs_2_ = bf16[128,1024]{1,0:T(8,128)(2,1)S(1)} collective-permute-done((bf16[128,1024]{1,0:T(8,128)(2,1)S(1)}, bf16[128,1024]{1,0:T(8,128)(2,1)S(1)}, u32[]{:S(2)}, u32[]{:S(2)}) %collective-permute-start.19) | collective-permute-done | bytes 262176 | tf_op jit(solution)/shard_map/ppermute | solution.py:379
  60.9 0.1 third.1
  61.1 1.9 %collective-permute-start.20 = (bf16[128,1024]{1,0:T(8,128)(2,1)S(1)}, bf16[128,1024]{1,0:T(8,128)(2,1)S(1)}, u32[]{:S(2)}, u32[]{:S(2)}) collective-permute-start(bf16[128,1024]{1,0:T(8,128)(2,1)S(1)} %third.1), channel_id=1, source_target_pairs={{0,24},{1,25},{2,26},{3,27},{4,28},{5,29},{6,30},{7,31},{8,0},{9,1... | collective-permute-start | bytes 786440 | tf_op jit(solution)/shard_map/ppermute | solution.py:379
  62.9 4.6 %collective-permute-done.17.refs_2_ = bf16[128,1024]{1,0:T(8,128)(2,1)S(1)} collective-permute-done((bf16[128,1024]{1,0:T(8,128)(2,1)S(1)}, bf16[128,1024]{1,0:T(8,128)(2,1)S(1)}, u32[]{:S(2)}, u32[]{:S(2)}) %collective-permute-start.17) | collective-permute-done | bytes 262176 | tf_op jit(solution)/shard_map/ppermute | solution.py:379
  67.5 0.6 collective-permute-done.20.refs_3_
  68.2 0.1 fourth.1
  68.3 0.1 collective-permute-start.21
  68.4 0.0 collective-permute-done.12.refs_1_
  68.4 0.0 collective-permute-done.15.refs_3_
  68.4 1.4 %assemble.1 = (bf16[64,8192]{1,0:T(8,128)(2,1)}, bf16[64,8192]{1,0:T(8,128)(2,1)}) custom-call(bf16[64,4096]{1,0:T(8,128)(2,1)S(1)} %get-tuple-element.47.refs_0_, bf16[64,4096]{1,0:T(8,128)(2,1)S(1)} %collective-permute-done.12.refs_1_, bf16[64,4096]{1,0:T(8,128)(2,1)S(1)} %get-tuple-element.65.refs_2_, bf16[64,4096]{1,0:T(8,128)(2,1)S(1)} %collective-permute-done.15.refs_3_), custom_call_target="tpu_custom_call" | custom-call | tf_op jit(solution)/shard_map/assemble/pallas_call | solution.py:228
  69.8 0.0 collective-permute-done.21.refs_1_
  69.8 0.7 %fifth.1 = (bf16[64,1024]{1,0:T(8,128)(2,1)}, bf16[64,1024]{1,0:T(8,128)(2,1)}) custom-call(bf16[64,1024]{1,0:T(8,128)(2,1)S(1)} %get-tuple-element.74.refs_0_, bf16[64,1024]{1,0:T(8,128)(2,1)S(1)} %collective-permute-done.21.refs_1_), custom_call_target="tpu_custom_call" | custom-call | tf_op jit(solution)/shard_map/fifth/pallas_call | solution.py:228
  (4 shorter events, 0.1 us)
Async XLA Ops:
  0.6 0.9 %copy-start.3 = (bf16[64,1024]{1,0:T(8,128)(2,1)S(1)}, bf16[64,1024]{1,0:T(8,128)(2,1)}, u32[]{:S(2)}) copy-start(bf16[64,1024]{1,0:T(8,128)(2,1)} %key_sent.1) | copy-start | bytes 393220
  1.5 0.9 %copy-start.4 = (bf16[64,1024]{1,0:T(8,128)(2,1)S(1)}, bf16[64,1024]{1,0:T(8,128)(2,1)}, u32[]{:S(2)}) copy-start(bf16[64,1024]{1,0:T(8,128)(2,1)} %value_sent.1) | copy-start | bytes 393220
  2.4 16.3 %copy-start = (bf16[64,8192]{1,0:T(8,128)(2,1)S(1)}, bf16[64,8192]{1,0:T(8,128)(2,1)}, u32[]{:S(2)}) copy-start(bf16[64,8192]{1,0:T(8,128)(2,1)} %refs_0_.1) | copy-start | bytes 3145732
  2.5 1.5 %collective-permute-start = (bf16[64,1024]{1,0:T(8,128)(2,1)S(1)}, bf16[64,1024]{1,0:T(8,128)(2,1)S(1)}, u32[]{:S(2)}, u32[]{:S(2)}) collective-permute-start(bf16[64,1024]{1,0:T(8,128)(2,1)S(1)} %get-tuple-element.42), channel_id=1, source_target_pairs={{0,1},{1,0},{2,3},{3,2},{4,5},{5,4},{6,7},{7,6},{8,9},{9,8},{10,11... | collective-permute-start | bytes 393224 | tf_op jit(solution)/shard_map/ppermute | solution.py:379
  4.0 11.6 %collective-permute-start.6 = (bf16[128,1024]{1,0:T(8,128)(2,1)S(1)}, bf16[128,1024]{1,0:T(8,128)(2,1)S(1)}, u32[]{:S(2)}, u32[]{:S(2)}) collective-permute-start(bf16[128,1024]{1,0:T(8,128)(2,1)S(1)} %stack.1.refs_13_.refs_2_), channel_id=1, source_target_pairs={{0,8},{1,9},{2,10},{3,11},{4,12},{5,13},{6,14},{7,15},{8,16},{9,17... | collective-permute-start | bytes 786440 | tf_op jit(solution)/shard_map/ppermute | solution.py:379
  7.0 11.8 %collective-permute-start.1 = (bf16[128,1024]{1,0:T(8,128)(2,1)S(1)}, bf16[128,1024]{1,0:T(8,128)(2,1)S(1)}, u32[]{:S(2)}, u32[]{:S(2)}) collective-permute-start(bf16[128,1024]{1,0:T(8,128)(2,1)S(1)} %stack.1.refs_13_.refs_2_), channel_id=1, source_target_pairs={{0,2},{1,3},{2,0},{3,1},{4,6},{5,7},{6,4},{7,5},{8,10},{9,11},{10,... | collective-permute-start | bytes 786440 | tf_op jit(solution)/shard_map/ppermute | solution.py:379
  15.6 7.8 %collective-permute-start.9 = (bf16[128,1024]{1,0:T(8,128)(2,1)S(1)}, bf16[128,1024]{1,0:T(8,128)(2,1)S(1)}, u32[]{:S(2)}, u32[]{:S(2)}) collective-permute-start(bf16[128,1024]{1,0:T(8,128)(2,1)S(1)} %collective-permute-done.6.refs_12_.refs_1_), channel_id=1, source_target_pairs={{0,2},{1,3},{2,0},{3,1},{4,6},{5,7},{6,4},{7,5},{8,10},{9,11},{10,... | collective-permute-start | bytes 786440 | tf_op jit(solution)/shard_map/ppermute | solution.py:379
  17.2 7.4 %collective-permute-start.11 = (bf16[128,1024]{1,0:T(8,128)(2,1)S(1)}, bf16[128,1024]{1,0:T(8,128)(2,1)S(1)}, u32[]{:S(2)}, u32[]{:S(2)}) collective-permute-start(bf16[128,1024]{1,0:T(8,128)(2,1)S(1)} %broadcast_select_fusion), channel_id=1, source_target_pairs={{0,4},{1,5},{2,6},{3,7},{4,0},{5,1},{6,2},{7,3},{8,12},{9,13},{10,... | collective-permute-start | bytes 786440 | tf_op jit(solution)/shard_map/ppermute | solution.py:379
  18.7 8.8 %collective-permute-start.7 = (bf16[128,1024]{1,0:T(8,128)(2,1)S(1)}, bf16[128,1024]{1,0:T(8,128)(2,1)S(1)}, u32[]{:S(2)}, u32[]{:S(2)}) collective-permute-start(bf16[128,1024]{1,0:T(8,128)(2,1)S(1)} %collective-permute-done.6.refs_12_.refs_1_), channel_id=1, source_target_pairs={{0,8},{1,9},{2,10},{3,11},{4,12},{5,13},{6,14},{7,15},{8,16},{9,17... | collective-permute-start | bytes 786440 | tf_op jit(solution)/shard_map/ppermute | solution.py:379
  18.7 1.2 %copy-start.1 = (bf16[64,8192]{1,0:T(8,128)(2,1)S(1)}, bf16[64,8192]{1,0:T(8,128)(2,1)}, u32[]{:S(2)}) copy-start(bf16[64,8192]{1,0:T(8,128)(2,1)} %refs_1_.1) | copy-start | bytes 3145732
  20.0 14.5 %copy-start.2 = (bf16[64,8192]{1,0:T(8,128)(2,1)S(1)}, bf16[64,8192]{1,0:T(8,128)(2,1)}, u32[]{:S(2)}) copy-start(bf16[64,8192]{1,0:T(8,128)(2,1)} %refs_1_.1) | copy-start | bytes 3145732
  20.0 8.0 %collective-permute-start.2 = (bf16[128,1024]{1,0:T(8,128)(2,1)S(1)}, bf16[128,1024]{1,0:T(8,128)(2,1)S(1)}, u32[]{:S(2)}, u32[]{:S(2)}) collective-permute-start(bf16[128,1024]{1,0:T(8,128)(2,1)S(1)} %get-tuple-element.43), channel_id=1, source_target_pairs={{0,1},{1,0},{2,3},{3,2},{4,5},{5,4},{6,7},{7,6},{8,9},{9,8},{10,11... | collective-permute-start | bytes 786440 | tf_op jit(solution)/shard_map/ppermute | solution.py:379
  20.1 8.7 %collective-permute-start.3 = (bf16[128,1024]{1,0:T(8,128)(2,1)S(1)}, bf16[128,1024]{1,0:T(8,128)(2,1)S(1)}, u32[]{:S(2)}, u32[]{:S(2)}) collective-permute-start(bf16[128,1024]{1,0:T(8,128)(2,1)S(1)} %get-tuple-element.44), channel_id=1, source_target_pairs={{0,1},{1,0},{2,3},{3,2},{4,5},{5,4},{6,7},{7,6},{8,9},{9,8},{10,11... | collective-permute-start | bytes 786440 | tf_op jit(solution)/shard_map/ppermute | solution.py:379
  23.5 5.4 %collective-permute-start.4 = (bf16[128,1024]{1,0:T(8,128)(2,1)S(1)}, bf16[128,1024]{1,0:T(8,128)(2,1)S(1)}, u32[]{:S(2)}, u32[]{:S(2)}) collective-permute-start(bf16[128,1024]{1,0:T(8,128)(2,1)S(1)} %get-tuple-element.45), channel_id=1, source_target_pairs={{0,1},{1,0},{2,3},{3,2},{4,5},{5,4},{6,7},{7,6},{8,9},{9,8},{10,11... | collective-permute-start | bytes 786440 | tf_op jit(solution)/shard_map/ppermute | solution.py:379
  24.6 4.3 %collective-permute-start.5 = (bf16[128,1024]{1,0:T(8,128)(2,1)S(1)}, bf16[128,1024]{1,0:T(8,128)(2,1)S(1)}, u32[]{:S(2)}, u32[]{:S(2)}) collective-permute-start(bf16[128,1024]{1,0:T(8,128)(2,1)S(1)} %get-tuple-element.46), channel_id=1, source_target_pairs={{0,1},{1,0},{2,3},{3,2},{4,5},{5,4},{6,7},{7,6},{8,9},{9,8},{10,11... | collective-permute-start | bytes 786440 | tf_op jit(solution)/shard_map/ppermute | solution.py:379
  27.6 6.4 %collective-permute-start.8 = (bf16[128,1024]{1,0:T(8,128)(2,1)S(1)}, bf16[128,1024]{1,0:T(8,128)(2,1)S(1)}, u32[]{:S(2)}, u32[]{:S(2)}) collective-permute-start(bf16[128,1024]{1,0:T(8,128)(2,1)S(1)} %collective-permute-done.7.refs_10_.refs_2_), channel_id=1, source_target_pairs={{0,2},{1,3},{2,0},{3,1},{4,6},{5,7},{6,4},{7,5},{8,10},{9,11},{10,... | collective-permute-start | bytes 786440 | tf_op jit(solution)/shard_map/ppermute | solution.py:379
  28.1 6.4 %collective-permute-start.10 = (bf16[128,1024]{1,0:T(8,128)(2,1)S(1)}, bf16[128,1024]{1,0:T(8,128)(2,1)S(1)}, u32[]{:S(2)}, u32[]{:S(2)}) collective-permute-start(bf16[128,1024]{1,0:T(8,128)(2,1)S(1)} %broadcast_select_fusion.1), channel_id=1, source_target_pairs={{0,4},{1,5},{2,6},{3,7},{4,0},{5,1},{6,2},{7,3},{8,12},{9,13},{10,... | collective-permute-start | bytes 786440 | tf_op jit(solution)/shard_map/ppermute | solution.py:379
  44.7 8.8 %collective-permute-start.13 = (bf16[128,1024]{1,0:T(8,128)(2,1)S(1)}, bf16[128,1024]{1,0:T(8,128)(2,1)S(1)}, u32[]{:S(2)}, u32[]{:S(2)}) collective-permute-start(bf16[128,1024]{1,0:T(8,128)(2,1)S(1)} %get-tuple-element.59), channel_id=1, source_target_pairs={{0,4},{1,5},{2,6},{3,7},{4,0},{5,1},{6,2},{7,3},{8,12},{9,13},{10,... | collective-permute-start | bytes 786440 | tf_op jit(solution)/shard_map/ppermute | solution.py:379
  45.6 8.0 %collective-permute-start.14 = (bf16[128,1024]{1,0:T(8,128)(2,1)S(1)}, bf16[128,1024]{1,0:T(8,128)(2,1)S(1)}, u32[]{:S(2)}, u32[]{:S(2)}) collective-permute-start(bf16[128,1024]{1,0:T(8,128)(2,1)S(1)} %get-tuple-element.61), channel_id=1, source_target_pairs={{0,2},{1,3},{2,0},{3,1},{4,6},{5,7},{6,4},{7,5},{8,10},{9,11},{10,... | collective-permute-start | bytes 786440 | tf_op jit(solution)/shard_map/ppermute | solution.py:379
  52.0 7.2 %collective-permute-start.16 = (bf16[128,1024]{1,0:T(8,128)(2,1)S(1)}, bf16[128,1024]{1,0:T(8,128)(2,1)S(1)}, u32[]{:S(2)}, u32[]{:S(2)}) collective-permute-start(bf16[128,1024]{1,0:T(8,128)(2,1)S(1)} %get-tuple-element.70), channel_id=1, source_target_pairs={{0,4},{1,5},{2,6},{3,7},{4,0},{5,1},{6,2},{7,3},{8,12},{9,13},{10,... | collective-permute-start | bytes 786440 | tf_op jit(solution)/shard_map/ppermute | solution.py:379
  53.8 6.4 %collective-permute-start.18 = (bf16[128,1024]{1,0:T(8,128)(2,1)S(1)}, bf16[128,1024]{1,0:T(8,128)(2,1)S(1)}, u32[]{:S(2)}, u32[]{:S(2)}) collective-permute-start(bf16[128,1024]{1,0:T(8,128)(2,1)S(1)} %get-tuple-element.73), channel_id=1, source_target_pairs={{0,24},{1,25},{2,26},{3,27},{4,28},{5,29},{6,30},{7,31},{8,0},{9,1... | collective-permute-start | bytes 786440 | tf_op jit(solution)/shard_map/ppermute | solution.py:379
  54.6 6.4 %collective-permute-start.19 = (bf16[128,1024]{1,0:T(8,128)(2,1)S(1)}, bf16[128,1024]{1,0:T(8,128)(2,1)S(1)}, u32[]{:S(2)}, u32[]{:S(2)}) collective-permute-start(bf16[128,1024]{1,0:T(8,128)(2,1)S(1)} %get-tuple-element.62.refs_0_), channel_id=1, source_target_pairs={{0,2},{1,3},{2,0},{3,1},{4,6},{5,7},{6,4},{7,5},{8,10},{9,11},{10,... | collective-permute-start | bytes 786440 | tf_op jit(solution)/shard_map/ppermute | solution.py:379
  55.9 12.5 %collective-permute-start.12 = (bf16[64,4096]{1,0:T(8,128)(2,1)S(1)}, bf16[64,4096]{1,0:T(8,128)(2,1)S(1)}, u32[]{:S(2)}, u32[]{:S(2)}) collective-permute-start(bf16[64,4096]{1,0:T(8,128)(2,1)S(1)} %get-tuple-element.48), channel_id=1, source_target_pairs={{0,1},{1,0},{2,3},{3,2},{4,5},{5,4},{6,7},{7,6},{8,9},{9,8},{10,11... | collective-permute-start | bytes 1572872 | tf_op jit(solution)/shard_map/ppermute | solution.py:379
  58.6 9.8 %collective-permute-start.15 = (bf16[64,4096]{1,0:T(8,128)(2,1)S(1)}, bf16[64,4096]{1,0:T(8,128)(2,1)S(1)}, u32[]{:S(2)}, u32[]{:S(2)}) collective-permute-start(bf16[64,4096]{1,0:T(8,128)(2,1)S(1)} %get-tuple-element.66), channel_id=1, source_target_pairs={{0,1},{1,0},{2,3},{3,2},{4,5},{5,4},{6,7},{7,6},{8,9},{9,8},{10,11... | collective-permute-start | bytes 1572872 | tf_op jit(solution)/shard_map/ppermute | solution.py:379
  59.2 8.3 %collective-permute-start.17 = (bf16[128,1024]{1,0:T(8,128)(2,1)S(1)}, bf16[128,1024]{1,0:T(8,128)(2,1)S(1)}, u32[]{:S(2)}, u32[]{:S(2)}) collective-permute-start(bf16[128,1024]{1,0:T(8,128)(2,1)S(1)} %get-tuple-element.71), channel_id=1, source_target_pairs={{0,2},{1,3},{2,0},{3,1},{4,6},{5,7},{6,4},{7,5},{8,10},{9,11},{10,... | collective-permute-start | bytes 786440 | tf_op jit(solution)/shard_map/ppermute | solution.py:379
  61.1 7.1 %collective-permute-start.20 = (bf16[128,1024]{1,0:T(8,128)(2,1)S(1)}, bf16[128,1024]{1,0:T(8,128)(2,1)S(1)}, u32[]{:S(2)}, u32[]{:S(2)}) collective-permute-start(bf16[128,1024]{1,0:T(8,128)(2,1)S(1)} %third.1), channel_id=1, source_target_pairs={{0,24},{1,25},{2,26},{3,27},{4,28},{5,29},{6,30},{7,31},{8,0},{9,1... | collective-permute-start | bytes 786440 | tf_op jit(solution)/shard_map/ppermute | solution.py:379
  68.3 1.5 %collective-permute-start.21 = (bf16[64,1024]{1,0:T(8,128)(2,1)S(1)}, bf16[64,1024]{1,0:T(8,128)(2,1)S(1)}, u32[]{:S(2)}, u32[]{:S(2)}) collective-permute-start(bf16[64,1024]{1,0:T(8,128)(2,1)S(1)} %get-tuple-element.75), channel_id=1, source_target_pairs={{0,1},{1,0},{2,3},{3,2},{4,5},{5,4},{6,7},{7,6},{8,9},{9,8},{10,11... | collective-permute-start | bytes 393224 | tf_op jit(solution)/shard_map/ppermute | solution.py:379

commit v4 on v3

--- a/solution.py
+++ b/solution.py
@@ -133,36 +133,46 @@
             self.top, self.total, self.out_t = None, None, None
             self.scores, self.weights = [], []
 
-        def score(self, place):
-            raw = mm(self.keys(shards[place]), self.queries_t, NN)
-            pieces = []
-            for index, (level, hi) in enumerate(groups[place]):
-                for j in range(2):
-                    at = (2 * index + j) * rows
-                    piece = raw[at : at + rows]
-                    if level == 0 and hi == 0:
-                        piece = jnp.where(diagonal[j], piece, LOW)
-                    best = choose(level, hi, j, jnp.max(piece, axis=0, keepdims=True), LOW)
-                    self.top = best if self.top is None else jnp.maximum(self.top, best)
-                    pieces.append(piece)
-            self.scores.append(pieces)
+        def score(self):
+            used = [shards[place][index] for place in places for index in active[place]]
+            raw = mm(self.keys(used), self.queries_t, NN)
+            at = 0
+            for place in places:
+                pieces = []
+                for index in active[place]:
+                    level, hi = groups[place][index]
+                    for j in range(2):
+                        piece = raw[at : at + rows]
+                        at += rows
+                        if level == 0 and hi == 0:
+                            piece = jnp.where(diagonal[j], piece, LOW)
+                        best = choose(level, hi, j, jnp.max(piece, axis=0, keepdims=True), LOW)
+                        self.top = best if self.top is None else jnp.maximum(self.top, best)
+                        pieces.append(piece)
+                self.scores.append(pieces)
 
         def weigh(self, place):
             top = self.top * factor
             pieces = []
-            for index, (level, hi) in enumerate(groups[place]):
+            for order, index in enumerate(active[place]):
+                level, hi = groups[place][index]
                 for j in range(2):
                     shift = choose(level, hi, j, top, -LOW)
-                    weight = jnp.exp2(self.scores[place][2 * index + j] * factor - shift)
+                    weight = jnp.exp2(self.scores[place][2 * order + j] * factor - shift)
                     part = jnp.sum(weight, axis=0, keepdims=True)
                     self.total = part if self.total is None else self.total + part
                     pieces.append(low(weight))
-            weights = jnp.concatenate(pieces, axis=0)
-            self.weights.append(weights)
+            self.weights.append(jnp.concatenate(pieces, axis=0) if pieces else None)
             if place:
-                weight_refs[place - 1][self.number] = weights
-            part = mm(self.values(shards[place]), weights, TN)
-            self.out_t = part if self.out_t is None else self.out_t + part
+                for index in range(len(groups[place])):
+                    value = jnp.zeros((2 * rows, span), jnp.bfloat16)
+                    if index in active[place]:
+                        at = active[place].index(index)
+                        value = self.weights[place][2 * rows * at : 2 * rows * (at + 1)]
+                    weight_refs[place - 1][self.number, 2 * rows * index : 2 * rows * (index + 1)] = value
+            if pieces:
+                part = mm(self.values([shards[place][index] for index in active[place]]), self.weights[place], TN)
+                self.out_t = part if self.out_t is None else self.out_t + part
 
         def finish(self):
             inverse = 1.0 / self.total
@@ -178,23 +188,42 @@
             delta_ref[self.number] = delta
             factor_ref[self.number] = inverse * scale
             dq_ref[self.number] = self.back(
-                shards[0], self.weights[0], self.grads_t, delta, queries_low, grads_low, homes
+                [shards[0][index] for index in active[0]],
+                self.weights[0],
+                self.grads_t,
+                delta,
+                queries_low,
+                grads_low,
+                [homes[index] for index in active[0]],
             )
 
-    heads = [Forward(index, per, group, width) for index in range(per)]
+    def run(counted):
+        active[:] = [[index for index, at in enumerate(part) if counted(at[0])] for part in groups]
+        heads = [Forward(index, per, group, width) for index in range(per)]
+        heads[0].start()
+        heads[0].score()
+        for index, head in enumerate(heads):
+            after = heads[index + 1] if index + 1 < per else None
+            if after:
+                after.start()
+                after.score()
+            for place in places:
+                head.weigh(place)
+            head.finish()
+
     places = range(len(groups))
-    heads[0].start()
-    for place in places:
-        heads[0].score(place)
-    for index, head in enumerate(heads):
-        after = heads[index + 1] if index + 1 < per else None
-        if after:
-            after.start()
-        for place in places:
-            head.weigh(place)
-            if after:
-                after.score(place)
-        head.finish()
+    active = []
+
+    @pl.when(ctx >= 2)
+    def _():
+        run(lambda level: True)
+
+    @pl.when(ctx < 2)
+    def _():
+        run(lambda level: level < 2)
+        for index, (level, _) in enumerate(groups[0]):
+            if level >= 2:
+                homes[index][...] = jnp.zeros_like(homes[index])
 
 
 def backward_kernel(groups, group, per, last, *refs):
@@ -315,20 +344,6 @@
     return pl.BlockSpec((rows, width // 2), lambda step: (0, side() ^ place))
 
 
-def deal(key, value):
-    rows, width = key.shape
-    half = width // 2
-
-    def kernel(key_kept, value_kept, key_sent, value_sent, kept, sent):
-        kept[:, :half] = key_kept[...]
-        kept[:, half:] = value_kept[...]
-        sent[:, :half] = key_sent[...]
-        sent[:, half:] = value_sent[...]
-
-    specs = [halves(array, place) for place in range(2) for array in (key, value)]
-    return call(kernel, [key, value] * 2, [like((rows, width))] * 2, "deal", grid=(1,), in_spec=specs, cost=FREE)
-
-
 def pack(query, grad, after, heads):
     rows, width = query.shape
     share = width // 2 // heads
@@ -369,18 +384,19 @@
     )
 
 
-def permute(array, target):
+def permute(array, target, wrap=True):
     blocks, peers = lax.axis_size("ctx"), lax.axis_size("kvh")
     pairs = []
     for c in range(blocks):
         for k in range(peers):
             to_c, to_k = target(c, k)
-            pairs.append((c * peers + k, to_c % blocks * peers + to_k))
+            if wrap or 0 <= to_c < blocks:
+                pairs.append((c * peers + k, to_c % blocks * peers + to_k))
     return lax.ppermute(array, AXES, pairs)
 
 
-def along(array, by):
-    return permute(array, lambda c, k: (c + by, k))
+def along(array, by, wrap=True):
+    return permute(array, lambda c, k: (c + by, k), wrap)
 
 
 def pair_swap(array):
@@ -418,7 +434,14 @@
     rows, width = key_act.shape
     shape = (2 * rows, width)
 
-    kept, sent = deal(key_act, value_act)
+    def part(place):
+        half = width // 2
+        start = (side() ^ place) * half
+        return jnp.concatenate(
+            [lax.dynamic_slice_in_dim(array, start, half, 1) for array in (key_act, value_act)], axis=1
+        )
+
+    kept, sent = part(0), part(1)
 
     def stack(ins, outs):
         outs[0][:rows] = ins[0][...]
@@ -430,37 +453,40 @@
     others = [sibling(array) for array in pack(query_act, grad_out, held[0, 2], heads)]
 
     group_a = [(level, 2) for level in later] + [(1, 2)]
-    group_b = [(2, 2), (0, 2)]
-    group_c = [(level, 0) for level in later] + [(1, 0)]
+    group_b = [(2, 2), (0, 2)] + [(level, 0) for level in later] + [(1, 0)]
     group_d = [(2, 0), (0, 0)]
-    outs, sums_a, weights, state = forward(query_act, grad_out, others, held, [group_a, group_b, group_c, group_d])
+    outs, sums_a, weights, state = forward(query_act, grad_out, others, held, [group_a, group_b, group_d])
     *far_2, near_2 = sums_a
     got_far = [across(array) for array in far_2]
     got_near = pair_swap(near_2)
-    (dq_t,), sums = backward(others, held, [group_b, group_c], weights[:2], state, False)
+    (dq_t,), sums = backward(others, held, [group_b], weights[:1], state, False)
     got_out = sibling(outs[1])
 
     def second(ins, outs):
-        two, zero, swapped, *rest = ins
+        for index, out in enumerate(outs):
+            out[...] = low(wide(ins[2 * index][...]) + wide(ins[2 * index + 1][...]))
+
+    far_0 = [array for pair in zip([sums[level, 0] for level in later], got_far) for array in pair]
+    far_0 = merge(second, far_0, [shape] * len(later), "second")
+
+    def aside(ins, outs):
+        two, zero, swapped = ins
         from_pair = wide(swapped[...])
         odd = is_odd()
         none = jnp.zeros_like(from_pair)
         outs[0][...] = low(wide(two[...]) + jnp.where(odd, from_pair, none))
         outs[1][...] = low(wide(zero[...]) + jnp.where(odd, none, from_pair))
-        for index in range(len(later)):
-            outs[2 + index][...] = low(wide(rest[2 * index][...]) + wide(rest[2 * index + 1][...]))
-
-    far_0 = [array for pair in zip([sums[level, 0] for level in later], got_far) for array in pair]
-    two_2, zero_2, *far_0 = merge(
-        second, [sums[2, 2], sums[0, 2], got_near] + far_0, [shape] * (len(later) + 2), "second"
+
+    two_2, zero_2 = merge(
+        aside, [sums[2, 2], sums[0, 2], got_near], [shape] * 2, "aside"
     )
     chain = far_0[-1]
     for level in range(levels - 1, 3, -1):
         chain = low(wide(far_0[level - 4]) + wide(along(chain, -(1 << (level - 2)))))
-    got_chain = along(chain, -2)
+    got_chain = along(chain, -2, False)
     got_two = across(two_2)
     got_one = pair_swap(sums[1, 0])
-    dqs, last_sums = backward(others, held, [group_d], weights[2:], state[:-1] + [dq_t], True, [two_2])
+    dqs, last_sums = backward(others, held, [group_d], weights[1:], state[:-1] + [dq_t], True, [two_2])
     got_dq = sibling(dqs[1])
 
     def third(ins, outs):
@@ -470,7 +496,7 @@
         outs[0][...] = low(wide(base[...]) + wide(chain[...]) + wide(two[...]) + terms)
 
     (two_0,) = merge(third, [last_sums[2, 0], got_chain, got_two, got_one], [shape], "third")
-    got_chain = along(two_0, -2)
+    got_chain = along(two_0, -2, False)
     got_zero = across(zero_2)
     out, grad_query = assemble([(outs[0], got_out), (dqs[0], got_dq)])
 

time: 70.7 us -> 69.4 us (0.982)
  waiting for transfers between devices: 26.8 us -> 31.9 us
  Pallas kernels: 20.9 us -> 16.2 us
  local copies, waits for them, and re-layouts: 3.03 us -> 1.11 us
    ppermute x22, waiting for transfers between devices: 26.8 us -> 31.9 us  [permute(): return lax.ppermute(array, AXES, pairs)]
    pallas_call x11, Pallas kernels: 20.9 us -> 16.2 us  [call(): pl.pallas_call(kernel, grid=grid, out_shape=shapes, in_specs=in_spec if i...]
    unnamed x10 -> x4, local copies, waits for them, and re-layouts: 3.03 us -> 0.01 us
    dynamic_slice x0 -> x1, local copies, waits for them, and re-layouts: none -> 1.1 us  [part(): lax.dynamic_slice_in_dim(array, start, half, 1)]
  transfers between devices with their start and end apart: 22 -> 22, of which waited for: 11 -> 10; matrix products, arithmetic and copies ran while one was open for 0% -> 0% of each run, Pallas kernels for 14% -> 13%
where the time goes in v4:
time: 69.4 us; the launch traced here: 69 us
  waiting for transfers between devices  31.9 us (46%)
  starting transfers between devices  19 us (27%)
  Pallas kernels  16.2 us (23%)
  local copies, waits for them, and re-layouts  1.11 us (2%)
  between operations  0.84 us (1%)
    ppermute x22, waiting for transfers between devices, permute(): return lax.ppermute(array, AXES, pairs)  31.9 us
    ppermute x22, starting transfers between devices, permute(): return lax.ppermute(array, AXES, pairs)  19 us
    pallas_call x11, Pallas kernels, call(): pl.pallas_call(kernel, grid=grid, out_shape=shapes, in_specs=in_spec if i...  16.2 us
  transfers between devices with their start and end apart: 22, of which 10 were waited for; matrix products, arithmetic and copies ran while one was open for 0% of the time, Pallas kernels for 13%

profile of v4, /device:TPU:0, one launch (start us, length us, event | category | flops | bytes accessed | tf_op | source)
XLA Modules:
  0.0 69.0 jit_solution(15822127765243597741)
XLA Ops:
  0.6 0.0 copy-start.1
  0.6 0.0 copy-start
  0.7 1.1 %constant_dynamic-slice_fusion = (bf16[64,512]{1,0:T(8,128)(2,1)S(1)}, bf16[64,512]{1,0:T(8,128)(2,1)S(1)}, bf16[64,512]{1,0:T(8,128)(2,1)S(1)}, bf16[64,512]{1,0:T(8,128)(2,1)S(1)}) fusion(bf16[64,1024]{1,0:T(8,128)(2,1)} %param.6, s32[]{:T(128)S(6)} %select_n.35, s32[]{:T(128)S(6)} %select_n.34, bf16[64,1024]{1,0:T(8,128)(2,1)} %param.5), kind=kLoop, calls=%fused_computation.4 | loop fusion | bytes 524296 | tf_op jit(solution)/shard_map/dynamic_slice | solution.py:441
  1.8 0.5 collective-permute-start
  2.3 1.0 %collective-permute-done.refs_1_ = bf16[64,1024]{1,0:T(8,128)(2,1)S(1)} collective-permute-done((bf16[64,1024]{1,0:T(8,128)(2,1)S(1)}, bf16[64,1024]{1,0:T(8,128)(2,1)S(1)}, u32[]{:S(2)}, u32[]{:S(2)}) %collective-permute-start) | collective-permute-done | bytes 131104 | tf_op jit(solution)/shard_map/ppermute | solution.py:395
  3.3 3.0 %collective-permute-start.6 = (bf16[128,1024]{1,0:T(8,128)(2,1)S(1)}, bf16[128,1024]{1,0:T(8,128)(2,1)S(1)}, u32[]{:S(2)}, u32[]{:S(2)}) collective-permute-start(bf16[128,1024]{1,0:T(8,128)(2,1)S(1)} %stack.1.refs_13_.refs_2_), channel_id=1, source_target_pairs={{0,8},{1,9},{2,10},{3,11},{4,12},{5,13},{6,14},{7,15},{8,16},{9,17... | collective-permute-start | bytes 786440 | tf_op jit(solution)/shard_map/ppermute | solution.py:395
  6.3 1.5 %collective-permute-start.1 = (bf16[128,1024]{1,0:T(8,128)(2,1)S(1)}, bf16[128,1024]{1,0:T(8,128)(2,1)S(1)}, u32[]{:S(2)}, u32[]{:S(2)}) collective-permute-start(bf16[128,1024]{1,0:T(8,128)(2,1)S(1)} %stack.1.refs_13_.refs_2_), channel_id=1, source_target_pairs={{0,2},{1,3},{2,0},{3,1},{4,6},{5,7},{6,4},{7,5},{8,10},{9,11},{10,... | collective-permute-start | bytes 786440 | tf_op jit(solution)/shard_map/ppermute | solution.py:395
  7.8 7.1 %collective-permute-done.6.refs_12_.refs_1_ = bf16[128,1024]{1,0:T(8,128)(2,1)S(1)} collective-permute-done((bf16[128,1024]{1,0:T(8,128)(2,1)S(1)}, bf16[128,1024]{1,0:T(8,128)(2,1)S(1)}, u32[]{:S(2)}, u32[]{:S(2)}) %collective-permute-start.6) | collective-permute-done | bytes 262176 | tf_op jit(solution)/shard_map/ppermute | solution.py:395
  15.0 1.5 %collective-permute-start.9 = (bf16[128,1024]{1,0:T(8,128)(2,1)S(1)}, bf16[128,1024]{1,0:T(8,128)(2,1)S(1)}, u32[]{:S(2)}, u32[]{:S(2)}) collective-permute-start(bf16[128,1024]{1,0:T(8,128)(2,1)S(1)} %collective-permute-done.6.refs_12_.refs_1_), channel_id=1, source_target_pairs={{0,2},{1,3},{2,0},{3,1},{4,6},{5,7},{6,4},{7,5},{8,10},{9,11},{10,... | collective-permute-start | bytes 786440 | tf_op jit(solution)/shard_map/ppermute | solution.py:395
  16.5 1.6 %collective-permute-start.11 = (bf16[128,1024]{1,0:T(8,128)(2,1)S(1)}, bf16[128,1024]{1,0:T(8,128)(2,1)S(1)}, u32[]{:S(2)}, u32[]{:S(2)}) collective-permute-start(bf16[128,1024]{1,0:T(8,128)(2,1)S(1)} %broadcast_select_fusion), channel_id=1, source_target_pairs={{0,4},{1,5},{2,6},{3,7},{4,0},{5,1},{6,2},{7,3},{8,12},{9,13},{10,... | collective-permute-start | bytes 786440 | tf_op jit(solution)/shard_map/ppermute | solution.py:395
  18.1 0.0 collective-permute-start.7
  18.1 0.0 collective-permute-done.1.after_ref.refs_9_.refs_1_
  18.1 0.0 copy-done.1
  18.1 0.0 copy-done
  18.1 0.1 pack.1
  18.2 0.1 collective-permute-start.2
  18.3 0.5 collective-permute-start.3
  18.7 4.1 %collective-permute-done.9.refs_8_.refs_0_ = bf16[128,1024]{1,0:T(8,128)(2,1)S(1)} collective-permute-done((bf16[128,1024]{1,0:T(8,128)(2,1)S(1)}, bf16[128,1024]{1,0:T(8,128)(2,1)S(1)}, u32[]{:S(2)}, u32[]{:S(2)}) %collective-permute-start.9) | collective-permute-done | bytes 262176 | tf_op jit(solution)/shard_map/ppermute | solution.py:395
  22.8 0.0 collective-permute-start.4
  22.8 1.1 %collective-permute-done.11.refs_11_.refs_3_ = bf16[128,1024]{1,0:T(8,128)(2,1)S(1)} collective-permute-done((bf16[128,1024]{1,0:T(8,128)(2,1)S(1)}, bf16[128,1024]{1,0:T(8,128)(2,1)S(1)}, u32[]{:S(2)}, u32[]{:S(2)}) %collective-permute-start.11) | collective-permute-done | bytes 262176 | tf_op jit(solution)/shard_map/ppermute | solution.py:395
  23.9 0.0 collective-permute-start.5
  23.9 3.0 %collective-permute-done.7.refs_10_.refs_2_ = bf16[128,1024]{1,0:T(8,128)(2,1)S(1)} collective-permute-done((bf16[128,1024]{1,0:T(8,128)(2,1)S(1)}, bf16[128,1024]{1,0:T(8,128)(2,1)S(1)}, u32[]{:S(2)}, u32[]{:S(2)}) %collective-permute-start.7) | collective-permute-done | bytes 262176 | tf_op jit(solution)/shard_map/ppermute | solution.py:395
  26.9 0.5 collective-permute-start.8
  27.4 0.0 collective-permute-done.2.refs_2_
  27.4 0.8 %collective-permute-start.10 = (bf16[128,1024]{1,0:T(8,128)(2,1)S(1)}, bf16[128,1024]{1,0:T(8,128)(2,1)S(1)}, u32[]{:S(2)}, u32[]{:S(2)}) collective-permute-start(bf16[128,1024]{1,0:T(8,128)(2,1)S(1)} %broadcast_select_fusion.1), channel_id=1, source_target_pairs={{0,4},{1,5},{2,6},{3,7},{4,0},{5,1},{6,2},{7,3},{8,12},{9,13},{10,... | collective-permute-start | bytes 786440 | tf_op jit(solution)/shard_map/ppermute | solution.py:395
  28.2 0.0 collective-permute-done.3.refs_3_
  28.2 0.0 collective-permute-done.4.refs_4_
  28.2 0.0 collective-permute-done.5.refs_5_
  28.2 5.1 %collective-permute-done.8.refs_6_ = bf16[128,1024]{1,0:T(8,128)(2,1)S(1)} collective-permute-done((bf16[128,1024]{1,0:T(8,128)(2,1)S(1)}, bf16[128,1024]{1,0:T(8,128)(2,1)S(1)}, u32[]{:S(2)}, u32[]{:S(2)}) %collective-permute-start.8) | collective-permute-done | bytes 262176 | tf_op jit(solution)/shard_map/ppermute | solution.py:395
  33.3 0.5 collective-permute-done.10.refs_7_
  33.8 6.4 %forward.1 = (bf16[64,4096]{1,0:T(8,128)(2,1)S(1)}, bf16[64,4096]{1,0:T(8,128)(2,1)S(1)}, bf16[128,1024]{1,0:T(8,128)(2,1)S(1)}, bf16[128,1024]{1,0:T(8,128)(2,1...) custom-call(bf16[64,8192]{1,0:T(8,128)(2,1)S(1)} %copy-done, ...), custom_call_target="tpu_custom_call" | custom-call | flops 3221225472 | tf_op jit(solution)/shard_map/forward/pallas_call | solution.py:257
  40.2 0.8 %collective-permute-start.13 = (bf16[128,1024]{1,0:T(8,128)(2,1)S(1)}, bf16[128,1024]{1,0:T(8,128)(2,1)S(1)}, u32[]{:S(2)}, u32[]{:S(2)}) collective-permute-start(bf16[128,1024]{1,0:T(8,128)(2,1)S(1)} %get-tuple-element.52), channel_id=1, source_target_pairs={{0,4},{1,5},{2,6},{3,7},{4,0},{5,1},{6,2},{7,3},{8,12},{9,13},{10,... | collective-permute-start | bytes 786440 | tf_op jit(solution)/shard_map/ppermute | solution.py:395
  41.0 1.3 %collective-permute-start.17 = (bf16[128,1024]{1,0:T(8,128)(2,1)S(1)}, bf16[128,1024]{1,0:T(8,128)(2,1)S(1)}, u32[]{:S(2)}, u32[]{:S(2)}) collective-permute-start(bf16[128,1024]{1,0:T(8,128)(2,1)S(1)} %get-tuple-element.65), channel_id=1, source_target_pairs={{0,2},{1,3},{2,0},{3,1},{4,6},{5,7},{6,4},{7,5},{8,10},{9,11},{10,... | collective-permute-start | bytes 786440 | tf_op jit(solution)/shard_map/ppermute | solution.py:395
  42.3 4.3 %backward.2 = (f32[4,128,1024]{2,1,0:T(8,128)S(1)}, bf16[128,1024]{1,0:T(8,128)(2,1)S(1)}, bf16[128,1024]{1,0:T(8,128)(2,1)S(1)}, bf16[128,1024]{1,0:T(8,128)(2,1)S(1)}, bf16[128,1024]{1,0:T(8,128)(2,1)S(1)}) custom-call(bf16[128,1024]{1,0:T(8,128)(2,1)S(1)} %collective-permute-done.9.refs_8_.refs_0_, ...), custom_call_target="tpu_custom_call" | custom-call | flops 2147483648 | tf_op jit(solution)/shard_map/backward/pallas_call | solution.py:257
  46.6 1.5 %collective-permute-start.15 = (bf16[128,1024]{1,0:T(8,128)(2,1)S(1)}, bf16[128,1024]{1,0:T(8,128)(2,1)S(1)}, u32[]{:S(2)}, u32[]{:S(2)}) collective-permute-start(bf16[128,1024]{1,0:T(8,128)(2,1)S(1)} %get-tuple-element.61), channel_id=1, source_target_pairs={{0,4},{1,5},{2,6},{3,7},{4,0},{5,1},{6,2},{7,3},{8,12},{9,13},{10,... | collective-permute-start | bytes 786440 | tf_op jit(solution)/shard_map/ppermute | solution.py:395
  48.1 0.0 collective-permute-done.13.refs_2_
  48.1 0.2 aside.1
  48.3 1.6 %collective-permute-start.19 = (bf16[128,1024]{1,0:T(8,128)(2,1)S(1)}, bf16[128,1024]{1,0:T(8,128)(2,1)S(1)}, u32[]{:S(2)}, u32[]{:S(2)}) collective-permute-start(bf16[128,1024]{1,0:T(8,128)(2,1)S(1)} %get-tuple-element.53.refs_0_), channel_id=1, source_target_pairs={{0,2},{1,3},{2,0},{3,1},{4,6},{5,7},{6,4},{7,5},{8,10},{9,11},{10,... | collective-permute-start | bytes 786440 | tf_op jit(solution)/shard_map/ppermute | solution.py:395
  49.9 0.0 collective-permute-done.17.refs_1_
  49.9 0.1 second.1
  50.0 1.3 %collective-permute-start.18 = (bf16[128,1024]{1,0:T(8,128)(2,1)S(1)}, bf16[128,1024]{1,0:T(8,128)(2,1)S(1)}, u32[]{:S(2)}, u32[]{:S(2)}) collective-permute-start(bf16[128,1024]{1,0:T(8,128)(2,1)S(1)} %second.1), channel_id=1, source_target_pairs={{8,0},{9,1},{10,2},{11,3},{12,4},{13,5},{14,6},{15,7},{16,8},{17,9... | collective-permute-start | bytes 786440 | tf_op jit(solution)/shard_map/ppermute | solution.py:395
  51.3 0.1 collective-permute-start.12
  51.4 2.8 %backward.3 = (bf16[64,4096]{1,0:T(8,128)(2,1)S(1)}, bf16[64,4096]{1,0:T(8,128)(2,1)S(1)}, bf16[128,1024]{1,0:T(8,128)(2,1)S(1)}, bf16[128,1024]{1,0:T(8,128)(2,1)S(1)}) custom-call(bf16[128,1024]{1,0:T(8,128)(2,1)S(1)} %get-tuple-element.53.refs_0_, bf16[128,1024]{1,0:T(8,128)(2,1)S(1)} %collective-permute-done.6.refs_12_.refs_1_, ...), custom_call_target="tpu_custom_call" | custom-call | flops 1073741824 | tf_op jit(solution)/shard_map/backward/pallas_call | solution.py:257
  54.2 0.5 collective-permute-start.14
  54.7 0.0 collective-permute-done.15.refs_3_.refs_1_
  54.7 0.5 collective-permute-start.16
  55.2 0.0 collective-permute-done.19.refs_2_
  55.2 3.1 %collective-permute-done.18.refs_1_ = bf16[128,1024]{1,0:T(8,128)(2,1)S(1)} collective-permute-done((bf16[128,1024]{1,0:T(8,128)(2,1)S(1)}, bf16[128,1024]{1,0:T(8,128)(2,1)S(1)}, u32[]{:S(2)}, u32[]{:S(2)}) %collective-permute-start.18) | collective-permute-done | bytes 262176 | tf_op jit(solution)/shard_map/ppermute | solution.py:395
  58.3 0.1 third.1
  58.4 1.3 %collective-permute-start.20 = (bf16[128,1024]{1,0:T(8,128)(2,1)S(1)}, bf16[128,1024]{1,0:T(8,128)(2,1)S(1)}, u32[]{:S(2)}, u32[]{:S(2)}) collective-permute-start(bf16[128,1024]{1,0:T(8,128)(2,1)S(1)} %third.1), channel_id=1, source_target_pairs={{8,0},{9,1},{10,2},{11,3},{12,4},{13,5},{14,6},{15,7},{16,8},{17,9... | collective-permute-start | bytes 786440 | tf_op jit(solution)/shard_map/ppermute | solution.py:395
  59.7 3.3 %collective-permute-done.16.refs_2_ = bf16[128,1024]{1,0:T(8,128)(2,1)S(1)} collective-permute-done((bf16[128,1024]{1,0:T(8,128)(2,1)S(1)}, bf16[128,1024]{1,0:T(8,128)(2,1)S(1)}, u32[]{:S(2)}, u32[]{:S(2)}) %collective-permute-start.16) | collective-permute-done | bytes 262176 | tf_op jit(solution)/shard_map/ppermute | solution.py:395
  63.0 3.7 %collective-permute-done.20.refs_3_ = bf16[128,1024]{1,0:T(8,128)(2,1)S(1)} collective-permute-done((bf16[128,1024]{1,0:T(8,128)(2,1)S(1)}, bf16[128,1024]{1,0:T(8,128)(2,1)S(1)}, u32[]{:S(2)}, u32[]{:S(2)}) %collective-permute-start.20) | collective-permute-done | bytes 262176 | tf_op jit(solution)/shard_map/ppermute | solution.py:395
  66.7 0.1 fourth.1
  66.8 0.1 collective-permute-start.21
  66.9 0.0 collective-permute-done.12.refs_1_
  66.9 0.0 collective-permute-done.14.refs_3_
  66.9 1.4 %assemble.1 = (bf16[64,8192]{1,0:T(8,128)(2,1)}, bf16[64,8192]{1,0:T(8,128)(2,1)}) custom-call(bf16[64,4096]{1,0:T(8,128)(2,1)S(1)} %get-tuple-element.41.refs_0_, bf16[64,4096]{1,0:T(8,128)(2,1)S(1)} %collective-permute-done.12.refs_1_, bf16[64,4096]{1,0:T(8,128)(2,1)S(1)} %get-tuple-element.56.refs_2_, bf16[64,4096]{1,0:T(8,128)(2,1)S(1)} %collective-permute-done.14.refs_3_), custom_call_target="tpu_custom_call" | custom-call | tf_op jit(solution)/shard_map/assemble/pallas_call | solution.py:257
  68.3 0.0 collective-permute-done.21.refs_1_
  68.3 0.7 %fifth.1 = (bf16[64,1024]{1,0:T(8,128)(2,1)}, bf16[64,1024]{1,0:T(8,128)(2,1)}) custom-call(bf16[64,1024]{1,0:T(8,128)(2,1)S(1)} %get-tuple-element.66.refs_0_, bf16[64,1024]{1,0:T(8,128)(2,1)S(1)} %collective-permute-done.21.refs_1_), custom_call_target="tpu_custom_call" | custom-call | tf_op jit(solution)/shard_map/fifth/pallas_call | solution.py:257
  (5 shorter events, 0.1 us)
Async XLA Ops:
  0.6 17.4 %copy-start.1 = (bf16[64,8192]{1,0:T(8,128)(2,1)S(1)}, bf16[64,8192]{1,0:T(8,128)(2,1)}, u32[]{:S(2)}) copy-start(bf16[64,8192]{1,0:T(8,128)(2,1)} %refs_1_.1) | copy-start | bytes 3145732
  0.6 17.4 %copy-start = (bf16[64,8192]{1,0:T(8,128)(2,1)S(1)}, bf16[64,8192]{1,0:T(8,128)(2,1)}, u32[]{:S(2)}) copy-start(bf16[64,8192]{1,0:T(8,128)(2,1)} %refs_0_.1) | copy-start | bytes 3145732
  1.8 1.5 %collective-permute-start = (bf16[64,1024]{1,0:T(8,128)(2,1)S(1)}, bf16[64,1024]{1,0:T(8,128)(2,1)S(1)}, u32[]{:S(2)}, u32[]{:S(2)}) collective-permute-start(bf16[64,1024]{1,0:T(8,128)(2,1)S(1)} %pad_maximum_fusion.1), channel_id=1, source_target_pairs={{0,1},{1,0},{2,3},{3,2},{4,5},{5,4},{6,7},{7,6},{8,9},{9,8},{10,11... | collective-permute-start | bytes 393224 | tf_op jit(solution)/shard_map/ppermute | solution.py:395
  3.3 11.6 %collective-permute-start.6 = (bf16[128,1024]{1,0:T(8,128)(2,1)S(1)}, bf16[128,1024]{1,0:T(8,128)(2,1)S(1)}, u32[]{:S(2)}, u32[]{:S(2)}) collective-permute-start(bf16[128,1024]{1,0:T(8,128)(2,1)S(1)} %stack.1.refs_13_.refs_2_), channel_id=1, source_target_pairs={{0,8},{1,9},{2,10},{3,11},{4,12},{5,13},{6,14},{7,15},{8,16},{9,17... | collective-permute-start | bytes 786440 | tf_op jit(solution)/shard_map/ppermute | solution.py:395
  6.3 11.8 %collective-permute-start.1 = (bf16[128,1024]{1,0:T(8,128)(2,1)S(1)}, bf16[128,1024]{1,0:T(8,128)(2,1)S(1)}, u32[]{:S(2)}, u32[]{:S(2)}) collective-permute-start(bf16[128,1024]{1,0:T(8,128)(2,1)S(1)} %stack.1.refs_13_.refs_2_), channel_id=1, source_target_pairs={{0,2},{1,3},{2,0},{3,1},{4,6},{5,7},{6,4},{7,5},{8,10},{9,11},{10,... | collective-permute-start | bytes 786440 | tf_op jit(solution)/shard_map/ppermute | solution.py:395
  15.0 7.8 %collective-permute-start.9 = (bf16[128,1024]{1,0:T(8,128)(2,1)S(1)}, bf16[128,1024]{1,0:T(8,128)(2,1)S(1)}, u32[]{:S(2)}, u32[]{:S(2)}) collective-permute-start(bf16[128,1024]{1,0:T(8,128)(2,1)S(1)} %collective-permute-done.6.refs_12_.refs_1_), channel_id=1, source_target_pairs={{0,2},{1,3},{2,0},{3,1},{4,6},{5,7},{6,4},{7,5},{8,10},{9,11},{10,... | collective-permute-start | bytes 786440 | tf_op jit(solution)/shard_map/ppermute | solution.py:395
  16.5 7.4 %collective-permute-start.11 = (bf16[128,1024]{1,0:T(8,128)(2,1)S(1)}, bf16[128,1024]{1,0:T(8,128)(2,1)S(1)}, u32[]{:S(2)}, u32[]{:S(2)}) collective-permute-start(bf16[128,1024]{1,0:T(8,128)(2,1)S(1)} %broadcast_select_fusion), channel_id=1, source_target_pairs={{0,4},{1,5},{2,6},{3,7},{4,0},{5,1},{6,2},{7,3},{8,12},{9,13},{10,... | collective-permute-start | bytes 786440 | tf_op jit(solution)/shard_map/ppermute | solution.py:395
  18.1 8.8 %collective-permute-start.7 = (bf16[128,1024]{1,0:T(8,128)(2,1)S(1)}, bf16[128,1024]{1,0:T(8,128)(2,1)S(1)}, u32[]{:S(2)}, u32[]{:S(2)}) collective-permute-start(bf16[128,1024]{1,0:T(8,128)(2,1)S(1)} %collective-permute-done.6.refs_12_.refs_1_), channel_id=1, source_target_pairs={{0,8},{1,9},{2,10},{3,11},{4,12},{5,13},{6,14},{7,15},{8,16},{9,17... | collective-permute-start | bytes 786440 | tf_op jit(solution)/shard_map/ppermute | solution.py:395
  18.2 9.2 %collective-permute-start.2 = (bf16[128,1024]{1,0:T(8,128)(2,1)S(1)}, bf16[128,1024]{1,0:T(8,128)(2,1)S(1)}, u32[]{:S(2)}, u32[]{:S(2)}) collective-permute-start(bf16[128,1024]{1,0:T(8,128)(2,1)S(1)} %get-tuple-element.37), channel_id=1, source_target_pairs={{0,1},{1,0},{2,3},{3,2},{4,5},{5,4},{6,7},{7,6},{8,9},{9,8},{10,11... | collective-permute-start | bytes 786440 | tf_op jit(solution)/shard_map/ppermute | solution.py:395
  18.3 9.9 %collective-permute-start.3 = (bf16[128,1024]{1,0:T(8,128)(2,1)S(1)}, bf16[128,1024]{1,0:T(8,128)(2,1)S(1)}, u32[]{:S(2)}, u32[]{:S(2)}) collective-permute-start(bf16[128,1024]{1,0:T(8,128)(2,1)S(1)} %get-tuple-element.38), channel_id=1, source_target_pairs={{0,1},{1,0},{2,3},{3,2},{4,5},{5,4},{6,7},{7,6},{8,9},{9,8},{10,11... | collective-permute-start | bytes 786440 | tf_op jit(solution)/shard_map/ppermute | solution.py:395
  22.8 5.4 %collective-permute-start.4 = (bf16[128,1024]{1,0:T(8,128)(2,1)S(1)}, bf16[128,1024]{1,0:T(8,128)(2,1)S(1)}, u32[]{:S(2)}, u32[]{:S(2)}) collective-permute-start(bf16[128,1024]{1,0:T(8,128)(2,1)S(1)} %get-tuple-element.39), channel_id=1, source_target_pairs={{0,1},{1,0},{2,3},{3,2},{4,5},{5,4},{6,7},{7,6},{8,9},{9,8},{10,11... | collective-permute-start | bytes 786440 | tf_op jit(solution)/shard_map/ppermute | solution.py:395
  23.9 4.3 %collective-permute-start.5 = (bf16[128,1024]{1,0:T(8,128)(2,1)S(1)}, bf16[128,1024]{1,0:T(8,128)(2,1)S(1)}, u32[]{:S(2)}, u32[]{:S(2)}) collective-permute-start(bf16[128,1024]{1,0:T(8,128)(2,1)S(1)} %get-tuple-element.40), channel_id=1, source_target_pairs={{0,1},{1,0},{2,3},{3,2},{4,5},{5,4},{6,7},{7,6},{8,9},{9,8},{10,11... | collective-permute-start | bytes 786440 | tf_op jit(solution)/shard_map/ppermute | solution.py:395
  26.9 6.4 %collective-permute-start.8 = (bf16[128,1024]{1,0:T(8,128)(2,1)S(1)}, bf16[128,1024]{1,0:T(8,128)(2,1)S(1)}, u32[]{:S(2)}, u32[]{:S(2)}) collective-permute-start(bf16[128,1024]{1,0:T(8,128)(2,1)S(1)} %collective-permute-done.7.refs_10_.refs_2_), channel_id=1, source_target_pairs={{0,2},{1,3},{2,0},{3,1},{4,6},{5,7},{6,4},{7,5},{8,10},{9,11},{10,... | collective-permute-start | bytes 786440 | tf_op jit(solution)/shard_map/ppermute | solution.py:395
  27.4 6.4 %collective-permute-start.10 = (bf16[128,1024]{1,0:T(8,128)(2,1)S(1)}, bf16[128,1024]{1,0:T(8,128)(2,1)S(1)}, u32[]{:S(2)}, u32[]{:S(2)}) collective-permute-start(bf16[128,1024]{1,0:T(8,128)(2,1)S(1)} %broadcast_select_fusion.1), channel_id=1, source_target_pairs={{0,4},{1,5},{2,6},{3,7},{4,0},{5,1},{6,2},{7,3},{8,12},{9,13},{10,... | collective-permute-start | bytes 786440 | tf_op jit(solution)/shard_map/ppermute | solution.py:395
  40.2 8.0 %collective-permute-start.13 = (bf16[128,1024]{1,0:T(8,128)(2,1)S(1)}, bf16[128,1024]{1,0:T(8,128)(2,1)S(1)}, u32[]{:S(2)}, u32[]{:S(2)}) collective-permute-start(bf16[128,1024]{1,0:T(8,128)(2,1)S(1)} %get-tuple-element.52), channel_id=1, source_target_pairs={{0,4},{1,5},{2,6},{3,7},{4,0},{5,1},{6,2},{7,3},{8,12},{9,13},{10,... | collective-permute-start | bytes 786440 | tf_op jit(solution)/shard_map/ppermute | solution.py:395
  41.0 8.9 %collective-permute-start.17 = (bf16[128,1024]{1,0:T(8,128)(2,1)S(1)}, bf16[128,1024]{1,0:T(8,128)(2,1)S(1)}, u32[]{:S(2)}, u32[]{:S(2)}) collective-permute-start(bf16[128,1024]{1,0:T(8,128)(2,1)S(1)} %get-tuple-element.65), channel_id=1, source_target_pairs={{0,2},{1,3},{2,0},{3,1},{4,6},{5,7},{6,4},{7,5},{8,10},{9,11},{10,... | collective-permute-start | bytes 786440 | tf_op jit(solution)/shard_map/ppermute | solution.py:395
  46.6 8.1 %collective-permute-start.15 = (bf16[128,1024]{1,0:T(8,128)(2,1)S(1)}, bf16[128,1024]{1,0:T(8,128)(2,1)S(1)}, u32[]{:S(2)}, u32[]{:S(2)}) collective-permute-start(bf16[128,1024]{1,0:T(8,128)(2,1)S(1)} %get-tuple-element.61), channel_id=1, source_target_pairs={{0,4},{1,5},{2,6},{3,7},{4,0},{5,1},{6,2},{7,3},{8,12},{9,13},{10,... | collective-permute-start | bytes 786440 | tf_op jit(solution)/shard_map/ppermute | solution.py:395
  48.3 6.9 %collective-permute-start.19 = (bf16[128,1024]{1,0:T(8,128)(2,1)S(1)}, bf16[128,1024]{1,0:T(8,128)(2,1)S(1)}, u32[]{:S(2)}, u32[]{:S(2)}) collective-permute-start(bf16[128,1024]{1,0:T(8,128)(2,1)S(1)} %get-tuple-element.53.refs_0_), channel_id=1, source_target_pairs={{0,2},{1,3},{2,0},{3,1},{4,6},{5,7},{6,4},{7,5},{8,10},{9,11},{10,... | collective-permute-start | bytes 786440 | tf_op jit(solution)/shard_map/ppermute | solution.py:395
  50.0 8.3 %collective-permute-start.18 = (bf16[128,1024]{1,0:T(8,128)(2,1)S(1)}, bf16[128,1024]{1,0:T(8,128)(2,1)S(1)}, u32[]{:S(2)}, u32[]{:S(2)}) collective-permute-start(bf16[128,1024]{1,0:T(8,128)(2,1)S(1)} %second.1), channel_id=1, source_target_pairs={{8,0},{9,1},{10,2},{11,3},{12,4},{13,5},{14,6},{15,7},{16,8},{17,9... | collective-permute-start | bytes 786440 | tf_op jit(solution)/shard_map/ppermute | solution.py:395
  51.3 15.6 %collective-permute-start.12 = (bf16[64,4096]{1,0:T(8,128)(2,1)S(1)}, bf16[64,4096]{1,0:T(8,128)(2,1)S(1)}, u32[]{:S(2)}, u32[]{:S(2)}) collective-permute-start(bf16[64,4096]{1,0:T(8,128)(2,1)S(1)} %get-tuple-element.42), channel_id=1, source_target_pairs={{0,1},{1,0},{2,3},{3,2},{4,5},{5,4},{6,7},{7,6},{8,9},{9,8},{10,11... | collective-permute-start | bytes 1572872 | tf_op jit(solution)/shard_map/ppermute | solution.py:395
  54.2 12.8 %collective-permute-start.14 = (bf16[64,4096]{1,0:T(8,128)(2,1)S(1)}, bf16[64,4096]{1,0:T(8,128)(2,1)S(1)}, u32[]{:S(2)}, u32[]{:S(2)}) collective-permute-start(bf16[64,4096]{1,0:T(8,128)(2,1)S(1)} %get-tuple-element.57), channel_id=1, source_target_pairs={{0,1},{1,0},{2,3},{3,2},{4,5},{5,4},{6,7},{7,6},{8,9},{9,8},{10,11... | collective-permute-start | bytes 1572872 | tf_op jit(solution)/shard_map/ppermute | solution.py:395
  54.7 8.3 %collective-permute-start.16 = (bf16[128,1024]{1,0:T(8,128)(2,1)S(1)}, bf16[128,1024]{1,0:T(8,128)(2,1)S(1)}, u32[]{:S(2)}, u32[]{:S(2)}) collective-permute-start(bf16[128,1024]{1,0:T(8,128)(2,1)S(1)} %get-tuple-element.62), channel_id=1, source_target_pairs={{0,2},{1,3},{2,0},{3,1},{4,6},{5,7},{6,4},{7,5},{8,10},{9,11},{10,... | collective-permute-start | bytes 786440 | tf_op jit(solution)/shard_map/ppermute | solution.py:395
  58.4 8.3 %collective-permute-start.20 = (bf16[128,1024]{1,0:T(8,128)(2,1)S(1)}, bf16[128,1024]{1,0:T(8,128)(2,1)S(1)}, u32[]{:S(2)}, u32[]{:S(2)}) collective-permute-start(bf16[128,1024]{1,0:T(8,128)(2,1)S(1)} %third.1), channel_id=1, source_target_pairs={{8,0},{9,1},{10,2},{11,3},{12,4},{13,5},{14,6},{15,7},{16,8},{17,9... | collective-permute-start | bytes 786440 | tf_op jit(solution)/shard_map/ppermute | solution.py:395
  66.8 1.5 %collective-permute-start.21 = (bf16[64,1024]{1,0:T(8,128)(2,1)S(1)}, bf16[64,1024]{1,0:T(8,128)(2,1)S(1)}, u32[]{:S(2)}, u32[]{:S(2)}) collective-permute-start(bf16[64,1024]{1,0:T(8,128)(2,1)S(1)} %get-tuple-element.67), channel_id=1, source_target_pairs={{0,1},{1,0},{2,3},{3,2},{4,5},{5,4},{6,7},{7,6},{8,9},{9,8},{10,11... | collective-permute-start | bytes 393224 | tf_op jit(solution)/shard_map/ppermute | solution.py:395

commit v5 on v4

--- a/solution.py
+++ b/solution.py
@@ -59,7 +59,9 @@
     def stack(self, mine, other, at):
         base = self.index * self.group
         blocks = [mine[:, (base + r) * HD : (base + r + 1) * HD] for r in range(self.group)]
-        blocks += [other[at, r * HD : (r + 1) * HD] for r in range(self.group)]
+        each = other[0].shape[1] // (self.group * HD)
+        piece, base = other[self.index // each], self.index % each * self.group
+        blocks += [piece[at, (base + r) * HD : (base + r + 1) * HD] for r in range(self.group)]
         return jnp.concatenate(blocks, axis=0)
 
     def unstack(self, refs, value):
@@ -91,9 +93,9 @@
     return parts, refs
 
 
-def forward_kernel(groups, group, per, *refs):
+def forward_kernel(groups, group, per, pieces, *refs):
     q_ref, g_ref = refs[:2]
-    others, refs = refs[2 : 2 + per], refs[2 + per :]
+    others, refs = refs[2 : 2 + pieces], refs[2 + pieces :]
     shards, refs = split(refs, groups)
     outs, refs = refs[:2], refs[2:]
     homes, refs = refs[: len(groups[0])], refs[len(groups[0]) :]
@@ -127,8 +129,8 @@
 
     class Forward(Head):
         def start(self):
-            self.queries = self.stack(q_ref, others[self.index], slice(0, rows))
-            self.grads = self.stack(g_ref, others[self.index], slice(rows, 2 * rows))
+            self.queries = self.stack(q_ref, others, slice(0, rows))
+            self.grads = self.stack(g_ref, others, slice(rows, 2 * rows))
             self.queries_t, self.grads_t = self.queries.T, self.grads.T
             self.top, self.total, self.out_t = None, None, None
             self.scores, self.weights = [], []
@@ -281,12 +283,13 @@
     return pl.CostEstimate(flops=2 * keys * span * HD * heads * matmuls, bytes_accessed=0, transcendentals=0)
 
 
-def sizes(others):
-    return others[0].shape[0] // 2, len(others), others[0].shape[1] // HD
+def sizes(others, shard):
+    heads = shard.shape[1] // (2 * HD)
+    return others[0].shape[0] // 2, heads, len(others) * others[0].shape[1] // (heads * HD)
 
 
 def forward(query, grad, others, held, groups):
-    rows, heads, group = sizes(others)
+    rows, heads, group = sizes(others, held[0, 0])
     span = 2 * group * rows
     shards = [held[at] for part in groups for at in part]
     keys = shards[0].shape[0]
@@ -299,14 +302,14 @@
     shapes += [like((heads, HD, span)), like((heads, span, HD)), like((heads, span, HD))]
     shapes += [like((heads, 1, span), jnp.float32)] * 2 + [like((heads, HD, span), jnp.float32)]
     rest = call(
-        lambda *refs: forward_kernel(groups, group, per, *refs),
+        lambda *refs: forward_kernel(groups, group, per, len(others), *refs),
         [query, grad, *others] + shards,
         shapes,
         "forward",
         limit=28,
         grid=(steps,),
         cost=cost(keys, span, heads, 2 * len(shards) + 4 * len(groups[0])),
-        in_spec=[block] * 2 + [WHOLE] * (heads + len(shards)),
+        in_spec=[block] * 2 + [WHOLE] * (len(others) + len(shards)),
     )
     outs, rest = rest[:2], rest[2:]
     sums, rest = rest[: len(groups[0])], rest[len(groups[0]) :]
@@ -314,7 +317,7 @@
 
 
 def backward(others, held, groups, weights, state, last, after=()):
-    rows, heads, group = sizes(others)
+    rows, heads, group = sizes(others, held[0, 0])
     span = 2 * group * rows
     shards = [held[at] for part in groups for at in part]
     keys = shards[0].shape[0]
@@ -344,9 +347,9 @@
     return pl.BlockSpec((rows, width // 2), lambda step: (0, side() ^ place))
 
 
-def pack(query, grad, after, heads):
+def pack(query, grad, after, pieces):
     rows, width = query.shape
-    share = width // 2 // heads
+    share = width // 2 // pieces
 
     def kernel(query_ref, grad_ref, after_ref, *outs):
         for index, out in enumerate(outs):
@@ -354,7 +357,7 @@
             out[rows:] = grad_ref[:, index * share : (index + 1) * share]
 
     specs = [halves(query, 1), halves(grad, 1), WHOLE]
-    shapes = [like((2 * rows, share))] * heads
+    shapes = [like((2 * rows, share))] * pieces
     return call(kernel, [query, grad, after], shapes, "pack", grid=(1,), in_spec=specs, cost=FREE)
 
 
@@ -450,7 +453,7 @@
     (own,) = merge(stack, [kept, sibling(sent)], [shape], "stack")
     held = gather(own, levels)
     heads = width // (2 * HD)
-    others = [sibling(array) for array in pack(query_act, grad_out, held[0, 2], heads)]
+    others = [sibling(array) for array in pack(query_act, grad_out, held[0, 2], heads // 2)]
 
     group_a = [(level, 2) for level in later] + [(1, 2)]
     group_b = [(2, 2), (0, 2)] + [(level, 0) for level in later] + [(1, 0)]

time: 69.4 us -> 70.3 us (1.013)
  waiting for transfers between devices: 31.9 us -> 30.5 us
  local copies, waits for them, and re-layouts: 1.11 us -> 2.27 us
  starting transfers between devices: 19 us -> 20 us
    ppermute x22 -> x20, waiting for transfers between devices: 31.9 us -> 30.5 us  [permute(): return lax.ppermute(array, AXES, pairs)]
    unnamed x4 -> x6, local copies, waits for them, and re-layouts: 0.01 us -> 1.23 us
    ppermute x22 -> x20, starting transfers between devices: 19 us -> 20 us  [permute(): return lax.ppermute(array, AXES, pairs)]
  transfers between devices with their start and end apart: 22 -> 20, of which waited for: 10 -> 9; matrix products, arithmetic and copies ran while one was open for 0% -> 0% of each run, Pallas kernels for 13% -> 13%
where the time goes in v5:
time: 70.3 us; the launch traced here: 69.8 us
  waiting for transfers between devices  30.5 us (43%)
  starting transfers between devices  20 us (28%)
  Pallas kernels  16.2 us (23%)
  local copies, waits for them, and re-layouts  2.27 us (3%)
  between operations  0.82 us (1%)
    ppermute x20, waiting for transfers between devices, permute(): return lax.ppermute(array, AXES, pairs)  30.5 us
    ppermute x20, starting transfers between devices, permute(): return lax.ppermute(array, AXES, pairs)  20 us
    pallas_call x11, Pallas kernels, call(): pl.pallas_call(kernel, grid=grid, out_shape=shapes, in_specs=in_spec if i...  16.2 us
  transfers between devices with their start and end apart: 20, of which 9 were waited for; matrix products, arithmetic and copies ran while one was open for 0% of the time, Pallas kernels for 13%

profile of v5, /device:TPU:0, one launch (start us, length us, event | category | flops | bytes accessed | tf_op | source)
XLA Modules:
  0.0 69.8 jit_solution(7716820811120683141)
XLA Ops:
  0.6 0.0 copy-start
  0.7 1.0 %constant_dynamic-slice_fusion = (bf16[64,512]{1,0:T(8,128)(2,1)S(1)}, bf16[64,512]{1,0:T(8,128)(2,1)S(1)}, bf16[64,512]{1,0:T(8,128)(2,1)S(1)}, bf16[64,512]{1,0:T(8,128)(2,1)S(1)}) fusion(bf16[64,1024]{1,0:T(8,128)(2,1)} %param.6, s32[]{:T(128)S(6)} %select_n.35, s32[]{:T(128)S(6)} %select_n.34, bf16[64,1024]{1,0:T(8,128)(2,1)} %param.5), kind=kLoop, calls=%fused_computation.4 | loop fusion | bytes 524296 | tf_op jit(solution)/shard_map/dynamic_slice | solution.py:444
  1.7 0.5 collective-permute-start
  2.3 1.0 %collective-permute-done.refs_1_ = bf16[64,1024]{1,0:T(8,128)(2,1)S(1)} collective-permute-done((bf16[64,1024]{1,0:T(8,128)(2,1)S(1)}, bf16[64,1024]{1,0:T(8,128)(2,1)S(1)}, u32[]{:S(2)}, u32[]{:S(2)}) %collective-permute-start) | collective-permute-done | bytes 131104 | tf_op jit(solution)/shard_map/ppermute | solution.py:398
  3.3 3.0 %collective-permute-start.4 = (bf16[128,1024]{1,0:T(8,128)(2,1)S(1)}, bf16[128,1024]{1,0:T(8,128)(2,1)S(1)}, u32[]{:S(2)}, u32[]{:S(2)}) collective-permute-start(bf16[128,1024]{1,0:T(8,128)(2,1)S(1)} %stack.1.refs_11_.refs_2_), channel_id=1, source_target_pairs={{0,8},{1,9},{2,10},{3,11},{4,12},{5,13},{6,14},{7,15},{8,16},{9,17... | collective-permute-start | bytes 786440 | tf_op jit(solution)/shard_map/ppermute | solution.py:398
  6.2 1.5 %collective-permute-start.1 = (bf16[128,1024]{1,0:T(8,128)(2,1)S(1)}, bf16[128,1024]{1,0:T(8,128)(2,1)S(1)}, u32[]{:S(2)}, u32[]{:S(2)}) collective-permute-start(bf16[128,1024]{1,0:T(8,128)(2,1)S(1)} %stack.1.refs_11_.refs_2_), channel_id=1, source_target_pairs={{0,2},{1,3},{2,0},{3,1},{4,6},{5,7},{6,4},{7,5},{8,10},{9,11},{10,... | collective-permute-start | bytes 786440 | tf_op jit(solution)/shard_map/ppermute | solution.py:398
  7.8 7.1 %collective-permute-done.4.refs_10_.refs_1_ = bf16[128,1024]{1,0:T(8,128)(2,1)S(1)} collective-permute-done((bf16[128,1024]{1,0:T(8,128)(2,1)S(1)}, bf16[128,1024]{1,0:T(8,128)(2,1)S(1)}, u32[]{:S(2)}, u32[]{:S(2)}) %collective-permute-start.4) | collective-permute-done | bytes 262176 | tf_op jit(solution)/shard_map/ppermute | solution.py:398
  14.9 0.0 collective-permute-start.5
  14.9 1.5 %collective-permute-start.7 = (bf16[128,1024]{1,0:T(8,128)(2,1)S(1)}, bf16[128,1024]{1,0:T(8,128)(2,1)S(1)}, u32[]{:S(2)}, u32[]{:S(2)}) collective-permute-start(bf16[128,1024]{1,0:T(8,128)(2,1)S(1)} %collective-permute-done.4.refs_10_.refs_1_), channel_id=1, source_target_pairs={{0,2},{1,3},{2,0},{3,1},{4,6},{5,7},{6,4},{7,5},{8,10},{9,11},{10,... | collective-permute-start | bytes 786440 | tf_op jit(solution)/shard_map/ppermute | solution.py:398
  16.4 0.0 collective-permute-done.1.after_ref.refs_7_.refs_1_
  16.4 0.0 copy-done
  16.4 0.0 copy-start.1
  16.4 1.2 %copy-done.1 = bf16[64,8192]{1,0:T(8,128)(2,1)S(1)} copy-done((bf16[64,8192]{1,0:T(8,128)(2,1)S(1)}, bf16[64,8192]{1,0:T(8,128)(2,1)}, u32[]{:S(2)}) %copy-start.1) | copy-done | bytes 1048600
  17.6 0.0 copy-start.2
  17.6 0.1 pack.1
  17.7 0.1 collective-permute-start.2
  17.8 0.5 collective-permute-start.3
  18.3 1.6 %collective-permute-start.9 = (bf16[128,1024]{1,0:T(8,128)(2,1)S(1)}, bf16[128,1024]{1,0:T(8,128)(2,1)S(1)}, u32[]{:S(2)}, u32[]{:S(2)}) collective-permute-start(bf16[128,1024]{1,0:T(8,128)(2,1)S(1)} %broadcast_select_fusion), channel_id=1, source_target_pairs={{0,4},{1,5},{2,6},{3,7},{4,0},{5,1},{6,2},{7,3},{8,12},{9,13},{10,... | collective-permute-start | bytes 786440 | tf_op jit(solution)/shard_map/ppermute | solution.py:398
  19.9 4.7 %collective-permute-done.5.refs_8_.refs_2_ = bf16[128,1024]{1,0:T(8,128)(2,1)S(1)} collective-permute-done((bf16[128,1024]{1,0:T(8,128)(2,1)S(1)}, bf16[128,1024]{1,0:T(8,128)(2,1)S(1)}, u32[]{:S(2)}, u32[]{:S(2)}) %collective-permute-start.5) | collective-permute-done | bytes 262176 | tf_op jit(solution)/shard_map/ppermute | solution.py:398
  24.5 1.3 %collective-permute-start.6 = (bf16[128,1024]{1,0:T(8,128)(2,1)S(1)}, bf16[128,1024]{1,0:T(8,128)(2,1)S(1)}, u32[]{:S(2)}, u32[]{:S(2)}) collective-permute-start(bf16[128,1024]{1,0:T(8,128)(2,1)S(1)} %collective-permute-done.5.refs_8_.refs_2_), channel_id=1, source_target_pairs={{0,2},{1,3},{2,0},{3,1},{4,6},{5,7},{6,4},{7,5},{8,10},{9,11},{10,... | collective-permute-start | bytes 786440 | tf_op jit(solution)/shard_map/ppermute | solution.py:398
  25.8 0.0 collective-permute-done.7.refs_6_.refs_0_
  25.8 1.6 %collective-permute-start.8 = (bf16[128,1024]{1,0:T(8,128)(2,1)S(1)}, bf16[128,1024]{1,0:T(8,128)(2,1)S(1)}, u32[]{:S(2)}, u32[]{:S(2)}) collective-permute-start(bf16[128,1024]{1,0:T(8,128)(2,1)S(1)} %broadcast_select_fusion.1), channel_id=1, source_target_pairs={{0,4},{1,5},{2,6},{3,7},{4,0},{5,1},{6,2},{7,3},{8,12},{9,13},{10,... | collective-permute-start | bytes 786440 | tf_op jit(solution)/shard_map/ppermute | solution.py:398
  27.4 0.0 collective-permute-done.9.refs_9_.refs_3_
  27.4 4.1 %collective-permute-done.6.refs_4_ = bf16[128,1024]{1,0:T(8,128)(2,1)S(1)} collective-permute-done((bf16[128,1024]{1,0:T(8,128)(2,1)S(1)}, bf16[128,1024]{1,0:T(8,128)(2,1)S(1)}, u32[]{:S(2)}, u32[]{:S(2)}) %collective-permute-start.6) | collective-permute-done | bytes 262176 | tf_op jit(solution)/shard_map/ppermute | solution.py:398
  31.5 0.8 %collective-permute-done.8.refs_5_ = bf16[128,1024]{1,0:T(8,128)(2,1)S(1)} collective-permute-done((bf16[128,1024]{1,0:T(8,128)(2,1)S(1)}, bf16[128,1024]{1,0:T(8,128)(2,1)S(1)}, u32[]{:S(2)}, u32[]{:S(2)}) %collective-permute-start.8) | collective-permute-done | bytes 262176 | tf_op jit(solution)/shard_map/ppermute | solution.py:398
  32.3 0.0 collective-permute-done.2.refs_2_
  32.3 0.0 collective-permute-done.3.refs_3_
  32.3 0.0 copy-done.2
  32.3 6.4 %forward.1 = (bf16[64,4096]{1,0:T(8,128)(2,1)S(1)}, bf16[64,4096]{1,0:T(8,128)(2,1)S(1)}, bf16[128,1024]{1,0:T(8,128)(2,1)S(1)}, bf16[128,1024]{1,0:T(8,128)(2,1...) custom-call(bf16[64,8192]{1,0:T(8,128)(2,1)S(1)} %copy-done, ...), custom_call_target="tpu_custom_call" | custom-call | flops 3221225472 | tf_op jit(solution)/shard_map/forward/pallas_call | solution.py:259
  38.7 1.6 %collective-permute-start.11 = (bf16[128,1024]{1,0:T(8,128)(2,1)S(1)}, bf16[128,1024]{1,0:T(8,128)(2,1)S(1)}, u32[]{:S(2)}, u32[]{:S(2)}) collective-permute-start(bf16[128,1024]{1,0:T(8,128)(2,1)S(1)} %get-tuple-element.48), channel_id=1, source_target_pairs={{0,4},{1,5},{2,6},{3,7},{4,0},{5,1},{6,2},{7,3},{8,12},{9,13},{10,... | collective-permute-start | bytes 786440 | tf_op jit(solution)/shard_map/ppermute | solution.py:398
  40.3 0.5 collective-permute-start.15
  40.8 4.3 %backward.2 = (f32[4,128,1024]{2,1,0:T(8,128)S(1)}, bf16[128,1024]{1,0:T(8,128)(2,1)S(1)}, bf16[128,1024]{1,0:T(8,128)(2,1)S(1)}, bf16[128,1024]{1,0:T(8,128)(2,1)S(1)}, bf16[128,1024]{1,0:T(8,128)(2,1)S(1)}) custom-call(bf16[128,1024]{1,0:T(8,128)(2,1)S(1)} %collective-permute-done.7.refs_6_.refs_0_, ...), custom_call_target="tpu_custom_call" | custom-call | flops 2147483648 | tf_op jit(solution)/shard_map/backward/pallas_call | solution.py:259
  45.1 1.1 %collective-permute-start.13 = (bf16[128,1024]{1,0:T(8,128)(2,1)S(1)}, bf16[128,1024]{1,0:T(8,128)(2,1)S(1)}, u32[]{:S(2)}, u32[]{:S(2)}) collective-permute-start(bf16[128,1024]{1,0:T(8,128)(2,1)S(1)} %get-tuple-element.57), channel_id=1, source_target_pairs={{0,4},{1,5},{2,6},{3,7},{4,0},{5,1},{6,2},{7,3},{8,12},{9,13},{10,... | collective-permute-start | bytes 786440 | tf_op jit(solution)/shard_map/ppermute | solution.py:398
  46.2 0.0 collective-permute-done.11.refs_2_
  46.2 0.2 aside.1
  46.4 1.1 %collective-permute-start.17 = (bf16[128,1024]{1,0:T(8,128)(2,1)S(1)}, bf16[128,1024]{1,0:T(8,128)(2,1)S(1)}, u32[]{:S(2)}, u32[]{:S(2)}) collective-permute-start(bf16[128,1024]{1,0:T(8,128)(2,1)S(1)} %get-tuple-element.49.refs_0_), channel_id=1, source_target_pairs={{0,2},{1,3},{2,0},{3,1},{4,6},{5,7},{6,4},{7,5},{8,10},{9,11},{10,... | collective-permute-start | bytes 786440 | tf_op jit(solution)/shard_map/ppermute | solution.py:398
  47.4 0.1 collective-permute-done.15.refs_1_
  47.5 0.1 second.1
  47.6 1.3 %collective-permute-start.16 = (bf16[128,1024]{1,0:T(8,128)(2,1)S(1)}, bf16[128,1024]{1,0:T(8,128)(2,1)S(1)}, u32[]{:S(2)}, u32[]{:S(2)}) collective-permute-start(bf16[128,1024]{1,0:T(8,128)(2,1)S(1)} %second.1), channel_id=1, source_target_pairs={{8,0},{9,1},{10,2},{11,3},{12,4},{13,5},{14,6},{15,7},{16,8},{17,9... | collective-permute-start | bytes 786440 | tf_op jit(solution)/shard_map/ppermute | solution.py:398
  48.9 0.1 collective-permute-start.10
  48.9 2.8 %backward.3 = (bf16[64,4096]{1,0:T(8,128)(2,1)S(1)}, bf16[64,4096]{1,0:T(8,128)(2,1)S(1)}, bf16[128,1024]{1,0:T(8,128)(2,1)S(1)}, bf16[128,1024]{1,0:T(8,128)(2,1)S(1)}) custom-call(bf16[128,1024]{1,0:T(8,128)(2,1)S(1)} %get-tuple-element.49.refs_0_, bf16[128,1024]{1,0:T(8,128)(2,1)S(1)} %collective-permute-done.4.refs_10_.refs_1_, ...), custom_call_target="tpu_custom_call" | custom-call | flops 1073741824 | tf_op jit(solution)/shard_map/backward/pallas_call | solution.py:259
  51.7 0.5 collective-permute-start.12
  52.3 0.0 collective-permute-done.13.refs_3_.refs_1_
  52.3 1.0 %collective-permute-start.14 = (bf16[128,1024]{1,0:T(8,128)(2,1)S(1)}, bf16[128,1024]{1,0:T(8,128)(2,1)S(1)}, u32[]{:S(2)}, u32[]{:S(2)}) collective-permute-start(bf16[128,1024]{1,0:T(8,128)(2,1)S(1)} %get-tuple-element.58), channel_id=1, source_target_pairs={{0,2},{1,3},{2,0},{3,1},{4,6},{5,7},{6,4},{7,5},{8,10},{9,11},{10,... | collective-permute-start | bytes 786440 | tf_op jit(solution)/shard_map/ppermute | solution.py:398
  53.2 0.0 collective-permute-done.17.refs_2_
  53.2 5.8 %collective-permute-done.16.refs_1_ = bf16[128,1024]{1,0:T(8,128)(2,1)S(1)} collective-permute-done((bf16[128,1024]{1,0:T(8,128)(2,1)S(1)}, bf16[128,1024]{1,0:T(8,128)(2,1)S(1)}, u32[]{:S(2)}, u32[]{:S(2)}) %collective-permute-start.16) | collective-permute-done | bytes 262176 | tf_op jit(solution)/shard_map/ppermute | solution.py:398
  59.0 0.1 third.1
  59.1 1.3 %collective-permute-start.18 = (bf16[128,1024]{1,0:T(8,128)(2,1)S(1)}, bf16[128,1024]{1,0:T(8,128)(2,1)S(1)}, u32[]{:S(2)}, u32[]{:S(2)}) collective-permute-start(bf16[128,1024]{1,0:T(8,128)(2,1)S(1)} %third.1), channel_id=1, source_target_pairs={{8,0},{9,1},{10,2},{11,3},{12,4},{13,5},{14,6},{15,7},{16,8},{17,9... | collective-permute-start | bytes 786440 | tf_op jit(solution)/shard_map/ppermute | solution.py:398
  60.4 0.1 collective-permute-done.14.refs_2_
  60.6 6.9 %collective-permute-done.18.refs_3_ = bf16[128,1024]{1,0:T(8,128)(2,1)S(1)} collective-permute-done((bf16[128,1024]{1,0:T(8,128)(2,1)S(1)}, bf16[128,1024]{1,0:T(8,128)(2,1)S(1)}, u32[]{:S(2)}, u32[]{:S(2)}) %collective-permute-start.18) | collective-permute-done | bytes 262176 | tf_op jit(solution)/shard_map/ppermute | solution.py:398
  67.4 0.1 fourth.1
  67.6 0.1 collective-permute-start.19
  67.6 0.0 collective-permute-done.10.refs_1_
  67.7 0.0 collective-permute-done.12.refs_3_
  67.7 1.4 %assemble.1 = (bf16[64,8192]{1,0:T(8,128)(2,1)}, bf16[64,8192]{1,0:T(8,128)(2,1)}) custom-call(bf16[64,4096]{1,0:T(8,128)(2,1)S(1)} %get-tuple-element.37.refs_0_, bf16[64,4096]{1,0:T(8,128)(2,1)S(1)} %collective-permute-done.10.refs_1_, bf16[64,4096]{1,0:T(8,128)(2,1)S(1)} %get-tuple-element.52.refs_2_, bf16[64,4096]{1,0:T(8,128)(2,1)S(1)} %collective-permute-done.12.refs_3_), custom_call_target="tpu_custom_call" | custom-call | tf_op jit(solution)/shard_map/assemble/pallas_call | solution.py:259
  69.0 0.0 collective-permute-done.19.refs_1_
  69.0 0.7 %fifth.1 = (bf16[64,1024]{1,0:T(8,128)(2,1)}, bf16[64,1024]{1,0:T(8,128)(2,1)}) custom-call(bf16[64,1024]{1,0:T(8,128)(2,1)S(1)} %get-tuple-element.62.refs_0_, bf16[64,1024]{1,0:T(8,128)(2,1)S(1)} %collective-permute-done.19.refs_1_), custom_call_target="tpu_custom_call" | custom-call | tf_op jit(solution)/shard_map/fifth/pallas_call | solution.py:259
  (5 shorter events, 0.1 us)
Async XLA Ops:
  0.6 15.8 %copy-start = (bf16[64,8192]{1,0:T(8,128)(2,1)S(1)}, bf16[64,8192]{1,0:T(8,128)(2,1)}, u32[]{:S(2)}) copy-start(bf16[64,8192]{1,0:T(8,128)(2,1)} %refs_0_.1) | copy-start | bytes 3145732
  1.7 1.5 %collective-permute-start = (bf16[64,1024]{1,0:T(8,128)(2,1)S(1)}, bf16[64,1024]{1,0:T(8,128)(2,1)S(1)}, u32[]{:S(2)}, u32[]{:S(2)}) collective-permute-start(bf16[64,1024]{1,0:T(8,128)(2,1)S(1)} %pad_maximum_fusion.1), channel_id=1, source_target_pairs={{0,1},{1,0},{2,3},{3,2},{4,5},{5,4},{6,7},{7,6},{8,9},{9,8},{10,11... | collective-permute-start | bytes 393224 | tf_op jit(solution)/shard_map/ppermute | solution.py:398
  3.3 11.6 %collective-permute-start.4 = (bf16[128,1024]{1,0:T(8,128)(2,1)S(1)}, bf16[128,1024]{1,0:T(8,128)(2,1)S(1)}, u32[]{:S(2)}, u32[]{:S(2)}) collective-permute-start(bf16[128,1024]{1,0:T(8,128)(2,1)S(1)} %stack.1.refs_11_.refs_2_), channel_id=1, source_target_pairs={{0,8},{1,9},{2,10},{3,11},{4,12},{5,13},{6,14},{7,15},{8,16},{9,17... | collective-permute-start | bytes 786440 | tf_op jit(solution)/shard_map/ppermute | solution.py:398
  6.2 10.2 %collective-permute-start.1 = (bf16[128,1024]{1,0:T(8,128)(2,1)S(1)}, bf16[128,1024]{1,0:T(8,128)(2,1)S(1)}, u32[]{:S(2)}, u32[]{:S(2)}) collective-permute-start(bf16[128,1024]{1,0:T(8,128)(2,1)S(1)} %stack.1.refs_11_.refs_2_), channel_id=1, source_target_pairs={{0,2},{1,3},{2,0},{3,1},{4,6},{5,7},{6,4},{7,5},{8,10},{9,11},{10,... | collective-permute-start | bytes 786440 | tf_op jit(solution)/shard_map/ppermute | solution.py:398
  14.9 9.6 %collective-permute-start.5 = (bf16[128,1024]{1,0:T(8,128)(2,1)S(1)}, bf16[128,1024]{1,0:T(8,128)(2,1)S(1)}, u32[]{:S(2)}, u32[]{:S(2)}) collective-permute-start(bf16[128,1024]{1,0:T(8,128)(2,1)S(1)} %collective-permute-done.4.refs_10_.refs_1_), channel_id=1, source_target_pairs={{0,8},{1,9},{2,10},{3,11},{4,12},{5,13},{6,14},{7,15},{8,16},{9,17... | collective-permute-start | bytes 786440 | tf_op jit(solution)/shard_map/ppermute | solution.py:398
  14.9 10.9 %collective-permute-start.7 = (bf16[128,1024]{1,0:T(8,128)(2,1)S(1)}, bf16[128,1024]{1,0:T(8,128)(2,1)S(1)}, u32[]{:S(2)}, u32[]{:S(2)}) collective-permute-start(bf16[128,1024]{1,0:T(8,128)(2,1)S(1)} %collective-permute-done.4.refs_10_.refs_1_), channel_id=1, source_target_pairs={{0,2},{1,3},{2,0},{3,1},{4,6},{5,7},{6,4},{7,5},{8,10},{9,11},{10,... | collective-permute-start | bytes 786440 | tf_op jit(solution)/shard_map/ppermute | solution.py:398
  16.4 1.2 %copy-start.1 = (bf16[64,8192]{1,0:T(8,128)(2,1)S(1)}, bf16[64,8192]{1,0:T(8,128)(2,1)}, u32[]{:S(2)}) copy-start(bf16[64,8192]{1,0:T(8,128)(2,1)} %refs_1_.1) | copy-start | bytes 3145732
  17.6 14.7 %copy-start.2 = (bf16[64,8192]{1,0:T(8,128)(2,1)S(1)}, bf16[64,8192]{1,0:T(8,128)(2,1)}, u32[]{:S(2)}) copy-start(bf16[64,8192]{1,0:T(8,128)(2,1)} %refs_1_.1) | copy-start | bytes 3145732
  17.7 14.6 %collective-permute-start.2 = (bf16[128,2048]{1,0:T(8,128)(2,1)S(1)}, bf16[128,2048]{1,0:T(8,128)(2,1)S(1)}, u32[]{:S(2)}, u32[]{:S(2)}) collective-permute-start(bf16[128,2048]{1,0:T(8,128)(2,1)S(1)} %get-tuple-element.35), channel_id=1, source_target_pairs={{0,1},{1,0},{2,3},{3,2},{4,5},{5,4},{6,7},{7,6},{8,9},{9,8},{10,11... | collective-permute-start | bytes 1572872 | tf_op jit(solution)/shard_map/ppermute | solution.py:398
  17.8 14.5 %collective-permute-start.3 = (bf16[128,2048]{1,0:T(8,128)(2,1)S(1)}, bf16[128,2048]{1,0:T(8,128)(2,1)S(1)}, u32[]{:S(2)}, u32[]{:S(2)}) collective-permute-start(bf16[128,2048]{1,0:T(8,128)(2,1)S(1)} %get-tuple-element.36), channel_id=1, source_target_pairs={{0,1},{1,0},{2,3},{3,2},{4,5},{5,4},{6,7},{7,6},{8,9},{9,8},{10,11... | collective-permute-start | bytes 1572872 | tf_op jit(solution)/shard_map/ppermute | solution.py:398
  18.3 9.1 %collective-permute-start.9 = (bf16[128,1024]{1,0:T(8,128)(2,1)S(1)}, bf16[128,1024]{1,0:T(8,128)(2,1)S(1)}, u32[]{:S(2)}, u32[]{:S(2)}) collective-permute-start(bf16[128,1024]{1,0:T(8,128)(2,1)S(1)} %broadcast_select_fusion), channel_id=1, source_target_pairs={{0,4},{1,5},{2,6},{3,7},{4,0},{5,1},{6,2},{7,3},{8,12},{9,13},{10,... | collective-permute-start | bytes 786440 | tf_op jit(solution)/shard_map/ppermute | solution.py:398
  24.5 6.9 %collective-permute-start.6 = (bf16[128,1024]{1,0:T(8,128)(2,1)S(1)}, bf16[128,1024]{1,0:T(8,128)(2,1)S(1)}, u32[]{:S(2)}, u32[]{:S(2)}) collective-permute-start(bf16[128,1024]{1,0:T(8,128)(2,1)S(1)} %collective-permute-done.5.refs_8_.refs_2_), channel_id=1, source_target_pairs={{0,2},{1,3},{2,0},{3,1},{4,6},{5,7},{6,4},{7,5},{8,10},{9,11},{10,... | collective-permute-start | bytes 786440 | tf_op jit(solution)/shard_map/ppermute | solution.py:398
  25.8 6.5 %collective-permute-start.8 = (bf16[128,1024]{1,0:T(8,128)(2,1)S(1)}, bf16[128,1024]{1,0:T(8,128)(2,1)S(1)}, u32[]{:S(2)}, u32[]{:S(2)}) collective-permute-start(bf16[128,1024]{1,0:T(8,128)(2,1)S(1)} %broadcast_select_fusion.1), channel_id=1, source_target_pairs={{0,4},{1,5},{2,6},{3,7},{4,0},{5,1},{6,2},{7,3},{8,12},{9,13},{10,... | collective-permute-start | bytes 786440 | tf_op jit(solution)/shard_map/ppermute | solution.py:398
  38.7 7.5 %collective-permute-start.11 = (bf16[128,1024]{1,0:T(8,128)(2,1)S(1)}, bf16[128,1024]{1,0:T(8,128)(2,1)S(1)}, u32[]{:S(2)}, u32[]{:S(2)}) collective-permute-start(bf16[128,1024]{1,0:T(8,128)(2,1)S(1)} %get-tuple-element.48), channel_id=1, source_target_pairs={{0,4},{1,5},{2,6},{3,7},{4,0},{5,1},{6,2},{7,3},{8,12},{9,13},{10,... | collective-permute-start | bytes 786440 | tf_op jit(solution)/shard_map/ppermute | solution.py:398
  40.3 7.2 %collective-permute-start.15 = (bf16[128,1024]{1,0:T(8,128)(2,1)S(1)}, bf16[128,1024]{1,0:T(8,128)(2,1)S(1)}, u32[]{:S(2)}, u32[]{:S(2)}) collective-permute-start(bf16[128,1024]{1,0:T(8,128)(2,1)S(1)} %get-tuple-element.61), channel_id=1, source_target_pairs={{0,2},{1,3},{2,0},{3,1},{4,6},{5,7},{6,4},{7,5},{8,10},{9,11},{10,... | collective-permute-start | bytes 786440 | tf_op jit(solution)/shard_map/ppermute | solution.py:398
  45.1 7.2 %collective-permute-start.13 = (bf16[128,1024]{1,0:T(8,128)(2,1)S(1)}, bf16[128,1024]{1,0:T(8,128)(2,1)S(1)}, u32[]{:S(2)}, u32[]{:S(2)}) collective-permute-start(bf16[128,1024]{1,0:T(8,128)(2,1)S(1)} %get-tuple-element.57), channel_id=1, source_target_pairs={{0,4},{1,5},{2,6},{3,7},{4,0},{5,1},{6,2},{7,3},{8,12},{9,13},{10,... | collective-permute-start | bytes 786440 | tf_op jit(solution)/shard_map/ppermute | solution.py:398
  46.4 6.9 %collective-permute-start.17 = (bf16[128,1024]{1,0:T(8,128)(2,1)S(1)}, bf16[128,1024]{1,0:T(8,128)(2,1)S(1)}, u32[]{:S(2)}, u32[]{:S(2)}) collective-permute-start(bf16[128,1024]{1,0:T(8,128)(2,1)S(1)} %get-tuple-element.49.refs_0_), channel_id=1, source_target_pairs={{0,2},{1,3},{2,0},{3,1},{4,6},{5,7},{6,4},{7,5},{8,10},{9,11},{10,... | collective-permute-start | bytes 786440 | tf_op jit(solution)/shard_map/ppermute | solution.py:398
  47.6 11.4 %collective-permute-start.16 = (bf16[128,1024]{1,0:T(8,128)(2,1)S(1)}, bf16[128,1024]{1,0:T(8,128)(2,1)S(1)}, u32[]{:S(2)}, u32[]{:S(2)}) collective-permute-start(bf16[128,1024]{1,0:T(8,128)(2,1)S(1)} %second.1), channel_id=1, source_target_pairs={{8,0},{9,1},{10,2},{11,3},{12,4},{13,5},{14,6},{15,7},{16,8},{17,9... | collective-permute-start | bytes 786440 | tf_op jit(solution)/shard_map/ppermute | solution.py:398
  48.9 18.8 %collective-permute-start.10 = (bf16[64,4096]{1,0:T(8,128)(2,1)S(1)}, bf16[64,4096]{1,0:T(8,128)(2,1)S(1)}, u32[]{:S(2)}, u32[]{:S(2)}) collective-permute-start(bf16[64,4096]{1,0:T(8,128)(2,1)S(1)} %get-tuple-element.38), channel_id=1, source_target_pairs={{0,1},{1,0},{2,3},{3,2},{4,5},{5,4},{6,7},{7,6},{8,9},{9,8},{10,11... | collective-permute-start | bytes 1572872 | tf_op jit(solution)/shard_map/ppermute | solution.py:398
  51.7 15.9 %collective-permute-start.12 = (bf16[64,4096]{1,0:T(8,128)(2,1)S(1)}, bf16[64,4096]{1,0:T(8,128)(2,1)S(1)}, u32[]{:S(2)}, u32[]{:S(2)}) collective-permute-start(bf16[64,4096]{1,0:T(8,128)(2,1)S(1)} %get-tuple-element.53), channel_id=1, source_target_pairs={{0,1},{1,0},{2,3},{3,2},{4,5},{5,4},{6,7},{7,6},{8,9},{9,8},{10,11... | collective-permute-start | bytes 1572872 | tf_op jit(solution)/shard_map/ppermute | solution.py:398
  52.3 8.3 %collective-permute-start.14 = (bf16[128,1024]{1,0:T(8,128)(2,1)S(1)}, bf16[128,1024]{1,0:T(8,128)(2,1)S(1)}, u32[]{:S(2)}, u32[]{:S(2)}) collective-permute-start(bf16[128,1024]{1,0:T(8,128)(2,1)S(1)} %get-tuple-element.58), channel_id=1, source_target_pairs={{0,2},{1,3},{2,0},{3,1},{4,6},{5,7},{6,4},{7,5},{8,10},{9,11},{10,... | collective-permute-start | bytes 786440 | tf_op jit(solution)/shard_map/ppermute | solution.py:398
  59.1 8.3 %collective-permute-start.18 = (bf16[128,1024]{1,0:T(8,128)(2,1)S(1)}, bf16[128,1024]{1,0:T(8,128)(2,1)S(1)}, u32[]{:S(2)}, u32[]{:S(2)}) collective-permute-start(bf16[128,1024]{1,0:T(8,128)(2,1)S(1)} %third.1), channel_id=1, source_target_pairs={{8,0},{9,1},{10,2},{11,3},{12,4},{13,5},{14,6},{15,7},{16,8},{17,9... | collective-permute-start | bytes 786440 | tf_op jit(solution)/shard_map/ppermute | solution.py:398
  67.6 1.5 %collective-permute-start.19 = (bf16[64,1024]{1,0:T(8,128)(2,1)S(1)}, bf16[64,1024]{1,0:T(8,128)(2,1)S(1)}, u32[]{:S(2)}, u32[]{:S(2)}) collective-permute-start(bf16[64,1024]{1,0:T(8,128)(2,1)S(1)} %get-tuple-element.63), channel_id=1, source_target_pairs={{0,1},{1,0},{2,3},{3,2},{4,5},{5,4},{6,7},{7,6},{8,9},{9,8},{10,11... | collective-permute-start | bytes 393224 | tf_op jit(solution)/shard_map/ppermute | solution.py:398
